TPU v7x, 32 devices: a whole 2x2x4 slice. The times are simulated.
32 devices in a mesh: groups: 2 (over x), corpus: 16 (over z, y, core).
Axes of the slice: x: 2, y: 2, z: 4, core: 2. Of those that a mesh axis runs over, the one named last changes fastest.
Arguments:
- queries: bfloat16 [1792, 32, 128], P(('groups', 'corpus')), parts along dimension 0, may hold values from -6 to 6
- passages: bfloat16 [4096, 128, 128], P(('groups', 'corpus')), parts along dimension 0, may hold values from -0.5 to 0.5
- lengths: int32 [4096], P(('groups', 'corpus')), parts along dimension 0, may hold values from 8 to 128
- candidates: int32 [32, 128], P(('groups', 'corpus')), parts along dimension 0, may hold values from 0 to 2047, as said below
Outputs:
- scores: float32 [1792, 128], P(('groups', 'corpus')), parts along dimension 0
- best_scores: float32 [1792, 100], P(('groups', 'corpus')), parts along dimension 0
There are 2 independent parts, one for each index of `groups`. A program takes and returns all parts, laid end to end along the dimension named above; each array names one. Nothing has to cross between parts.
Inputs may be any that keep to these rules, and one draw needn't show every extreme that they name: Row b lists the candidates of queries b * 56 to (b + 1) * 56 - 1. Passage p is held by owner p // 128. In every row at most 12 entries share an owner, and in every row some owner holds exactly 12 of them. Entries may repeat. `lengths`: rows of a tile at or past its length are padding.
All inputs are finite; a program needn't handle non-finite values.
Results may differ from a plain program's by a relative error of at most 0.0003.
Values may be sent and summed in bfloat16 or wider, within the bound.
No kernel may reach another device: no remote copies, remote signals or barrier semaphores. Data moves between devices by JAX's collectives and lax.ppermute only.
A program may use at most 128 MiB of HBM per device.

v0:
```python
import math

import jax
import jax.numpy as jnp
from jax import lax
from jax.sharding import PartitionSpec as P

TOPK = 100


def maxsim_many(query_sets, tile_sets, per_device):
    similar = jnp.einsum(
        "srd,sgpd->srgp", query_sets, tile_sets, preferred_element_type=jnp.float32
    )
    nearest = jnp.max(similar, axis=3)
    shards_now = query_sets.shape[0]
    query_tok = query_sets.shape[1] // per_device
    return jnp.sum(
        nearest.reshape(shards_now, per_device, query_tok, nearest.shape[2]), axis=2
    ) / float(query_tok)


def fill_rows(tile_set, tile_len):
    inside = lax.broadcasted_iota(jnp.int32, tile_set.shape[:2], 1) < tile_len[:, None]
    return jnp.where(inside[:, :, None], tile_set, tile_set[:, :1, :])


def local(queries, passages, lengths, candidates):
    peers = lax.axis_size("corpus")
    per_owner, tile_rows, feature = passages.shape
    per_device, query_tok = (queries.shape[0], queries.shape[1])
    candidate_ids = candidates[0]
    number = candidate_ids.shape[0]
    capacity = max(2, 3 * number // (2 * peers))
    owner_of = candidate_ids // per_owner
    local_id = candidate_ids - owner_of * per_owner
    position = jnp.arange(number, dtype=jnp.int32)
    shared = (owner_of[:, None] == owner_of[None, :]) & (position[None, :] < position[:, None])
    rank_in = jnp.sum(shared.astype(jnp.int32), axis=1)
    slot_of = owner_of * capacity + rank_in
    matches = slot_of[None, :] == jnp.arange(peers * capacity, dtype=jnp.int32)[:, None]
    wanted = jnp.max(jnp.where(matches, local_id[None, :], -1), axis=1).reshape(peers, capacity)
    asked = lax.all_to_all(wanted, "corpus", split_axis=0, concat_axis=0, tiled=True)
    picked = jnp.maximum(asked.reshape(-1), 0)
    chosen = fill_rows(passages[picked], lengths[picked])
    by_scorer = chosen.reshape(peers, capacity, tile_rows, feature)
    stacked = queries.reshape(1, per_device * query_tok, feature)
    piece = lax.all_gather(stacked, "corpus", axis=0, tiled=True)
    shards_here = piece.shape[0]
    group_size = math.gcd(shards_here, 8)
    turns = shards_here // group_size
    query_groups = piece.reshape(turns, group_size, piece.shape[1], feature)
    tile_groups = by_scorer.reshape(turns, group_size, capacity, tile_rows, feature)
    fresh_scores = lax.map(
        lambda paired: maxsim_many(paired[0], paired[1], per_device), (query_groups, tile_groups)
    )
    fresh_scores = fresh_scores.reshape(shards_here, per_device, capacity)
    returned = lax.all_to_all(fresh_scores, "corpus", split_axis=0, concat_axis=0, tiled=True)
    spread = jnp.transpose(returned, (1, 0, 2)).reshape(per_device, peers * capacity)
    scores = jnp.take(spread, slot_of, axis=1)
    best_scores = lax.top_k(scores, TOPK)[0]
    return (scores, best_scores)


def solution(mesh):
    return jax.shard_map(
        local,
        mesh=mesh,
        in_specs=(
            P(("groups", "corpus"), None, None),
            P(("groups", "corpus"), None, None),
            P(("groups", "corpus")),
            P(("groups", "corpus"), None),
        ),
        out_specs=(P(("groups", "corpus"), None), P(("groups", "corpus"), None)),
        check_vma=False,
    )
```

profile of v0, /device:TPU:0, one launch (start us, length us, event | category | flops | bytes accessed | tf_op | source)
XLA Modules:
  0.0 137.6 jit_solution(5977993929277204286)
XLA Ops:
  7.2 0.0 copy-start
  7.2 0.0 all-gather.2.cloned.1.call-start
  7.2 0.7 all-gather.2.cloned.1.call-update
  7.9 0.7 subtract_bitcast_fusion
  8.6 0.7 and_select_fusion.2
  9.2 0.2 convert_reduce_fusion
  9.4 0.1 select_reduce_fusion
  9.6 0.7 all_to_all.9
  10.3 7.4 %all-to-all-start = ((s32[16,1,12]{2,1,0:T(1,128)}), s32[16,1,12]{2,1,0:T(1,128)S(1)}, u32[]{:S(2)}, u32[]{:S(2)}) async-start(s32[16,1,12]{2,1,0:T(1,128)} %bitcast.12), calls=%async_computation | async-start | bytes 16384 | tf_op jit(solution)/shard_map/all_to_all | solution.py:43
  17.7 0.7 fusion.6
  18.3 0.7 compare_and_fusion
  19.0 5.0 %all-to-all-done = s32[16,1,12]{2,1,0:T(1,128)S(1)} async-done(((s32[16,1,12]{2,1,0:T(1,128)}), s32[16,1,12]{2,1,0:T(1,128)S(1)}, u32[]{:S(2)}, u32[]{:S(2)}) %all-to-all-start) | async-done | bytes 800 | tf_op jit(solution)/shard_map/all_to_all | solution.py:43
  24.0 0.1 reshape.184
  24.1 10.2 %gather_fusion.1 = bf16[192,128,128]{2,1,0:T(8,128)(2,1)} fusion(bf16[128,128,128]{2,1,0:T(8,128)(2,1)} %param.7, s32[1024]{0:T(1024)S(1)} %pad_clamp_fusion.1), kind=kCustom, calls=%fused_computation.1 | custom fusion | bytes 12583680 | tf_op jit(solution)/shard_map/gather | solution.py:45
  34.3 1.3 slice_reduce_fusion
  35.6 0.0 copy-done
  35.6 1.6 %gather_fusion = s32[192]{0:T(256)S(1)} fusion(s32[128]{0:T(128)S(1)} %copy-done, s32[1024]{0:T(1024)S(1)} %pad_clamp_fusion.1), kind=kCustom, calls=%fused_computation | custom fusion | bytes 2304 | tf_op jit(solution)/shard_map/gather | solution.py:45
  37.2 0.1 lt.53
  37.2 0.1 iota_compare_fusion
  37.4 6.5 %broadcast_select_fusion = bf16[2,8,12,128,128]{4,3,2,1,0:T(8,128)(2,1)} fusion(bf16[2,8,12,128,128]{4,3,2,1,0:T(8,128)(2,1)} %bitcast.73, pred[2,8,12,128]{3,2,1,0:T(8,128)(4,1)S(1)} %iota_compare_fusion, bf16[2,8,12,128]{3,2,1,0:T(8,128)(2,1)S(1)} %broadcast_in_dim.64), kind=kLoop, calls=%fused_computation.10 | loop fusion | flops 3145728 | bytes 12656640 | tf_op jit(solution)/shard_map/jit(_where)/select_n | solution.py:25
  43.9 37.4 %all-gather.2.cloned.1.call-done = bf16[16,1792,128]{2,1,0:T(8,128)(2,1)} async-done(((bf16[1,1792,128]{2,1,0:T(8,128)(2,1)}), bf16[16,1792,128]{2,1,0:T(8,128)(2,1)}) %all-gather.2.cloned.1.call-update) | async-done | bytes 7340048 | tf_op jit(solution)/shard_map/all_gather | solution.py:48
  81.3 32.9 %while.10 = (s32[]{:T(128)}, f32[2,8,56,12]{2,1,0,3:T(8,128)S(1)}, bf16[2,8,1792,128]{3,2,1,0:T(8,128)(2,1)}, bf16[2,8,12,128,128]{4,3,2,1,0:T(8,128)(2,1)}, s32[]{:T(128)}, /*index=5*/f32[]{:T(128)}) while((s32[]{:T(128)}, f32[2,8,56,12]{2,1,0,3:T(8,128)S(1)}, bf16[2,8,1792,128]{3,2,1,0:T(8,128)(2,1)}, ...), condition=%wide.region_5.6_spmd, body=%wide.region_2.5_spmd.sunk | while | flops 5659164672 | bytes 11065421 | solution.py:54
  81.3 14.4 %convolution_reduce_fusion.2 = f32[8,1792,12]{1,2,0:T(8,128)S(1)} fusion(bf16[2,8,1792,128]{3,2,1,0:T(8,128)(2,1)} %get-tuple-element.87, s32[]{:T(128)} %get-tuple-element.79, bf16[2,8,12,128,128]{4,3,2,1,0:T(8,128)(2,1)} %get-tuple-element.88), kind=kOutput, calls=%fused_computation.3.clone.1 | convolution fusion | flops 5658992640 | bytes 7504896 | tf_op jit(solution)/shard_map/while/body/eval_jaxpr/srd,sgpd->srgp/dot_general | solution.py:12
  95.7 0.4 copy.35
  96.2 0.8 reshape.220
  97.0 0.8 reduce_sum.27
  97.8 14.4 %convolution_reduce_fusion.2 = f32[8,1792,12]{1,2,0:T(8,128)S(1)} fusion(bf16[2,8,1792,128]{3,2,1,0:T(8,128)(2,1)} %get-tuple-element.87, s32[]{:T(128)} %get-tuple-element.79, bf16[2,8,12,128,128]{4,3,2,1,0:T(8,128)(2,1)} %get-tuple-element.88), kind=kOutput, calls=%fused_computation.3.clone.1 | convolution fusion | flops 5658992640 | bytes 7504896 | tf_op jit(solution)/shard_map/while/body/eval_jaxpr/srd,sgpd->srgp/dot_general | solution.py:12
  112.2 0.4 copy.35
  112.6 0.8 reshape.220
  113.4 0.8 reduce_sum.27
  114.3 0.8 reshape.217
  115.1 3.5 %all-to-all-start.1 = ((f32[16,1,672]{2,1,0:T(1,128)}), f32[16,1,672]{2,1,0:T(1,128)S(1)}, u32[]{:S(2)}, u32[]{:S(2)}) async-start(f32[16,1,672]{2,1,0:T(1,128)} %reshape.217), calls=%async_computation.1 | async-start | bytes 98304 | tf_op jit(solution)/shard_map/all_to_all | solution.py:58
  118.6 6.7 %all-to-all-done.1 = f32[16,1,672]{2,1,0:T(1,128)S(1)} async-done(((f32[16,1,672]{2,1,0:T(1,128)}), f32[16,1,672]{2,1,0:T(1,128)S(1)}, u32[]{:S(2)}, u32[]{:S(2)}) %all-to-all-start.1) | async-done | bytes 43040 | tf_op jit(solution)/shard_map/all_to_all | solution.py:58
  125.3 0.5 broadcast.219
  125.8 0.8 reduce.6
  126.6 0.1 reshape.218
  126.7 0.6 gather_fusion.2
  127.4 0.1 select_bitcast_fusion
  127.5 0.1 copy.27
  127.5 0.0 copy-start.1
  127.6 3.2 %top_k.9 = (f32[56,128]{1,0:T(8,128)}, s32[56,128]{1,0:T(8,128)}) sort(f32[56,128]{1,0:T(8,128)S(1)} %copy.27, s32[56,128]{1,0:T(8,128)S(1)} %iota.22), dimensions={1}, to_apply=%region_6.7 | sort | flops 93184 | bytes 114688 | tf_op jit(solution)/shard_map/top_k | solution.py:61
  130.7 0.0 copy-done.1
  (12 shorter events, 0.1 us)
Async XLA Ops:
  7.2 28.4 %copy-start = (s32[128]{0:T(128)S(1)}, s32[128]{0:T(128)}, u32[]{:S(2)}) copy-start(s32[128]{0:T(128)} %param.8) | copy-start | bytes 1540
  7.2 74.1 %all-gather.2.cloned.1.call-start = ((), (), s32[]{:S(2)}) async-start(), calls=%async_computation.2 | async-start | bytes 7798784 | tf_op jit(solution)/shard_map/all_gather | solution.py:48
  10.3 13.7 %all-to-all-start = ((s32[16,1,12]{2,1,0:T(1,128)}), s32[16,1,12]{2,1,0:T(1,128)S(1)}, u32[]{:S(2)}, u32[]{:S(2)}) async-start(s32[16,1,12]{2,1,0:T(1,128)} %bitcast.12), calls=%async_computation | async-start | bytes 16384 | tf_op jit(solution)/shard_map/all_to_all | solution.py:43
  115.1 10.2 %all-to-all-start.1 = ((f32[16,1,672]{2,1,0:T(1,128)}), f32[16,1,672]{2,1,0:T(1,128)S(1)}, u32[]{:S(2)}, u32[]{:S(2)}) async-start(f32[16,1,672]{2,1,0:T(1,128)} %reshape.217), calls=%async_computation.1 | async-start | bytes 98304 | tf_op jit(solution)/shard_map/all_to_all | solution.py:58
  127.5 3.2 %copy-start.1 = (f32[56,128]{1,0:T(8,128)}, f32[56,128]{1,0:T(8,128)S(1)}, u32[]{:S(2)}) copy-start(f32[56,128]{1,0:T(8,128)S(1)} %copy.27) | copy-start | bytes 86020
Sparse Core Ops, SparseCore 0:
  10.3 70.9 all-gather.1
where the time goes:
time: 138 us
  waiting for transfers between devices  49.8 us (36%)
  matrix products  28.9 us (21%)
  local copies, waits for them, and re-layouts  18.4 us (13%)
  other arithmetic  15.3 us (11%)
  between operations  14.2 us (10%)
  starting transfers between devices  10.9 us (8%)
    all_gather x1, waiting for transfers between devices, local(): piece = lax.all_gather(stacked, 'corpus', axis=0, tiled=True)  37.4 us
    dot_general x2, matrix products, maxsim_many(): jnp.einsum('srd,sgpd->srgp', query_sets, tile_sets, preferred_element_typ...  28.9 us
    gather x2, local copies, waits for them, and re-layouts, local(): chosen = fill_rows(passages[picked], lengths[picked])  11.7 us
    all_to_all x1, starting transfers between devices, local(): lax.all_to_all(wanted, 'corpus', split_axis=0, concat_axis=0, tiled=True)  7.4 us
    all_to_all x1, waiting for transfers between devices, local(): lax.all_to_all(fresh_scores, 'corpus', split_axis=0, concat_axis=0, tiled...  6.71 us
    select_n x1, other arithmetic, fill_rows(): return jnp.where(inside[:, :, None], tile_set, tile_set[:, :1, :])  6.55 us
    all_to_all x1, waiting for transfers between devices, local(): lax.all_to_all(wanted, 'corpus', split_axis=0, concat_axis=0, tiled=True)  4.99 us
    all_to_all x1, starting transfers between devices, local(): lax.all_to_all(fresh_scores, 'corpus', split_axis=0, concat_axis=0, tiled...  3.5 us
  transfers between devices with their start and end apart: 3, of which 3 were waited for; matrix products, arithmetic and copies ran while one was open for 17% of the time, Pallas kernels for 0%

commit v1 on v0

v1 whole, which is shorter than its diff:
```python
import functools
import math

import jax
import jax.numpy as jnp
import numpy as np
from jax import lax
from jax.experimental import pallas as pl
from jax.experimental.pallas import tpu as pltpu
from jax.sharding import PartitionSpec as P

TOPK = 100
CORES = 2
LANES = 128
VMEM_LIMIT = 44 * 1024 * 1024


def ring_order(chips):
    return list(range(0, chips, 2)) + list(range(1, chips, 2))[::-1]


def split_exact(x):
    high = x.astype(jnp.bfloat16)
    rest = x - high.astype(jnp.float32)
    middle = rest.astype(jnp.bfloat16)
    low = (rest - middle.astype(jnp.float32)).astype(jnp.bfloat16)
    return high, middle, low


def score_kernel(
    blocks, slots, group, width, per_device, query_tok, offsets,
    plan, lens, rows, *refs,
):
    halves = refs[: 2 * blocks]
    own, other, out, tiles, best, pick, sems = refs[2 * blocks :]
    per_owner, tile_rows, feature = own.shape
    half_rows = halves[0].shape[0]
    query_rows = 2 * half_rows

    def copy(b, i, tile, source):
        return pltpu.make_async_copy(source.at[tile], tiles.at[b, i], sems.at[b, i])

    counts = []
    for b in range(blocks):
        row = rows[offsets[b]]
        count = plan[row, slots]
        counts.append(count)

        def begin(i, carry, b=b, row=row):
            tile = plan[row, i]

            @pl.when(tile < per_owner)
            def _():
                copy(b, i, tile, own).start()

            @pl.when(tile >= per_owner)
            def _():
                copy(b, i, tile - per_owner, other).start()

            return carry

        lax.fori_loop(0, count, begin, 0)

    token_query = lax.broadcasted_iota(jnp.int32, (query_rows, LANES), 0) // query_tok
    query_lane = lax.broadcasted_iota(jnp.int32, (query_rows, LANES), 1)
    pick[...] = (token_query == query_lane).astype(jnp.float32).astype(jnp.bfloat16)
    tile_row = lax.broadcasted_iota(jnp.int32, (tile_rows, feature), 0)

    for b in range(blocks):
        row = rows[offsets[b]]
        count = counts[b]

        def fill(i, carry, b=b, row=row):
            copy(b, i, 0, own).wait()
            tile = tiles[b, i].astype(jnp.float32)
            inside = tile_row < lens[plan[row, i]]
            tiles[b, i] = jnp.where(inside, tile, tile[0:1, :]).astype(jnp.bfloat16)
            return carry

        lax.fori_loop(0, count, fill, 0)

        def chunk(start, size, b=b):
            first, second = halves[2 * b], halves[2 * b + 1]
            if start + size <= half_rows:
                return first[start : start + size, :]
            if start >= half_rows:
                return second[start - half_rows : start - half_rows + size, :]
            return jnp.concatenate(
                [first[start:, :], second[: start + size - half_rows, :]], axis=0
            )

        def score_group(g, carry, b=b):
            start = pl.multiple_of(g * group, group)
            left = tiles[b, pl.ds(start, group)].reshape(group * tile_rows, feature)
            for at in range(0, query_rows, width):
                size = min(width, query_rows - at)
                similar = lax.dot_general(
                    left, chunk(at, size), (((1,), (1,)), ((), ())),
                    preferred_element_type=jnp.float32,
                )
                nearest = jnp.max(similar.reshape(group, tile_rows // 8, 8, size), axis=1)
                best[pl.ds(start, group), :, at : at + size] = nearest
            return carry

        lax.fori_loop(0, pl.cdiv(count, group), score_group, 0)
        nearest = jnp.max(best[...], axis=1)
        total = jnp.zeros((slots, LANES), jnp.float32)
        for part in split_exact(nearest):
            total += jnp.dot(part, pick[...], preferred_element_type=jnp.float32)
        used = lax.broadcasted_iota(jnp.int32, (slots, LANES), 0) < count
        out[b] = jnp.where(used, total / float(query_tok), 0.0)


def score(offsets, slots, per_device, query_tok, plan, lens, rows, halves, own, other):
    blocks = len(offsets)
    per_owner, tile_rows, feature = own.shape
    query_rows = 2 * halves[0].shape[0]
    flops = 2 * blocks * slots * tile_rows * feature * query_rows
    return pl.pallas_call(
        functools.partial(
            score_kernel, blocks, slots, math.gcd(slots, 4), 256, per_device, query_tok, offsets
        ),
        out_shape=jax.ShapeDtypeStruct((blocks, slots, LANES), jnp.float32),
        grid_spec=pltpu.PrefetchScalarGridSpec(
            num_scalar_prefetch=3,
            grid=(),
            in_specs=[pl.BlockSpec(memory_space=pltpu.VMEM)] * (2 * blocks)
            + [pl.BlockSpec(memory_space=pl.ANY)] * 2,
            out_specs=pl.BlockSpec(memory_space=pltpu.VMEM),
            scratch_shapes=[
                pltpu.VMEM((blocks, slots, tile_rows, feature), jnp.bfloat16),
                pltpu.VMEM((slots, 8, query_rows), jnp.float32),
                pltpu.VMEM((query_rows, LANES), jnp.bfloat16),
                pltpu.SemaphoreType.DMA((blocks, slots)),
            ],
        ),
        compiler_params=pltpu.CompilerParams(vmem_limit_bytes=VMEM_LIMIT),
        cost_estimate=pl.CostEstimate(
            flops=3 * flops,
            bytes_accessed=blocks * (slots * tile_rows + query_rows) * feature * 2,
            transcendentals=0,
        ),
        name="score",
    )(plan, lens, rows, *halves, own, other)


def sort_descending(parts, lanes):
    parts = list(parts)
    many = len(parts)
    number = many * 8
    sub = lax.broadcasted_iota(jnp.int32, (8, lanes), 0)
    size = 2
    while size <= number:
        reach = size // 2
        while reach >= 1:
            if reach < many:
                for v in range(many):
                    if v & reach:
                        continue
                    a, b = parts[v], parts[v | reach]
                    high, low = jnp.maximum(a, b), jnp.minimum(a, b)
                    if size >= number:
                        parts[v], parts[v | reach] = high, low
                    elif size < many:
                        down = (v & size) == 0
                        parts[v], parts[v | reach] = (high, low) if down else (low, high)
                    else:
                        down = (sub & (size // many)) == 0
                        parts[v] = jnp.where(down, high, low)
                        parts[v | reach] = jnp.where(down, low, high)
            else:
                step = reach // many
                is_first = (sub & step) == 0
                if size >= number:
                    keep_high = is_first
                else:
                    keep_high = is_first == ((sub & (size // many)) == 0)
                for v in range(many):
                    x = parts[v]
                    partner = jnp.where(is_first, pltpu.roll(x, 8 - step, 0), pltpu.roll(x, step, 0))
                    parts[v] = jnp.where(keep_high, jnp.maximum(x, partner), jnp.minimum(x, partner))
            reach //= 2
        size *= 2
    return parts


def finish_kernel(arrays, per_device, topk, slot_of, *refs):
    returned = refs[:arrays]
    scores, best_scores, spread, ranked = refs[arrays:]
    number = slot_of.shape[0]
    at = 0
    for ref in returned:
        rows = ref.shape[0] * ref.shape[1]
        spread[at : at + rows, :] = ref[...].reshape(rows, LANES)
        at += rows
    total = spread.shape[0]
    lane = lax.broadcasted_iota(jnp.int32, (number, total), 1)
    choose = (slot_of[...] == lane).astype(jnp.float32).astype(jnp.bfloat16)
    by_candidate = jnp.zeros((number, LANES), jnp.float32)
    for part in split_exact(spread[...]):
        by_candidate += jnp.dot(choose, part, preferred_element_type=jnp.float32)
    scores[...] = by_candidate.T[:per_device, :]
    many = number // 8
    parts = sort_descending([by_candidate[8 * v : 8 * v + 8, :] for v in range(many)], LANES)
    for v in range(many):
        ranked[pl.ds(v, 8, stride=many), :] = parts[v]
    best_scores[...] = ranked[...].T[:per_device, :topk]


def finish(per_device, slot_of, returned):
    number = slot_of.shape[0]
    total = sum(r.shape[0] * r.shape[1] for r in returned)
    return pl.pallas_call(
        functools.partial(finish_kernel, len(returned), per_device, TOPK),
        out_shape=(
            jax.ShapeDtypeStruct((per_device, number), jnp.float32),
            jax.ShapeDtypeStruct((per_device, TOPK), jnp.float32),
        ),
        in_specs=[pl.BlockSpec(memory_space=pltpu.VMEM)] * (1 + len(returned)),
        out_specs=(pl.BlockSpec(memory_space=pltpu.VMEM),) * 2,
        scratch_shapes=[
            pltpu.VMEM((total, LANES), jnp.float32),
            pltpu.VMEM((number, LANES), jnp.float32),
        ],
        compiler_params=pltpu.CompilerParams(vmem_limit_bytes=VMEM_LIMIT),
        name="finish",
    )(slot_of, *returned)


def local(queries, passages, lengths, candidates):
    peers = lax.axis_size("corpus")
    chips = peers // CORES
    per_owner, tile_rows, feature = passages.shape
    per_device, query_tok = queries.shape[0], queries.shape[1]
    number = candidates.shape[1]
    capacity = max(2, 3 * number // (2 * peers))
    slots = -(-CORES * capacity // 8) * 8
    per_chip = CORES * per_owner
    order = ring_order(chips)
    place = [order.index(chip) for chip in range(chips)]

    def moved(x, distance):
        pairs = [
            (order[i] * CORES + core, order[(i + distance) % chips] * CORES + core)
            for i in range(chips)
            for core in range(CORES)
        ]
        return lax.ppermute(x, "corpus", pairs)

    swap = [(i, i ^ 1) for i in range(peers)]
    me = lax.axis_index("corpus")
    core = me % CORES
    chip = me // CORES
    my_place = jnp.asarray(place, jnp.int32)[chip]

    half = per_device // 2
    first = queries[:half].reshape(half * query_tok, feature)
    second = queries[half:].reshape(half * query_tok, feature)
    arrived = {0: (first, second)}
    middle = chips // 2

    def send_on(step):
        if step < middle:
            arrived[step] = tuple(moved(x, 1) for x in arrived[step - 1])
            arrived[-step] = tuple(moved(x, -1) for x in arrived[1 - step])
        else:
            arrived[step] = (moved(arrived[step - 1][0], 1), moved(arrived[1 - step][1], -1))

    send_on(1)
    other = lax.ppermute(passages, "corpus", swap)
    facts = lax.all_gather(
        jnp.concatenate([candidates[0], lengths])[None, :], "corpus", axis=0, tiled=True
    ).reshape(chips, CORES, number + per_owner)
    listed = lax.dynamic_index_in_dim(facts, core, 1, keepdims=False)[:, :number]
    other_lengths = lax.dynamic_slice(
        facts, (chip, 1 - core, number), (1, 1, per_owner)
    ).reshape(per_owner)
    lens = jnp.concatenate([lengths, other_lengths])

    position = jnp.arange(number, dtype=jnp.int32)
    before = position[None, :] < position[:, None]
    mine = listed // per_chip == chip
    rank = jnp.sum((mine[:, None, :] & before[None]).astype(jnp.int32), axis=2)
    tile = listed % per_chip
    tile = jnp.where(tile // per_owner == core, tile % per_owner, per_owner + tile % per_owner)
    at_slot = mine[:, None, :] & (rank[:, None, :] == jnp.arange(slots, dtype=jnp.int32)[None, :, None])
    plan = jnp.max(jnp.where(at_slot, tile[:, None, :], 0), axis=2)
    count = jnp.sum(mine.astype(jnp.int32), axis=1, keepdims=True)
    plan = jnp.concatenate([plan, count], axis=1)
    rows = jnp.asarray(order, jnp.int32)[(my_place - jnp.arange(chips, dtype=jnp.int32)) % chips]

    ids = candidates[0]
    chip_of = ids // per_chip
    rank_in = jnp.sum(((chip_of[:, None] == chip_of[None, :]) & before).astype(jnp.int32), axis=1)
    ahead = (jnp.asarray(place, jnp.int32)[chip_of] - my_place) % chips
    slot_of = (ahead * slots + rank_in)[:, None]

    def run(offsets):
        halves = [x for offset in offsets for x in arrived[offset]]
        return score(
            tuple(offset % chips for offset in offsets), slots, per_device, query_tok,
            plan, lens, rows, halves, passages, other,
        )

    back = {}

    def keep(offsets, fresh):
        for k, offset in enumerate(offsets):
            result = fresh[k : k + 1]
            back[offset % chips] = moved(result, -offset) if offset else result

    for step in range(1, middle + 1):
        if step < middle:
            send_on(step + 1)
        offsets = (0, 1, -1) if step == 1 else (middle,) if step == middle else (step, -step)
        fresh = run(offsets)
        if step < middle:
            names = [step + 1, -step - 1] if step + 1 < middle else [middle]
            held, fresh = lax.optimization_barrier(([arrived[name] for name in names], fresh))
            arrived.update(zip(names, held))
        keep(offsets, fresh)
    return finish(per_device, slot_of, [back[j] for j in range(chips)])


def solution(mesh):
    return jax.shard_map(
        local,
        mesh=mesh,
        in_specs=(
            P(("groups", "corpus"), None, None),
            P(("groups", "corpus"), None, None),
            P(("groups", "corpus")),
            P(("groups", "corpus"), None),
        ),
        out_specs=(P(("groups", "corpus"), None), P(("groups", "corpus"), None)),
        check_vma=False,
    )
```

time: 138 us -> 112 us (0.81)
  waiting for transfers between devices: 49.8 us -> 3.96 us
  Pallas kernels: 0 us -> 45.5 us
  matrix products: 28.9 us -> 0 us
  blocking collectives: 0 us -> 23.4 us
  starting transfers between devices: 10.9 us -> 26.1 us
  between operations: 14.2 us -> 0.92 us
  local copies, waits for them, and re-layouts: 18.4 us -> 6.92 us
  other arithmetic: 15.3 us -> 5.16 us
    pallas_call x0 -> x5, Pallas kernels: none -> 45.5 us  [the longest x4 44.4 us: score(): pl.pallas_call(functools.partial(score_kernel, blocks, slots, math.gcd(sl...]
    all_gather x1 -> x0, waiting for transfers between devices: 37.4 us -> none  [local(): piece = lax.all_gather(stacked, 'corpus', axis=0, tiled=True)]
    dot_general x2 -> x0, matrix products: 28.9 us -> none  [maxsim_many(): jnp.einsum('srd,sgpd->srgp', query_sets, tile_sets, preferred_element_typ...]
    ppermute x0 -> x22, starting transfers between devices: none -> 26.1 us  [the longest x21 25.6 us: moved(): return lax.ppermute(x, 'corpus', pairs)]
    all_gather x0 -> x1, blocking collectives: none -> 23.4 us  [local(): lax.all_gather(jnp.concatenate([candidates[0], lengths])[None, :], 'corpu...]
    all_to_all x2 -> x0, waiting for transfers between devices: 11.7 us -> none  [the longest x1 6.71 us: local(): lax.all_to_all(fresh_scores, 'corpus', split_axis=0, concat_axis=0, tiled...]
    gather x3 -> x1, local copies, waits for them, and re-layouts: 12.4 us -> 1.29 us  [local(): jnp.asarray(order, jnp.int32)]
    all_to_all x2 -> x0, starting transfers between devices: 10.9 us -> none  [the longest x1 7.4 us: local(): lax.all_to_all(wanted, 'corpus', split_axis=0, concat_axis=0, tiled=True)]
  transfers between devices with their start and end apart: 3 -> 22, of which waited for: 3 -> 3; matrix products, arithmetic and copies ran while one was open for 17% -> 9% of each run, Pallas kernels for 0% -> 40%
where the time goes in v1:
time: 112 us
  Pallas kernels  45.5 us (41%)
  starting transfers between devices  26.1 us (23%)
  blocking collectives  23.4 us (21%)
  local copies, waits for them, and re-layouts  6.92 us (6%)
  other arithmetic  5.16 us (5%)
  waiting for transfers between devices  3.96 us (4%)
    pallas_call x4, Pallas kernels, score(): pl.pallas_call(functools.partial(score_kernel, blocks, slots, math.gcd(sl...  44.4 us
    ppermute x21, starting transfers between devices, moved(): return lax.ppermute(x, 'corpus', pairs)  25.6 us
    all_gather x1, blocking collectives, local(): lax.all_gather(jnp.concatenate([candidates[0], lengths])[None, :], 'corpu...  23.4 us
    ppermute x21, waiting for transfers between devices, moved(): return lax.ppermute(x, 'corpus', pairs)  3.95 us
  transfers between devices with their start and end apart: 22, of which 3 were waited for; matrix products, arithmetic and copies ran while one was open for 9% of the time, Pallas kernels for 40%

profile of v1, /device:TPU:0, one launch (start us, length us, event | category | flops | bytes accessed | tf_op | source)
XLA Modules:
  0.0 112.1 jit_solution(12496308230549553725)
XLA Ops:
  0.6 0.5 collective-permute-start.8
  1.1 1.1 fusion.17
  2.2 2.6 %collective-permute-start = (bf16[896,128]{1,0:T(8,128)(2,1)S(1)}, bf16[896,128]{1,0:T(8,128)(2,1)S(1)}, u32[]{:S(2)}, u32[]{:S(2)}) collective-permute-start(bf16[896,128]{1,0:T(8,128)(2,1)S(1)} %bitcast.23), channel_id=1, source_target_pairs={{0,4},{1,5},{4,8},{5,9},{8,12},{9,13},{12,14},{13,15},{14,10},{15,... | collective-permute-start | bytes 688136 | tf_op jit(solution)/shard_map/ppermute | solution.py:248
  4.9 0.0 collective-permute-start.4
  4.9 2.0 %collective-permute-start.2 = (bf16[896,128]{1,0:T(8,128)(2,1)S(1)}, bf16[896,128]{1,0:T(8,128)(2,1)S(1)}, u32[]{:S(2)}, u32[]{:S(2)}) collective-permute-start(bf16[896,128]{1,0:T(8,128)(2,1)S(1)} %bitcast.20), channel_id=1, source_target_pairs={{0,4},{1,5},{4,8},{5,9},{8,12},{9,13},{12,14},{13,15},{14,10},{15,... | collective-permute-start | bytes 688136 | tf_op jit(solution)/shard_map/ppermute | solution.py:248
  6.9 0.0 collective-permute-start.6
  6.9 0.7 pad_add_fusion.1
  7.6 23.4 %all-gather.1 = s32[16,1,256]{2,1,0:T(1,128)S(1)} all-gather(s32[1,1,256]{2,1,0:T(1,128)S(1)} %bitcast.28), channel_id=2, replica_groups=mesh['groups'=2,'corpus'=16] {'corpus'}, dimensions={0}, use_global_device_ids=true | all-gather | bytes 17408 | tf_op jit(solution)/shard_map/all_gather | solution.py:271
  31.2 0.8 copy.45
  31.9 1.2 %dynamic_slice.10 = s32[1]{0:T(128)} dynamic-slice(s32[8]{0:T(128)} %constant.126.clone, s32[]{:T(128)S(6)} %select_n.118), dynamic_slice_sizes={1} | dynamic-slice | bytes 12 | tf_op jit(solution)/shard_map/dynamic_slice | solution.py:254
  33.2 0.7 fusion.13
  33.9 0.7 and_select_fusion.2
  34.5 0.7 fusion.15
  35.2 0.2 convert_reduce_fusion.1
  35.4 0.2 select_reduce_fusion.1
  35.5 0.1 compare_reduce_fusion
  35.7 0.1 convert_reduce_fusion.2
  35.8 0.2 convert_reduce_fusion
  36.0 0.7 fusion.14
  36.7 0.7 pad_add_fusion.2.lens
  37.4 0.1 copy.54
  37.4 0.1 copy.49
  37.5 0.1 copy.53
  37.7 1.3 %gather_fusion = s32[8]{0:T(128)S(1)} fusion(s32[8]{0:T(128)} %constant.127.clone, s32[1024]{0:T(1024)S(1)} %pad_clamp_fusion), kind=kCustom, calls=%fused_computation | custom fusion | bytes 96 | tf_op jit(solution)/shard_map/gather | solution.py:290
  39.0 0.2 select_reduce_fusion
  39.2 0.1 pad_add_fusion.plan
  39.3 0.0 collective-permute-done.refs_2_
  39.3 0.0 collective-permute-start.1
  39.3 0.0 collective-permute-done.2.refs_3_
  39.3 0.1 collective-permute-start.3
  39.4 2.0 %collective-permute-start.5 = (bf16[896,128]{1,0:T(8,128)(2,1)S(1)}, bf16[896,128]{1,0:T(8,128)(2,1)S(1)}, u32[]{:S(2)}, u32[]{:S(2)}) collective-permute-start(bf16[896,128]{1,0:T(8,128)(2,1)S(1)} %collective-permute-done.4.refs_4_), channel_id=1, source_target_pairs={{0,2},{1,3},{4,0},{5,1},{8,4},{9,5},{12,8},{13,9},{14,12},{15,13},... | collective-permute-start | bytes 688136 | tf_op jit(solution)/shard_map/ppermute | solution.py:248
  41.4 0.0 collective-permute-done.6.refs_5_
  41.4 2.0 %collective-permute-start.7 = (bf16[896,128]{1,0:T(8,128)(2,1)S(1)}, bf16[896,128]{1,0:T(8,128)(2,1)S(1)}, u32[]{:S(2)}, u32[]{:S(2)}) collective-permute-start(bf16[896,128]{1,0:T(8,128)(2,1)S(1)} %collective-permute-done.6.refs_5_), channel_id=1, source_target_pairs={{0,2},{1,3},{4,0},{5,1},{8,4},{9,5},{12,8},{13,9},{14,12},{15,13},... | collective-permute-start | bytes 688136 | tf_op jit(solution)/shard_map/ppermute | solution.py:248
  43.4 0.0 collective-permute-done.8.refs_7_.refs_5_.refs_3_
  43.4 2.2 %copy-done = bf16[128,128,128]{2,1,0:T(8,128)(2,1)S(1)} copy-done((bf16[128,128,128]{2,1,0:T(8,128)(2,1)S(1)}, bf16[128,128,128]{2,1,0:T(8,128)(2,1)}, u32[]{:S(2)}) %copy-start) | copy-done | bytes 4194328
  45.5 15.9 %score.4 = f32[3,24,128]{2,1,0:T(8,128)S(1)} custom-call(s32[8,25]{1,0:T(8,128)S(1)} %pad_add_fusion.plan, s32[256]{0:T(256)S(1)} %pad_add_fusion.2.lens, s32[8]{0:T(128)S(1)} %gather_fusion, bf16[896,128]{1,0:T(8,128)(2,1)S(1)} %bitcast.25, bf16[896,128]{1,0:T(8,128)(2,1)S(1)} %bitcast.22, bf16[896,128]{1,0:T(8,128)(2,1)S(1)} %collective-permute-done.refs_2_, ...), custom_call_target="tpu_custom_call" | custom-call | flops 12683575296 | bytes 3735552 | tf_op jit(solution)/shard_map/score/pallas_call | solution.py:119
  61.5 0.0 collective-permute-done.3.refs_1_
  61.5 0.0 collective-permute-done.5.refs_2_
  61.5 0.1 collective-permute-start.10
  61.6 0.9 collective-permute-start.11
  62.5 1.2 %collective-permute-start.12 = (bf16[896,128]{1,0:T(8,128)(2,1)S(1)}, bf16[896,128]{1,0:T(8,128)(2,1)S(1)}, u32[]{:S(2)}, u32[]{:S(2)}) collective-permute-start(bf16[896,128]{1,0:T(8,128)(2,1)S(1)} %collective-permute-done.5.refs_2_), channel_id=1, source_target_pairs={{0,2},{1,3},{4,0},{5,1},{8,4},{9,5},{12,8},{13,9},{14,12},{15,13},... | collective-permute-start | bytes 688136 | tf_op jit(solution)/shard_map/ppermute | solution.py:248
  63.7 2.0 %collective-permute-start.13 = (bf16[896,128]{1,0:T(8,128)(2,1)S(1)}, bf16[896,128]{1,0:T(8,128)(2,1)S(1)}, u32[]{:S(2)}, u32[]{:S(2)}) collective-permute-start(bf16[896,128]{1,0:T(8,128)(2,1)S(1)} %collective-permute-done.7.refs_3_), channel_id=1, source_target_pairs={{0,2},{1,3},{4,0},{5,1},{8,4},{9,5},{12,8},{13,9},{14,12},{15,13},... | collective-permute-start | bytes 688136 | tf_op jit(solution)/shard_map/ppermute | solution.py:248
  65.6 0.1 collective-permute-start.21
  65.7 10.5 %score.5 = f32[2,24,128]{2,1,0:T(8,128)S(1)} custom-call(s32[8,25]{1,0:T(8,128)S(1)} %pad_add_fusion.plan, s32[256]{0:T(256)S(1)} %pad_add_fusion.2.lens, s32[8]{0:T(128)S(1)} %gather_fusion, bf16[896,128]{1,0:T(8,128)(2,1)S(1)} %collective-permute-done.1.refs_0_, bf16[896,128]{1,0:T(8,128)(2,1)S(1)} %collective-permute-done.3.refs_1_, ...), custom_call_target="tpu_custom_call" | custom-call | flops 8455716864 | bytes 2490368 | tf_op jit(solution)/shard_map/score/pallas_call | solution.py:119
  76.2 0.0 collective-permute-done.10.refs_0_
  76.2 1.5 %collective-permute-start.9 = (f32[1,24,128]{2,1,0:T(8,128)S(1)}, f32[1,24,128]{2,1,0:T(8,128)S(1)}, u32[]{:S(2)}, u32[]{:S(2)}) collective-permute-start(f32[1,24,128]{2,1,0:T(8,128)S(1)} %get-tuple-element.37), channel_id=1, source_target_pairs={{0,2},{1,3},{4,0},{5,1},{8,4},{9,5},{12,8},{13,9},{14,12},{15,13},... | collective-permute-start | bytes 36872 | tf_op jit(solution)/shard_map/ppermute | solution.py:248
  77.7 0.0 collective-permute-done.12.refs_2_
  77.7 0.0 collective-permute-done.13.refs_3_
  77.7 0.6 collective-permute-start.15
  78.4 1.5 %collective-permute-start.16 = (bf16[896,128]{1,0:T(8,128)(2,1)S(1)}, bf16[896,128]{1,0:T(8,128)(2,1)S(1)}, u32[]{:S(2)}, u32[]{:S(2)}) collective-permute-start(bf16[896,128]{1,0:T(8,128)(2,1)S(1)} %collective-permute-done.13.refs_3_), channel_id=1, source_target_pairs={{0,2},{1,3},{4,0},{5,1},{8,4},{9,5},{12,8},{13,9},{14,12},{15,13},... | collective-permute-start | bytes 688136 | tf_op jit(solution)/shard_map/ppermute | solution.py:248
  79.8 0.0 collective-permute-start.14
  79.8 11.6 %score.6 = f32[2,24,128]{2,1,0:T(8,128)S(1)} custom-call(s32[8,25]{1,0:T(8,128)S(1)} %pad_add_fusion.plan, s32[256]{0:T(256)S(1)} %pad_add_fusion.2.lens, s32[8]{0:T(128)S(1)} %gather_fusion, bf16[896,128]{1,0:T(8,128)(2,1)S(1)} %collective-permute-done.10.refs_0_, bf16[896,128]{1,0:T(8,128)(2,1)S(1)} %collective-permute-done.11.refs_1_, ...), custom_call_target="tpu_custom_call" | custom-call | flops 8455716864 | bytes 2490368 | tf_op jit(solution)/shard_map/score/pallas_call | solution.py:119
  91.4 0.0 collective-permute-done.15.refs_0_
  91.4 2.9 %collective-permute-start.20 = (f32[1,24,128]{2,1,0:T(8,128)S(1)}, f32[1,24,128]{2,1,0:T(8,128)S(1)}, u32[]{:S(2)}, u32[]{:S(2)}) collective-permute-start(f32[1,24,128]{2,1,0:T(8,128)S(1)} %get-tuple-element.39), channel_id=1, source_target_pairs={{0,8},{1,9},{4,12},{5,13},{8,14},{9,15},{12,10},{13,11},{14,6},{15... | collective-permute-start | bytes 36872 | tf_op jit(solution)/shard_map/ppermute | solution.py:248
  94.3 0.0 collective-permute-done.16.refs_1_
  94.3 6.4 %score.7 = f32[1,24,128]{2,1,0:T(8,128)S(1)} custom-call(s32[8,25]{1,0:T(8,128)S(1)} %pad_add_fusion.plan, s32[256]{0:T(256)S(1)} %pad_add_fusion.2.lens, s32[8]{0:T(128)S(1)} %gather_fusion, bf16[896,128]{1,0:T(8,128)(2,1)S(1)} %collective-permute-done.15.refs_0_, bf16[896,128]{1,0:T(8,128)(2,1)S(1)} %collective-permute-done.16.refs_1_, ...), custom_call_target="tpu_custom_call" | custom-call | flops 4227858432 | bytes 1245184 | tf_op jit(solution)/shard_map/score/pallas_call | solution.py:119
  100.8 2.4 %collective-permute-start.18 = (f32[1,24,128]{2,1,0:T(8,128)S(1)}, f32[1,24,128]{2,1,0:T(8,128)S(1)}, u32[]{:S(2)}, u32[]{:S(2)}) collective-permute-start(f32[1,24,128]{2,1,0:T(8,128)S(1)} %score.7), channel_id=1, source_target_pairs={{0,14},{1,15},{4,10},{5,11},{8,6},{9,7},{12,2},{13,3},{14,0},{15,1... | collective-permute-start | bytes 36872 | tf_op jit(solution)/shard_map/ppermute | solution.py:248
  103.2 0.0 collective-permute-done.21.refs_7_
  103.2 2.3 %collective-permute-start.17 = (f32[1,24,128]{2,1,0:T(8,128)S(1)}, f32[1,24,128]{2,1,0:T(8,128)S(1)}, u32[]{:S(2)}, u32[]{:S(2)}) collective-permute-start(f32[1,24,128]{2,1,0:T(8,128)S(1)} %get-tuple-element.42), channel_id=1, source_target_pairs={{0,10},{1,11},{4,6},{5,7},{8,2},{9,3},{12,0},{13,1},{14,4},{15,5},... | collective-permute-start | bytes 36872 | tf_op jit(solution)/shard_map/ppermute | solution.py:248
  105.5 1.5 %collective-permute-start.19 = (f32[1,24,128]{2,1,0:T(8,128)S(1)}, f32[1,24,128]{2,1,0:T(8,128)S(1)}, u32[]{:S(2)}, u32[]{:S(2)}) collective-permute-start(f32[1,24,128]{2,1,0:T(8,128)S(1)} %get-tuple-element.41), channel_id=1, source_target_pairs={{0,12},{1,13},{4,14},{5,15},{8,10},{9,11},{12,6},{13,7},{14,2},{15... | collective-permute-start | bytes 36872 | tf_op jit(solution)/shard_map/ppermute | solution.py:248
  107.1 0.2 collective-permute-done.18.refs_4_
  107.3 1.4 %collective-permute-done.17.refs_3_ = f32[1,24,128]{2,1,0:T(8,128)S(1)} collective-permute-done((f32[1,24,128]{2,1,0:T(8,128)S(1)}, f32[1,24,128]{2,1,0:T(8,128)S(1)}, u32[]{:S(2)}, u32[]{:S(2)}) %collective-permute-start.17) | collective-permute-done | bytes 12320 | tf_op jit(solution)/shard_map/ppermute | solution.py:248
  108.7 2.3 %collective-permute-done.19.refs_5_ = f32[1,24,128]{2,1,0:T(8,128)S(1)} collective-permute-done((f32[1,24,128]{2,1,0:T(8,128)S(1)}, f32[1,24,128]{2,1,0:T(8,128)S(1)}, u32[]{:S(2)}, u32[]{:S(2)}) %collective-permute-start.19) | collective-permute-done | bytes 12320 | tf_op jit(solution)/shard_map/ppermute | solution.py:248
  111.0 1.1 finish.1
  (22 shorter events, 0.2 us)
Async XLA Ops:
  0.6 42.7 %collective-permute-start.8 = (bf16[128,128,128]{2,1,0:T(8,128)(2,1)}, bf16[128,128,128]{2,1,0:T(8,128)(2,1)}, u32[]{:S(2)}, u32[]{:S(2)}) collective-permute-start(bf16[128,128,128]{2,1,0:T(8,128)(2,1)} %refs_2_.1), channel_id=1, source_target_pairs={{0,1},{1,0},{2,3},{3,2},{4,5},{5,4},{6,7},{7,6},{8,9},{9,8},{10,11... | collective-permute-start | bytes 12582920 | tf_op jit(solution)/shard_map/ppermute | solution.py:270
  2.2 37.0 %collective-permute-start = (bf16[896,128]{1,0:T(8,128)(2,1)S(1)}, bf16[896,128]{1,0:T(8,128)(2,1)S(1)}, u32[]{:S(2)}, u32[]{:S(2)}) collective-permute-start(bf16[896,128]{1,0:T(8,128)(2,1)S(1)} %bitcast.23), channel_id=1, source_target_pairs={{0,4},{1,5},{4,8},{5,9},{8,12},{9,13},{12,14},{13,15},{14,10},{15,... | collective-permute-start | bytes 688136 | tf_op jit(solution)/shard_map/ppermute | solution.py:248
  4.9 34.5 %collective-permute-start.4 = (bf16[896,128]{1,0:T(8,128)(2,1)S(1)}, bf16[896,128]{1,0:T(8,128)(2,1)S(1)}, u32[]{:S(2)}, u32[]{:S(2)}) collective-permute-start(bf16[896,128]{1,0:T(8,128)(2,1)S(1)} %bitcast.24), channel_id=1, source_target_pairs={{0,2},{1,3},{4,0},{5,1},{8,4},{9,5},{12,8},{13,9},{14,12},{15,13},... | collective-permute-start | bytes 688136 | tf_op jit(solution)/shard_map/ppermute | solution.py:248
  4.9 34.4 %collective-permute-start.2 = (bf16[896,128]{1,0:T(8,128)(2,1)S(1)}, bf16[896,128]{1,0:T(8,128)(2,1)S(1)}, u32[]{:S(2)}, u32[]{:S(2)}) collective-permute-start(bf16[896,128]{1,0:T(8,128)(2,1)S(1)} %bitcast.20), channel_id=1, source_target_pairs={{0,4},{1,5},{4,8},{5,9},{8,12},{9,13},{12,14},{13,15},{14,10},{15,... | collective-permute-start | bytes 688136 | tf_op jit(solution)/shard_map/ppermute | solution.py:248
  6.9 34.5 %collective-permute-start.6 = (bf16[896,128]{1,0:T(8,128)(2,1)S(1)}, bf16[896,128]{1,0:T(8,128)(2,1)S(1)}, u32[]{:S(2)}, u32[]{:S(2)}) collective-permute-start(bf16[896,128]{1,0:T(8,128)(2,1)S(1)} %bitcast.21), channel_id=1, source_target_pairs={{0,2},{1,3},{4,0},{5,1},{8,4},{9,5},{12,8},{13,9},{14,12},{15,13},... | collective-permute-start | bytes 688136 | tf_op jit(solution)/shard_map/ppermute | solution.py:248
  39.3 22.2 %collective-permute-start.1 = (bf16[896,128]{1,0:T(8,128)(2,1)S(1)}, bf16[896,128]{1,0:T(8,128)(2,1)S(1)}, u32[]{:S(2)}, u32[]{:S(2)}) collective-permute-start(bf16[896,128]{1,0:T(8,128)(2,1)S(1)} %collective-permute-done.refs_2_), channel_id=1, source_target_pairs={{0,4},{1,5},{4,8},{5,9},{8,12},{9,13},{12,14},{13,15},{14,10},{15,... | collective-permute-start | bytes 688136 | tf_op jit(solution)/shard_map/ppermute | solution.py:248
  39.3 22.2 %collective-permute-start.3 = (bf16[896,128]{1,0:T(8,128)(2,1)S(1)}, bf16[896,128]{1,0:T(8,128)(2,1)S(1)}, u32[]{:S(2)}, u32[]{:S(2)}) collective-permute-start(bf16[896,128]{1,0:T(8,128)(2,1)S(1)} %collective-permute-done.2.refs_3_), channel_id=1, source_target_pairs={{0,4},{1,5},{4,8},{5,9},{8,12},{9,13},{12,14},{13,15},{14,10},{15,... | collective-permute-start | bytes 688136 | tf_op jit(solution)/shard_map/ppermute | solution.py:248
  39.4 22.1 %collective-permute-start.5 = (bf16[896,128]{1,0:T(8,128)(2,1)S(1)}, bf16[896,128]{1,0:T(8,128)(2,1)S(1)}, u32[]{:S(2)}, u32[]{:S(2)}) collective-permute-start(bf16[896,128]{1,0:T(8,128)(2,1)S(1)} %collective-permute-done.4.refs_4_), channel_id=1, source_target_pairs={{0,2},{1,3},{4,0},{5,1},{8,4},{9,5},{12,8},{13,9},{14,12},{15,13},... | collective-permute-start | bytes 688136 | tf_op jit(solution)/shard_map/ppermute | solution.py:248
  41.4 20.1 %collective-permute-start.7 = (bf16[896,128]{1,0:T(8,128)(2,1)S(1)}, bf16[896,128]{1,0:T(8,128)(2,1)S(1)}, u32[]{:S(2)}, u32[]{:S(2)}) collective-permute-start(bf16[896,128]{1,0:T(8,128)(2,1)S(1)} %collective-permute-done.6.refs_5_), channel_id=1, source_target_pairs={{0,2},{1,3},{4,0},{5,1},{8,4},{9,5},{12,8},{13,9},{14,12},{15,13},... | collective-permute-start | bytes 688136 | tf_op jit(solution)/shard_map/ppermute | solution.py:248
  43.4 2.2 %copy-start = (bf16[128,128,128]{2,1,0:T(8,128)(2,1)S(1)}, bf16[128,128,128]{2,1,0:T(8,128)(2,1)}, u32[]{:S(2)}) copy-start(bf16[128,128,128]{2,1,0:T(8,128)(2,1)} %refs_2_.1) | copy-start | bytes 12582916
  45.5 20.1 %copy-start.1 = (bf16[128,128,128]{2,1,0:T(8,128)(2,1)S(1)}, bf16[128,128,128]{2,1,0:T(8,128)(2,1)}, u32[]{:S(2)}) copy-start(bf16[128,128,128]{2,1,0:T(8,128)(2,1)} %refs_2_.1) | copy-start | bytes 12582916
  61.5 14.7 %collective-permute-start.10 = (bf16[896,128]{1,0:T(8,128)(2,1)S(1)}, bf16[896,128]{1,0:T(8,128)(2,1)S(1)}, u32[]{:S(2)}, u32[]{:S(2)}) collective-permute-start(bf16[896,128]{1,0:T(8,128)(2,1)S(1)} %collective-permute-done.1.refs_0_), channel_id=1, source_target_pairs={{0,4},{1,5},{4,8},{5,9},{8,12},{9,13},{12,14},{13,15},{14,10},{15,... | collective-permute-start | bytes 688136 | tf_op jit(solution)/shard_map/ppermute | solution.py:248
  61.6 16.1 %collective-permute-start.11 = (bf16[896,128]{1,0:T(8,128)(2,1)S(1)}, bf16[896,128]{1,0:T(8,128)(2,1)S(1)}, u32[]{:S(2)}, u32[]{:S(2)}) collective-permute-start(bf16[896,128]{1,0:T(8,128)(2,1)S(1)} %collective-permute-done.3.refs_1_), channel_id=1, source_target_pairs={{0,4},{1,5},{4,8},{5,9},{8,12},{9,13},{12,14},{13,15},{14,10},{15,... | collective-permute-start | bytes 688136 | tf_op jit(solution)/shard_map/ppermute | solution.py:248
  62.5 15.3 %collective-permute-start.12 = (bf16[896,128]{1,0:T(8,128)(2,1)S(1)}, bf16[896,128]{1,0:T(8,128)(2,1)S(1)}, u32[]{:S(2)}, u32[]{:S(2)}) collective-permute-start(bf16[896,128]{1,0:T(8,128)(2,1)S(1)} %collective-permute-done.5.refs_2_), channel_id=1, source_target_pairs={{0,2},{1,3},{4,0},{5,1},{8,4},{9,5},{12,8},{13,9},{14,12},{15,13},... | collective-permute-start | bytes 688136 | tf_op jit(solution)/shard_map/ppermute | solution.py:248
  63.7 14.1 %collective-permute-start.13 = (bf16[896,128]{1,0:T(8,128)(2,1)S(1)}, bf16[896,128]{1,0:T(8,128)(2,1)S(1)}, u32[]{:S(2)}, u32[]{:S(2)}) collective-permute-start(bf16[896,128]{1,0:T(8,128)(2,1)S(1)} %collective-permute-done.7.refs_3_), channel_id=1, source_target_pairs={{0,2},{1,3},{4,0},{5,1},{8,4},{9,5},{12,8},{13,9},{14,12},{15,13},... | collective-permute-start | bytes 688136 | tf_op jit(solution)/shard_map/ppermute | solution.py:248
  65.6 37.6 %collective-permute-start.21 = (f32[1,24,128]{2,1,0:T(8,128)S(1)}, f32[1,24,128]{2,1,0:T(8,128)S(1)}, u32[]{:S(2)}, u32[]{:S(2)}) collective-permute-start(f32[1,24,128]{2,1,0:T(8,128)S(1)} %get-tuple-element.36), channel_id=1, source_target_pairs={{0,4},{1,5},{4,8},{5,9},{8,12},{9,13},{12,14},{13,15},{14,10},{15,... | collective-permute-start | bytes 36872 | tf_op jit(solution)/shard_map/ppermute | solution.py:248
  76.2 29.3 %collective-permute-start.9 = (f32[1,24,128]{2,1,0:T(8,128)S(1)}, f32[1,24,128]{2,1,0:T(8,128)S(1)}, u32[]{:S(2)}, u32[]{:S(2)}) collective-permute-start(f32[1,24,128]{2,1,0:T(8,128)S(1)} %get-tuple-element.37), channel_id=1, source_target_pairs={{0,2},{1,3},{4,0},{5,1},{8,4},{9,5},{12,8},{13,9},{14,12},{15,13},... | collective-permute-start | bytes 36872 | tf_op jit(solution)/shard_map/ppermute | solution.py:248
  77.7 13.7 %collective-permute-start.15 = (bf16[896,128]{1,0:T(8,128)(2,1)S(1)}, bf16[896,128]{1,0:T(8,128)(2,1)S(1)}, u32[]{:S(2)}, u32[]{:S(2)}) collective-permute-start(bf16[896,128]{1,0:T(8,128)(2,1)S(1)} %collective-permute-done.10.refs_0_), channel_id=1, source_target_pairs={{0,4},{1,5},{4,8},{5,9},{8,12},{9,13},{12,14},{13,15},{14,10},{15,... | collective-permute-start | bytes 688136 | tf_op jit(solution)/shard_map/ppermute | solution.py:248
  78.4 16.0 %collective-permute-start.16 = (bf16[896,128]{1,0:T(8,128)(2,1)S(1)}, bf16[896,128]{1,0:T(8,128)(2,1)S(1)}, u32[]{:S(2)}, u32[]{:S(2)}) collective-permute-start(bf16[896,128]{1,0:T(8,128)(2,1)S(1)} %collective-permute-done.13.refs_3_), channel_id=1, source_target_pairs={{0,2},{1,3},{4,0},{5,1},{8,4},{9,5},{12,8},{13,9},{14,12},{15,13},... | collective-permute-start | bytes 688136 | tf_op jit(solution)/shard_map/ppermute | solution.py:248
  79.8 27.2 %collective-permute-start.14 = (f32[1,24,128]{2,1,0:T(8,128)S(1)}, f32[1,24,128]{2,1,0:T(8,128)S(1)}, u32[]{:S(2)}, u32[]{:S(2)}) collective-permute-start(f32[1,24,128]{2,1,0:T(8,128)S(1)} %get-tuple-element.40), channel_id=1, source_target_pairs={{0,6},{1,7},{4,2},{5,3},{8,0},{9,1},{12,4},{13,5},{14,8},{15,9},{1... | collective-permute-start | bytes 36872 | tf_op jit(solution)/shard_map/ppermute | solution.py:248
  91.4 15.6 %collective-permute-start.20 = (f32[1,24,128]{2,1,0:T(8,128)S(1)}, f32[1,24,128]{2,1,0:T(8,128)S(1)}, u32[]{:S(2)}, u32[]{:S(2)}) collective-permute-start(f32[1,24,128]{2,1,0:T(8,128)S(1)} %get-tuple-element.39), channel_id=1, source_target_pairs={{0,8},{1,9},{4,12},{5,13},{8,14},{9,15},{12,10},{13,11},{14,6},{15... | collective-permute-start | bytes 36872 | tf_op jit(solution)/shard_map/ppermute | solution.py:248
  100.8 6.5 %collective-permute-start.18 = (f32[1,24,128]{2,1,0:T(8,128)S(1)}, f32[1,24,128]{2,1,0:T(8,128)S(1)}, u32[]{:S(2)}, u32[]{:S(2)}) collective-permute-start(f32[1,24,128]{2,1,0:T(8,128)S(1)} %score.7), channel_id=1, source_target_pairs={{0,14},{1,15},{4,10},{5,11},{8,6},{9,7},{12,2},{13,3},{14,0},{15,1... | collective-permute-start | bytes 36872 | tf_op jit(solution)/shard_map/ppermute | solution.py:248
  103.2 5.5 %collective-permute-start.17 = (f32[1,24,128]{2,1,0:T(8,128)S(1)}, f32[1,24,128]{2,1,0:T(8,128)S(1)}, u32[]{:S(2)}, u32[]{:S(2)}) collective-permute-start(f32[1,24,128]{2,1,0:T(8,128)S(1)} %get-tuple-element.42), channel_id=1, source_target_pairs={{0,10},{1,11},{4,6},{5,7},{8,2},{9,3},{12,0},{13,1},{14,4},{15,5},... | collective-permute-start | bytes 36872 | tf_op jit(solution)/shard_map/ppermute | solution.py:248
  105.5 5.5 %collective-permute-start.19 = (f32[1,24,128]{2,1,0:T(8,128)S(1)}, f32[1,24,128]{2,1,0:T(8,128)S(1)}, u32[]{:S(2)}, u32[]{:S(2)}) collective-permute-start(f32[1,24,128]{2,1,0:T(8,128)S(1)} %get-tuple-element.41), channel_id=1, source_target_pairs={{0,12},{1,13},{4,14},{5,15},{8,10},{9,11},{12,6},{13,7},{14,2},{15... | collective-permute-start | bytes 36872 | tf_op jit(solution)/shard_map/ppermute | solution.py:248

commit v2 on v1

v2 whole, which is shorter than its diff:
```python
import functools

import jax
import jax.numpy as jnp
from jax import lax
from jax.experimental import pallas as pl
from jax.experimental.pallas import tpu as pltpu
from jax.sharding import PartitionSpec as P

TOPK = 100
CORES = 2
LANES = 128
FACT_ROWS = 16
VMEM_LIMIT = 32 * 1024 * 1024


def ring_order(chips):
    return list(range(0, chips, 2)) + list(range(1, chips, 2))[::-1]


def ring_place(chip, chips):
    return jnp.where(chip % 2 == 0, chip // 2, chips - (chip + 1) // 2)


def split_exact(x):
    high = x.astype(jnp.bfloat16)
    rest = x - high.astype(jnp.float32)
    middle = rest.astype(jnp.bfloat16)
    low = (rest - middle.astype(jnp.float32)).astype(jnp.bfloat16)
    return high, middle, low


def pack_kernel(per_owner, queries, candidates, block):
    query_rows = queries.shape[0]
    for at in range(0, query_rows, LANES):
        block[at : at + LANES, :] = queries[at : at + LANES, :].T
    ids = jnp.broadcast_to(candidates[...], (FACT_ROWS, candidates.shape[1]))
    row = lax.broadcasted_iota(jnp.int32, ids.shape, 0)
    facts = jnp.where(row == 0, ids // per_owner, jnp.where(row == 1, ids % per_owner, 0))
    block[query_rows:, :] = facts.astype(jnp.float32).astype(jnp.bfloat16)


def pack(queries, candidates, per_owner):
    rows, feature = queries.shape
    return pl.pallas_call(
        functools.partial(pack_kernel, per_owner),
        out_shape=jax.ShapeDtypeStruct((rows + FACT_ROWS, feature), queries.dtype),
        in_specs=[pl.BlockSpec(memory_space=pltpu.VMEM)] * 2,
        out_specs=pl.BlockSpec(memory_space=pltpu.VMEM),
        compiler_params=pltpu.CompilerParams(vmem_limit_bytes=VMEM_LIMIT),
        name="pack",
    )(queries, candidates)


def ready_kernel(chips, slots, candidates, passages, slot_of, own, sem):
    load = pltpu.make_async_copy(passages, own, sem)
    load.start()
    number = candidates.shape[1]
    per_owner = passages.shape[0]
    my_place = ring_place(lax.axis_index("corpus") // CORES, chips)
    wide = jnp.broadcast_to(candidates[...], (number, number)) // (CORES * per_owner)
    tall = wide.astype(jnp.float32).T.astype(jnp.int32)
    row = lax.broadcasted_iota(jnp.int32, (number, number), 0)
    lane = lax.broadcasted_iota(jnp.int32, (number, number), 1)
    earlier = jnp.where((wide == tall) & (lane < row), 1.0, 0.0)
    rank = jnp.sum(earlier, axis=1, keepdims=True).astype(jnp.int32)
    ahead = ring_place(tall, chips) - my_place
    ahead = jnp.where(ahead < 0, ahead + chips, ahead)
    slot_of[...] = ahead * slots + rank
    load.wait()


def ready(candidates, passages, chips, slots):
    number = candidates.shape[1]
    return pl.pallas_call(
        functools.partial(ready_kernel, chips, slots),
        out_shape=(
            jax.ShapeDtypeStruct((number, number), jnp.int32),
            jax.ShapeDtypeStruct(passages.shape, passages.dtype),
        ),
        in_specs=[
            pl.BlockSpec(memory_space=pltpu.VMEM), pl.BlockSpec(memory_space=pl.ANY)
        ],
        out_specs=(pl.BlockSpec(memory_space=pltpu.VMEM),) * 2,
        scratch_shapes=[pltpu.SemaphoreType.DMA],
        compiler_params=pltpu.CompilerParams(vmem_limit_bytes=VMEM_LIMIT),
        name="ready",
    )(candidates, passages)


def score_kernel(pieces, slots, query_tok, *refs):
    blocks = len(pieces)
    arrays = sum(pieces)
    own_lens, other_lens, own, other = refs[:4]
    held = refs[4 : 4 + arrays]
    outs = refs[4 + arrays : 4 + arrays + blocks]
    mixed, left, nearest, plan_v, plan, sem = refs[4 + arrays + blocks :]
    per_owner, tile_rows, feature = own.shape
    query_rows = nearest.shape[1]
    me = lax.axis_index("corpus")
    first_owner = me // CORES * CORES

    chunks, facts = [], []
    at = 0
    for count in pieces:
        where = [(ref, r) for ref in held[at : at + count] for r in range(0, ref.shape[0], LANES)]
        facts.append(where[-1])
        chunks.append(where[:-1])
        at += count

    sub = lax.broadcasted_iota(jnp.int32, (8, LANES), 0)
    lane = lax.broadcasted_iota(jnp.int32, (8, LANES), 1)
    owner = jnp.full((8, LANES), -1.0, jnp.float32)
    local_id = jnp.zeros((8, LANES), jnp.float32)
    for b, (ref, r) in enumerate(facts):
        fact = ref[r : r + FACT_ROWS, :].astype(jnp.float32)
        owner = jnp.where(sub == b, fact[0:1, :], owner)
        local_id = jnp.where(sub == b, fact[1:2, :], local_id)
    owner = owner.astype(jnp.int32)
    mine = (owner >= first_owner) & (owner < first_owner + CORES)
    ones = jnp.where(mine, 1.0, 0.0)
    rank = ones
    shift = 1
    while shift < LANES:
        rank = rank + jnp.where(lane >= shift, pltpu.roll(rank, shift, 1), 0.0)
        shift *= 2
    rank = jnp.where(mine, rank - 1.0, -1.0)
    tile = local_id + jnp.where(owner == me, 0.0, float(per_owner))
    wanted = jnp.where(lane == slots, jnp.sum(ones, axis=1, keepdims=True), 0.0)
    for s in range(slots):
        found = jnp.sum(jnp.where(rank == float(s), tile, 0.0), axis=1, keepdims=True)
        wanted = jnp.where(lane == s, found, wanted)
    plan_v[...] = wanted.astype(jnp.int32)
    to_scalar = pltpu.make_async_copy(plan_v, plan, sem)
    to_scalar.start()
    to_scalar.wait()

    tile_row = lax.broadcasted_iota(jnp.int32, (tile_rows, feature), 0)
    slot_row = lax.broadcasted_iota(jnp.int32, (slots, LANES), 0)
    slot_lane = lax.broadcasted_iota(jnp.int32, (slots, LANES), 1)
    for b in range(blocks):
        count = plan[b, slots]

        def score_group(g, carry, b=b):
            start = pl.multiple_of(g * 8, 8)
            for t in range(8):
                at = plan[b, start + t]
                here = at < per_owner
                at_own = jnp.minimum(at, per_owner - 1)
                at_other = jnp.maximum(at - per_owner, 0)
                length = jnp.where(here, own_lens[at_own], other_lens[at_other])
                tile = jnp.where(
                    here, own[at_own].astype(jnp.float32), other[at_other].astype(jnp.float32)
                )
                tile = jnp.where(tile_row < length, tile, tile[0:1, :])
                mixed[pl.ds(t, tile_rows, stride=8), :] = tile
            left[...] = mixed[...].astype(jnp.bfloat16)
            for c in range(0, len(chunks[b]), 2):
                pair = [ref[r : r + LANES, :] for ref, r in chunks[b][c : c + 2]]
                similar = jnp.dot(
                    left[...], jnp.concatenate(pair, axis=1), preferred_element_type=jnp.float32
                )
                width = similar.shape[1]
                nearest[pl.ds(start, 8), c * LANES : c * LANES + width] = jnp.max(
                    similar.reshape(tile_rows, 8, width), axis=0
                )
            return carry

        lax.fori_loop(0, pl.cdiv(count, 8), score_group, 0)
        total = jnp.zeros((slots, LANES), jnp.float32)
        for k in range(query_rows // LANES):
            x = nearest[:, k * LANES : (k + 1) * LANES]
            shift = query_tok // 2
            while shift >= 1:
                x = x + pltpu.roll(x, LANES - shift, 1)
                shift //= 2
            if k:
                x = pltpu.roll(x, k, 1)
            total = jnp.where(slot_lane % query_tok == k, x, total)
        outs[b][...] = jnp.where(slot_row < count, total / float(query_tok), 0.0)


def score(held, slots, query_tok, own_lens, other_lens, own, other):
    pieces = tuple(len(arrays) for arrays in held)
    flat = [x for arrays in held for x in arrays]
    blocks = len(pieces)
    _, tile_rows, feature = own.shape
    query_rows = sum(x.shape[0] for x in held[0]) - FACT_ROWS
    flops = 2 * blocks * slots * tile_rows * feature * query_rows
    return pl.pallas_call(
        functools.partial(score_kernel, pieces, slots, query_tok),
        out_shape=(jax.ShapeDtypeStruct((slots, LANES), jnp.float32),) * blocks,
        in_specs=[pl.BlockSpec(memory_space=pltpu.SMEM)] * 2
        + [pl.BlockSpec(memory_space=pltpu.VMEM)] * (2 + len(flat)),
        out_specs=(pl.BlockSpec(memory_space=pltpu.VMEM),) * blocks,
        scratch_shapes=[
            pltpu.VMEM((8 * tile_rows, feature), jnp.float32),
            pltpu.VMEM((8 * tile_rows, feature), jnp.bfloat16),
            pltpu.VMEM((slots, query_rows), jnp.float32),
            pltpu.VMEM((8, LANES), jnp.int32),
            pltpu.SMEM((8, LANES), jnp.int32),
            pltpu.SemaphoreType.DMA,
        ],
        compiler_params=pltpu.CompilerParams(vmem_limit_bytes=VMEM_LIMIT),
        cost_estimate=pl.CostEstimate(
            flops=3 * flops,
            bytes_accessed=blocks * (slots * tile_rows + query_rows) * feature * 2,
            transcendentals=0,
        ),
        name="score",
    )(own_lens, other_lens, own, other, *flat)


def sort_descending(parts, lanes):
    parts = list(parts)
    many = len(parts)
    number = many * 8
    sub = lax.broadcasted_iota(jnp.int32, (8, lanes), 0)
    size = 2
    while size <= number:
        reach = size // 2
        while reach >= 1:
            if reach < many:
                for v in range(many):
                    if v & reach:
                        continue
                    a, b = parts[v], parts[v | reach]
                    high, low = jnp.maximum(a, b), jnp.minimum(a, b)
                    if size >= number:
                        parts[v], parts[v | reach] = high, low
                    elif size < many:
                        down = (v & size) == 0
                        parts[v], parts[v | reach] = (high, low) if down else (low, high)
                    else:
                        down = (sub & (size // many)) == 0
                        parts[v] = jnp.where(down, high, low)
                        parts[v | reach] = jnp.where(down, low, high)
            else:
                step = reach // many
                is_first = (sub & step) == 0
                if size >= number:
                    keep_high = is_first
                else:
                    keep_high = is_first == ((sub & (size // many)) == 0)
                for v in range(many):
                    x = parts[v]
                    partner = jnp.where(is_first, pltpu.roll(x, 8 - step, 0), pltpu.roll(x, step, 0))
                    parts[v] = jnp.where(keep_high, jnp.maximum(x, partner), jnp.minimum(x, partner))
            reach //= 2
        size *= 2
    return parts


def finish_kernel(arrays, per_device, query_tok, topk, slot_of, *refs):
    returned = refs[:arrays]
    scores, best_scores, spread, ranked, rows = refs[arrays:]
    number = slot_of.shape[0]
    step = returned[0].shape[0]
    for at, ref in enumerate(returned):
        spread[at * step : (at + 1) * step, :] = ref[...]
    total = spread.shape[0]
    lane = lax.broadcasted_iota(jnp.int32, (number, total), 1)
    choose = (slot_of[:, 0:1] == lane).astype(jnp.float32).astype(jnp.bfloat16)
    by_candidate = jnp.zeros((number, LANES), jnp.float32)
    for part in split_exact(spread[...]):
        by_candidate += jnp.dot(choose, part, preferred_element_type=jnp.float32)

    def in_order(x):
        x = x.T
        each = LANES // query_tok
        for m in range(each):
            rows[pl.ds(m, query_tok, stride=each), :] = x[m * query_tok : (m + 1) * query_tok, :]
        return rows[...]

    scores[...] = in_order(by_candidate)[:per_device, :]
    many = number // 8
    parts = sort_descending([by_candidate[8 * v : 8 * v + 8, :] for v in range(many)], LANES)
    for v in range(many):
        ranked[pl.ds(v, 8, stride=many), :] = parts[v]
    best_scores[...] = in_order(ranked[...])[:per_device, :topk]


def finish(per_device, query_tok, slot_of, returned):
    number = slot_of.shape[0]
    total = sum(r.shape[0] for r in returned)
    return pl.pallas_call(
        functools.partial(finish_kernel, len(returned), per_device, query_tok, TOPK),
        out_shape=(
            jax.ShapeDtypeStruct((per_device, number), jnp.float32),
            jax.ShapeDtypeStruct((per_device, TOPK), jnp.float32),
        ),
        in_specs=[pl.BlockSpec(memory_space=pltpu.VMEM)] * (1 + len(returned)),
        out_specs=(pl.BlockSpec(memory_space=pltpu.VMEM),) * 2,
        scratch_shapes=[
            pltpu.VMEM((total, LANES), jnp.float32),
            pltpu.VMEM((number, LANES), jnp.float32),
            pltpu.VMEM((LANES, number), jnp.float32),
        ],
        compiler_params=pltpu.CompilerParams(vmem_limit_bytes=VMEM_LIMIT),
        name="finish",
    )(slot_of, *returned)


def local(queries, passages, lengths, candidates):
    peers = lax.axis_size("corpus")
    chips = peers // CORES
    per_owner, tile_rows, feature = passages.shape
    per_device, query_tok = queries.shape[0], queries.shape[1]
    number = candidates.shape[1]
    capacity = max(2, 3 * number // (2 * peers))
    slots = -(-CORES * capacity // 8) * 8
    order = ring_order(chips)

    def moved(x, distance):
        pairs = [
            (order[i] * CORES + core, order[(i + distance) % chips] * CORES + core)
            for i in range(chips)
            for core in range(CORES)
        ]
        return lax.ppermute(x, "corpus", pairs)

    swap = [(i, i ^ 1) for i in range(peers)]
    other = lax.ppermute(passages, "corpus", swap)
    other_lengths = lax.ppermute(lengths, "corpus", swap)
    slot_of, own = ready(candidates, passages, chips, slots)

    block = pack(queries.reshape(per_device * query_tok, feature), candidates, per_owner)
    half = per_device * query_tok // LANES // 2 * LANES
    middle = chips // 2
    arrived = {0: [block]}

    def send_on(step):
        if step < middle:
            arrived[step] = [moved(x, 1) for x in arrived[step - 1]]
            arrived[-step] = [moved(x, -1) for x in arrived[1 - step]]
        else:
            arrived[step] = [
                moved(arrived[step - 1][0][:half], 1), moved(arrived[1 - step][0][half:], -1)
            ]

    send_on(1)
    back = {}
    for step in range(1, middle + 1):
        if step < middle:
            send_on(step + 1)
        offsets = (0, 1, -1) if step == 1 else (middle,) if step == middle else (step, -step)
        fresh = score(
            [arrived[offset] for offset in offsets], slots, query_tok,
            lengths, other_lengths, own, other,
        )
        if step < middle:
            names = [step + 1, -step - 1] if step + 1 < middle else [middle]
            held, fresh = lax.optimization_barrier(([arrived[name] for name in names], fresh))
            arrived.update(zip(names, held))
        for offset, result in zip(offsets, fresh):
            back[offset % chips] = moved(result, -offset) if offset else result
    return finish(per_device, query_tok, slot_of, [back[j] for j in range(chips)])


def solution(mesh):
    return jax.shard_map(
        local,
        mesh=mesh,
        in_specs=(
            P(("groups", "corpus"), None, None),
            P(("groups", "corpus"), None, None),
            P(("groups", "corpus")),
            P(("groups", "corpus"), None),
        ),
        out_specs=(P(("groups", "corpus"), None), P(("groups", "corpus"), None)),
        check_vma=False,
    )
```

time: 112 us -> 78.2 us (0.70)
  blocking collectives: 23.4 us -> 0 us
  waiting for transfers between devices: 3.96 us -> 12.2 us
  Pallas kernels: 45.5 us -> 39.5 us
  other arithmetic: 5.16 us -> 0 us
  starting transfers between devices: 26.1 us -> 22.8 us
  local copies, waits for them, and re-layouts: 6.92 us -> 3.9 us
    all_gather x1 -> x0, blocking collectives: 23.4 us -> none  [local(): lax.all_gather(jnp.concatenate([candidates[0], lengths])[None, :], 'corpu...]
    ppermute x21 -> x15, waiting for transfers between devices: 3.95 us -> 12.2 us  [moved(): return lax.ppermute(x, 'corpus', pairs)]
    pallas_call x4 -> x6, Pallas kernels: 44.4 us -> 38.4 us  [the longest x4 37.7 us: score(): pl.pallas_call(functools.partial(score_kernel, pieces, slots, query_tok),...]
    ppermute x21 -> x15, starting transfers between devices: 25.6 us -> 22 us  [moved(): return lax.ppermute(x, 'corpus', pairs)]
    unnamed x5 -> x8, local copies, waits for them, and re-layouts: 2.19 us -> 3.87 us
    concatenate x3 -> x0, other arithmetic: 1.42 us -> none  [the longest x1 0.68 us: local(): jnp.concatenate([candidates[0], lengths])[None, :]]
    select_n x3 -> x0, other arithmetic: 1.34 us -> none  [the longest x1 0.67 us: local(): chip_of = ids // per_chip]
    gather x1 -> x0, local copies, waits for them, and re-layouts: 1.29 us -> none  [local(): jnp.asarray(order, jnp.int32)]
  transfers between devices with their start and end apart: 22 -> 17, of which waited for: 3 -> 3; matrix products, arithmetic and copies ran while one was open for 9% -> 0% of each run, Pallas kernels for 40% -> 48%
where the time goes in v2:
time: 78.2 us; the launch traced here: 79.1 us
  Pallas kernels  39.5 us (51%)
  starting transfers between devices  22.8 us (29%)
  waiting for transfers between devices  12.2 us (16%)
  local copies, waits for them, and re-layouts  3.9 us (5%)
    pallas_call x4, Pallas kernels, score(): pl.pallas_call(functools.partial(score_kernel, pieces, slots, query_tok),...  37.7 us
    ppermute x15, starting transfers between devices, moved(): return lax.ppermute(x, 'corpus', pairs)  22 us
    ppermute x15, waiting for transfers between devices, moved(): return lax.ppermute(x, 'corpus', pairs)  12.2 us
    unnamed x8, local copies, waits for them, and re-layouts  3.87 us
  transfers between devices with their start and end apart: 17, of which 3 were waited for; matrix products, arithmetic and copies ran while one was open for 0% of the time, Pallas kernels for 48%

profile of v2, /device:TPU:0, one launch (start us, length us, event | category | flops | bytes accessed | tf_op | source)
XLA Modules:
  0.0 79.1 jit_solution(17055800334453354516)
XLA Ops:
  0.6 0.0 copy-start.3
  0.6 0.5 collective-permute-start.5
  1.2 0.0 copy-start.1
  1.2 1.0 %copy-done.1 = bf16[56,32,128]{2,1,0:T(8,128)(2,1)S(1)} copy-done((bf16[56,32,128]{2,1,0:T(8,128)(2,1)S(1)}, bf16[56,32,128]{2,1,0:T(8,128)(2,1)}, u32[]{:S(2)}) %copy-start.1) | copy-done | bytes 458776
  2.2 0.0 copy-start.2
  2.2 0.7 copy-done.2
  2.8 0.2 pack.1.refs_4_
  3.0 2.6 %collective-permute-start = (bf16[1808,128]{1,0:T(8,128)(2,1)S(1)}, bf16[1808,128]{1,0:T(8,128)(2,1)S(1)}, u32[]{:S(2)}, u32[]{:S(2)}) collective-permute-start(bf16[1808,128]{1,0:T(8,128)(2,1)S(1)} %pack.1.refs_4_), channel_id=1, source_target_pairs={{0,4},{1,5},{4,8},{5,9},{8,12},{9,13},{12,14},{13,15},{14,10},{15,... | collective-permute-start | bytes 1388552 | tf_op jit(solution)/shard_map/ppermute | solution.py:320
  5.7 0.0 collective-permute-start.2
  5.7 0.2 collective-permute-start.4
  5.9 0.0 copy-start
  5.9 2.2 %copy-done = bf16[128,128,128]{2,1,0:T(8,128)(2,1)S(1)} copy-done((bf16[128,128,128]{2,1,0:T(8,128)(2,1)S(1)}, bf16[128,128,128]{2,1,0:T(8,128)(2,1)}, u32[]{:S(2)}) %copy-start) | copy-done | bytes 4194328
  8.1 0.5 ready.1
  8.6 8.3 %collective-permute-done.refs_5_ = bf16[1808,128]{1,0:T(8,128)(2,1)S(1)} collective-permute-done((bf16[1808,128]{1,0:T(8,128)(2,1)S(1)}, bf16[1808,128]{1,0:T(8,128)(2,1)S(1)}, u32[]{:S(2)}, u32[]{:S(2)}) %collective-permute-start) | collective-permute-done | bytes 462880 | tf_op jit(solution)/shard_map/ppermute | solution.py:320
  16.9 1.8 %collective-permute-start.1 = (bf16[1808,128]{1,0:T(8,128)(2,1)S(1)}, bf16[1808,128]{1,0:T(8,128)(2,1)S(1)}, u32[]{:S(2)}, u32[]{:S(2)}) collective-permute-start(bf16[1808,128]{1,0:T(8,128)(2,1)S(1)} %collective-permute-done.refs_5_), channel_id=1, source_target_pairs={{0,4},{1,5},{4,8},{5,9},{8,12},{9,13},{12,14},{13,15},{14,10},{15,... | collective-permute-start | bytes 1388552 | tf_op jit(solution)/shard_map/ppermute | solution.py:320
  18.7 0.0 collective-permute-done.2.refs_6_
  18.7 0.2 collective-permute-start.3
  18.9 0.0 collective-permute-done.4.refs_1_
  18.9 0.0 collective-permute-done.5.refs_3_
  18.9 0.0 copy-done.3
  18.9 14.2 %score.4 = (f32[24,128]{1,0:T(8,128)S(1)}, f32[24,128]{1,0:T(8,128)S(1)}, f32[24,128]{1,0:T(8,128)S(1)}) custom-call(s32[128]{0:T(128)S(1)} %copy-done.3, s32[128]{0:T(128)S(1)} %collective-permute-done.4.refs_1_, bf16[128,128,128]{2,1,0:T(8,128)(2,1)S(1)} %get-tuple-element.25.refs_2_, bf16[128,128,128]{2,1,0:T(8,128)(2,1)S(1)} %collective-permute-done.5.refs_3_, ...), custom_call_target="tpu_custom_call" | custom-call | flops 12683575296 | bytes 3735552 | tf_op jit(solution)/shard_map/score/pallas_call | solution.py:190
  33.1 0.0 collective-permute-done.1.refs_4_
  33.1 0.0 collective-permute-done.3.refs_5_
  33.1 1.8 %collective-permute-start.7 = (bf16[1808,128]{1,0:T(8,128)(2,1)S(1)}, bf16[1808,128]{1,0:T(8,128)(2,1)S(1)}, u32[]{:S(2)}, u32[]{:S(2)}) collective-permute-start(bf16[1808,128]{1,0:T(8,128)(2,1)S(1)} %collective-permute-done.1.refs_4_), channel_id=1, source_target_pairs={{0,4},{1,5},{4,8},{5,9},{8,12},{9,13},{12,14},{13,15},{14,10},{15,... | collective-permute-start | bytes 1388552 | tf_op jit(solution)/shard_map/ppermute | solution.py:320
  34.9 0.2 collective-permute-start.8
  35.2 1.8 %collective-permute-start.16 = (f32[24,128]{1,0:T(8,128)S(1)}, f32[24,128]{1,0:T(8,128)S(1)}, u32[]{:S(2)}, u32[]{:S(2)}) collective-permute-start(f32[24,128]{1,0:T(8,128)S(1)} %get-tuple-element.45), channel_id=1, source_target_pairs={{0,4},{1,5},{4,8},{5,9},{8,12},{9,13},{12,14},{13,15},{14,10},{15,... | collective-permute-start | bytes 36872 | tf_op jit(solution)/shard_map/ppermute | solution.py:320
  37.0 0.2 collective-permute-start.6
  37.2 10.0 %score.5 = (f32[24,128]{1,0:T(8,128)S(1)}, f32[24,128]{1,0:T(8,128)S(1)}) custom-call(s32[128]{0:T(128)S(1)} %copy-done.3, s32[128]{0:T(128)S(1)} %collective-permute-done.4.refs_1_, bf16[128,128,128]{2,1,0:T(8,128)(2,1)S(1)} %get-tuple-element.25.refs_2_, bf16[128,128,128]{2,1,0:T(8,128)(2,1)S(1)} %collective-permute-done.5.refs_3_, ...), custom_call_target="tpu_custom_call" | custom-call | flops 8455716864 | bytes 2490368 | tf_op jit(solution)/shard_map/score/pallas_call | solution.py:190
  47.2 0.0 collective-permute-done.7.refs_4_
  47.2 0.0 collective-permute-done.8.refs_5_
  47.2 0.1 collective-permute-start.11
  47.3 2.1 %collective-permute-start.10 = (bf16[896,128]{1,0:T(8,128)(2,1)S(1)}, bf16[896,128]{1,0:T(8,128)(2,1)S(1)}, u32[]{:S(2)}, u32[]{:S(2)}) collective-permute-start(bf16[896,128]{1,0:T(8,128)(2,1)S(1)} %slice.6), channel_id=1, source_target_pairs={{0,4},{1,5},{4,8},{5,9},{8,12},{9,13},{12,14},{13,15},{14,10},{15,... | collective-permute-start | bytes 688136 | tf_op jit(solution)/shard_map/ppermute | solution.py:320
  49.4 1.6 %collective-permute-start.15 = (f32[24,128]{1,0:T(8,128)S(1)}, f32[24,128]{1,0:T(8,128)S(1)}, u32[]{:S(2)}, u32[]{:S(2)}) collective-permute-start(f32[24,128]{1,0:T(8,128)S(1)} %get-tuple-element.44), channel_id=1, source_target_pairs={{0,8},{1,9},{4,12},{5,13},{8,14},{9,15},{12,10},{13,11},{14,6},{15... | collective-permute-start | bytes 36872 | tf_op jit(solution)/shard_map/ppermute | solution.py:320
  51.0 7.7 %score.6 = (f32[24,128]{1,0:T(8,128)S(1)}, f32[24,128]{1,0:T(8,128)S(1)}) custom-call(s32[128]{0:T(128)S(1)} %copy-done.3, s32[128]{0:T(128)S(1)} %collective-permute-done.4.refs_1_, bf16[128,128,128]{2,1,0:T(8,128)(2,1)S(1)} %get-tuple-element.25.refs_2_, bf16[128,128,128]{2,1,0:T(8,128)(2,1)S(1)} %collective-permute-done.5.refs_3_, ...), custom_call_target="tpu_custom_call" | custom-call | flops 8455716864 | bytes 2490368 | tf_op jit(solution)/shard_map/score/pallas_call | solution.py:190
  58.7 0.0 collective-permute-done.10.refs_4_
  58.7 1.4 %collective-permute-start.9 = (f32[24,128]{1,0:T(8,128)S(1)}, f32[24,128]{1,0:T(8,128)S(1)}, u32[]{:S(2)}, u32[]{:S(2)}) collective-permute-start(f32[24,128]{1,0:T(8,128)S(1)} %get-tuple-element.35), channel_id=1, source_target_pairs={{0,6},{1,7},{4,2},{5,3},{8,0},{9,1},{12,4},{13,5},{14,8},{15,9},{1... | collective-permute-start | bytes 36872 | tf_op jit(solution)/shard_map/ppermute | solution.py:320
  60.1 0.0 collective-permute-done.11.refs_5_
  60.1 5.8 %score.7 = f32[24,128]{1,0:T(8,128)S(1)} custom-call(s32[128]{0:T(128)S(1)} %copy-done.3, s32[128]{0:T(128)S(1)} %collective-permute-done.4.refs_1_, bf16[128,128,128]{2,1,0:T(8,128)(2,1)S(1)} %get-tuple-element.25.refs_2_, bf16[128,128,128]{2,1,0:T(8,128)(2,1)S(1)} %collective-permute-done.5.refs_3_, bf16[896,128]{1,0:T(8,128)(2,1)S(1)} %collective-permute-done.10.refs_4_, ...), custom_call_target="tpu_custom_call" | custom-call | flops 4227858432 | bytes 1245184 | tf_op jit(solution)/shard_map/score/pallas_call | solution.py:190
  65.9 4.3 %collective-permute-start.13 = (f32[24,128]{1,0:T(8,128)S(1)}, f32[24,128]{1,0:T(8,128)S(1)}, u32[]{:S(2)}, u32[]{:S(2)}) collective-permute-start(f32[24,128]{1,0:T(8,128)S(1)} %score.7), channel_id=1, source_target_pairs={{0,14},{1,15},{4,10},{5,11},{8,6},{9,7},{12,2},{13,3},{14,0},{15,1... | collective-permute-start | bytes 36872 | tf_op jit(solution)/shard_map/ppermute | solution.py:320
  70.3 0.0 collective-permute-done.16.refs_7_
  70.3 2.0 %collective-permute-start.12 = (f32[24,128]{1,0:T(8,128)S(1)}, f32[24,128]{1,0:T(8,128)S(1)}, u32[]{:S(2)}, u32[]{:S(2)}) collective-permute-start(f32[24,128]{1,0:T(8,128)S(1)} %get-tuple-element.40), channel_id=1, source_target_pairs={{0,10},{1,11},{4,6},{5,7},{8,2},{9,3},{12,0},{13,1},{14,4},{15,5},... | collective-permute-start | bytes 36872 | tf_op jit(solution)/shard_map/ppermute | solution.py:320
  72.3 0.0 collective-permute-done.6.refs_1_
  72.3 1.8 %collective-permute-start.14 = (f32[24,128]{1,0:T(8,128)S(1)}, f32[24,128]{1,0:T(8,128)S(1)}, u32[]{:S(2)}, u32[]{:S(2)}) collective-permute-start(f32[24,128]{1,0:T(8,128)S(1)} %get-tuple-element.43), channel_id=1, source_target_pairs={{0,12},{1,13},{4,14},{5,15},{8,10},{9,11},{12,6},{13,7},{14,2},{15... | collective-permute-start | bytes 36872 | tf_op jit(solution)/shard_map/ppermute | solution.py:320
  74.1 0.0 collective-permute-done.15.refs_6_
  74.1 0.0 collective-permute-done.9.refs_2_
  74.1 0.0 collective-permute-done.13.refs_4_
  74.1 1.7 %collective-permute-done.12.refs_3_ = f32[24,128]{1,0:T(8,128)S(1)} collective-permute-done((f32[24,128]{1,0:T(8,128)S(1)}, f32[24,128]{1,0:T(8,128)S(1)}, u32[]{:S(2)}, u32[]{:S(2)}) %collective-permute-start.12) | collective-permute-done | bytes 12320 | tf_op jit(solution)/shard_map/ppermute | solution.py:320
  75.8 2.2 %collective-permute-done.14.refs_5_ = f32[24,128]{1,0:T(8,128)S(1)} collective-permute-done((f32[24,128]{1,0:T(8,128)S(1)}, f32[24,128]{1,0:T(8,128)S(1)}, u32[]{:S(2)}, u32[]{:S(2)}) %collective-permute-start.14) | collective-permute-done | bytes 12320 | tf_op jit(solution)/shard_map/ppermute | solution.py:320
  78.0 1.1 %finish.1 = (f32[56,128]{1,0:T(8,128)}, f32[56,100]{1,0:T(8,128)}) custom-call(s32[128,128]{1,0:T(8,128)S(1)} %get-tuple-element.24.slot_of, f32[24,128]{1,0:T(8,128)S(1)} %get-tuple-element.29.refs_0_, f32[24,128]{1,0:T(8,128)S(1)} %collective-permute-done.6.refs_1_, f32[24,128]{1,0:T(8,128)S(1)} %collective-permute-done.9.refs_2_, ...), custom_call_target="tpu_custom_call" | custom-call | tf_op jit(solution)/shard_map/finish/pallas_call | solution.py:286
  (2 shorter events, 0.0 us)
Async XLA Ops:
  0.6 18.3 %copy-start.3 = (s32[128]{0:T(128)S(1)}, s32[128]{0:T(128)}, u32[]{:S(2)}) copy-start(s32[128]{0:T(128)} %refs_0_.7) | copy-start | bytes 1540
  0.6 18.3 %collective-permute-start.5 = (bf16[128,128,128]{2,1,0:T(8,128)(2,1)}, bf16[128,128,128]{2,1,0:T(8,128)(2,1)S(1)}, u32[]{:S(2)}, u32[]{:S(2)}) collective-permute-start(bf16[128,128,128]{2,1,0:T(8,128)(2,1)} %passages.1), channel_id=1, source_target_pairs={{0,1},{1,0},{2,3},{3,2},{4,5},{5,4},{6,7},{7,6},{8,9},{9,8},{10,11... | collective-permute-start | bytes 12582920 | tf_op jit(solution)/shard_map/ppermute | solution.py:323
  1.2 1.0 %copy-start.1 = (bf16[56,32,128]{2,1,0:T(8,128)(2,1)S(1)}, bf16[56,32,128]{2,1,0:T(8,128)(2,1)}, u32[]{:S(2)}) copy-start(bf16[56,32,128]{2,1,0:T(8,128)(2,1)} %param.4) | copy-start | bytes 1376260
  2.2 0.7 copy-start.2
  3.0 13.8 %collective-permute-start = (bf16[1808,128]{1,0:T(8,128)(2,1)S(1)}, bf16[1808,128]{1,0:T(8,128)(2,1)S(1)}, u32[]{:S(2)}, u32[]{:S(2)}) collective-permute-start(bf16[1808,128]{1,0:T(8,128)(2,1)S(1)} %pack.1.refs_4_), channel_id=1, source_target_pairs={{0,4},{1,5},{4,8},{5,9},{8,12},{9,13},{12,14},{13,15},{14,10},{15,... | collective-permute-start | bytes 1388552 | tf_op jit(solution)/shard_map/ppermute | solution.py:320
  5.7 13.0 %collective-permute-start.2 = (bf16[1808,128]{1,0:T(8,128)(2,1)S(1)}, bf16[1808,128]{1,0:T(8,128)(2,1)S(1)}, u32[]{:S(2)}, u32[]{:S(2)}) collective-permute-start(bf16[1808,128]{1,0:T(8,128)(2,1)S(1)} %pack.1.refs_4_), channel_id=1, source_target_pairs={{0,2},{1,3},{4,0},{5,1},{8,4},{9,5},{12,8},{13,9},{14,12},{15,13},... | collective-permute-start | bytes 1388552 | tf_op jit(solution)/shard_map/ppermute | solution.py:320
  5.7 13.2 %collective-permute-start.4 = (s32[128]{0:T(128)}, s32[128]{0:T(128)S(1)}, u32[]{:S(2)}, u32[]{:S(2)}) collective-permute-start(s32[128]{0:T(128)} %refs_0_.7), channel_id=1, source_target_pairs={{0,1},{1,0},{2,3},{3,2},{4,5},{5,4},{6,7},{7,6},{8,9},{9,8},{10,11... | collective-permute-start | bytes 1544 | tf_op jit(solution)/shard_map/ppermute | solution.py:324
  5.9 2.2 %copy-start = (bf16[128,128,128]{2,1,0:T(8,128)(2,1)S(1)}, bf16[128,128,128]{2,1,0:T(8,128)(2,1)}, u32[]{:S(2)}) copy-start(bf16[128,128,128]{2,1,0:T(8,128)(2,1)} %passages.1) | copy-start | bytes 12582916
  16.9 16.2 %collective-permute-start.1 = (bf16[1808,128]{1,0:T(8,128)(2,1)S(1)}, bf16[1808,128]{1,0:T(8,128)(2,1)S(1)}, u32[]{:S(2)}, u32[]{:S(2)}) collective-permute-start(bf16[1808,128]{1,0:T(8,128)(2,1)S(1)} %collective-permute-done.refs_5_), channel_id=1, source_target_pairs={{0,4},{1,5},{4,8},{5,9},{8,12},{9,13},{12,14},{13,15},{14,10},{15,... | collective-permute-start | bytes 1388552 | tf_op jit(solution)/shard_map/ppermute | solution.py:320
  18.7 14.4 %collective-permute-start.3 = (bf16[1808,128]{1,0:T(8,128)(2,1)S(1)}, bf16[1808,128]{1,0:T(8,128)(2,1)S(1)}, u32[]{:S(2)}, u32[]{:S(2)}) collective-permute-start(bf16[1808,128]{1,0:T(8,128)(2,1)S(1)} %collective-permute-done.2.refs_6_), channel_id=1, source_target_pairs={{0,2},{1,3},{4,0},{5,1},{8,4},{9,5},{12,8},{13,9},{14,12},{15,13},... | collective-permute-start | bytes 1388552 | tf_op jit(solution)/shard_map/ppermute | solution.py:320
  33.1 14.1 %collective-permute-start.7 = (bf16[1808,128]{1,0:T(8,128)(2,1)S(1)}, bf16[1808,128]{1,0:T(8,128)(2,1)S(1)}, u32[]{:S(2)}, u32[]{:S(2)}) collective-permute-start(bf16[1808,128]{1,0:T(8,128)(2,1)S(1)} %collective-permute-done.1.refs_4_), channel_id=1, source_target_pairs={{0,4},{1,5},{4,8},{5,9},{8,12},{9,13},{12,14},{13,15},{14,10},{15,... | collective-permute-start | bytes 1388552 | tf_op jit(solution)/shard_map/ppermute | solution.py:320
  34.9 12.3 %collective-permute-start.8 = (bf16[1808,128]{1,0:T(8,128)(2,1)S(1)}, bf16[1808,128]{1,0:T(8,128)(2,1)S(1)}, u32[]{:S(2)}, u32[]{:S(2)}) collective-permute-start(bf16[1808,128]{1,0:T(8,128)(2,1)S(1)} %collective-permute-done.3.refs_5_), channel_id=1, source_target_pairs={{0,2},{1,3},{4,0},{5,1},{8,4},{9,5},{12,8},{13,9},{14,12},{15,13},... | collective-permute-start | bytes 1388552 | tf_op jit(solution)/shard_map/ppermute | solution.py:320
  35.2 35.1 %collective-permute-start.16 = (f32[24,128]{1,0:T(8,128)S(1)}, f32[24,128]{1,0:T(8,128)S(1)}, u32[]{:S(2)}, u32[]{:S(2)}) collective-permute-start(f32[24,128]{1,0:T(8,128)S(1)} %get-tuple-element.45), channel_id=1, source_target_pairs={{0,4},{1,5},{4,8},{5,9},{8,12},{9,13},{12,14},{13,15},{14,10},{15,... | collective-permute-start | bytes 36872 | tf_op jit(solution)/shard_map/ppermute | solution.py:320
  37.0 35.3 %collective-permute-start.6 = (f32[24,128]{1,0:T(8,128)S(1)}, f32[24,128]{1,0:T(8,128)S(1)}, u32[]{:S(2)}, u32[]{:S(2)}) collective-permute-start(f32[24,128]{1,0:T(8,128)S(1)} %get-tuple-element.30), channel_id=1, source_target_pairs={{0,2},{1,3},{4,0},{5,1},{8,4},{9,5},{12,8},{13,9},{14,12},{15,13},... | collective-permute-start | bytes 36872 | tf_op jit(solution)/shard_map/ppermute | solution.py:320
  47.2 12.9 %collective-permute-start.11 = (bf16[912,128]{1,0:T(8,128)(2,1)S(1)}, bf16[912,128]{1,0:T(8,128)(2,1)S(1)}, u32[]{:S(2)}, u32[]{:S(2)}) collective-permute-start(bf16[912,128]{1,0:T(8,128)(2,1)S(1)} %slice.7), channel_id=1, source_target_pairs={{0,2},{1,3},{4,0},{5,1},{8,4},{9,5},{12,8},{13,9},{14,12},{15,13},... | collective-permute-start | bytes 700424 | tf_op jit(solution)/shard_map/ppermute | solution.py:320
  47.3 11.4 %collective-permute-start.10 = (bf16[896,128]{1,0:T(8,128)(2,1)S(1)}, bf16[896,128]{1,0:T(8,128)(2,1)S(1)}, u32[]{:S(2)}, u32[]{:S(2)}) collective-permute-start(bf16[896,128]{1,0:T(8,128)(2,1)S(1)} %slice.6), channel_id=1, source_target_pairs={{0,4},{1,5},{4,8},{5,9},{8,12},{9,13},{12,14},{13,15},{14,10},{15,... | collective-permute-start | bytes 688136 | tf_op jit(solution)/shard_map/ppermute | solution.py:320
  49.4 24.8 %collective-permute-start.15 = (f32[24,128]{1,0:T(8,128)S(1)}, f32[24,128]{1,0:T(8,128)S(1)}, u32[]{:S(2)}, u32[]{:S(2)}) collective-permute-start(f32[24,128]{1,0:T(8,128)S(1)} %get-tuple-element.44), channel_id=1, source_target_pairs={{0,8},{1,9},{4,12},{5,13},{8,14},{9,15},{12,10},{13,11},{14,6},{15... | collective-permute-start | bytes 36872 | tf_op jit(solution)/shard_map/ppermute | solution.py:320
  58.7 15.4 %collective-permute-start.9 = (f32[24,128]{1,0:T(8,128)S(1)}, f32[24,128]{1,0:T(8,128)S(1)}, u32[]{:S(2)}, u32[]{:S(2)}) collective-permute-start(f32[24,128]{1,0:T(8,128)S(1)} %get-tuple-element.35), channel_id=1, source_target_pairs={{0,6},{1,7},{4,2},{5,3},{8,0},{9,1},{12,4},{13,5},{14,8},{15,9},{1... | collective-permute-start | bytes 36872 | tf_op jit(solution)/shard_map/ppermute | solution.py:320
  65.9 8.2 %collective-permute-start.13 = (f32[24,128]{1,0:T(8,128)S(1)}, f32[24,128]{1,0:T(8,128)S(1)}, u32[]{:S(2)}, u32[]{:S(2)}) collective-permute-start(f32[24,128]{1,0:T(8,128)S(1)} %score.7), channel_id=1, source_target_pairs={{0,14},{1,15},{4,10},{5,11},{8,6},{9,7},{12,2},{13,3},{14,0},{15,1... | collective-permute-start | bytes 36872 | tf_op jit(solution)/shard_map/ppermute | solution.py:320
  70.3 5.5 %collective-permute-start.12 = (f32[24,128]{1,0:T(8,128)S(1)}, f32[24,128]{1,0:T(8,128)S(1)}, u32[]{:S(2)}, u32[]{:S(2)}) collective-permute-start(f32[24,128]{1,0:T(8,128)S(1)} %get-tuple-element.40), channel_id=1, source_target_pairs={{0,10},{1,11},{4,6},{5,7},{8,2},{9,3},{12,0},{13,1},{14,4},{15,5},... | collective-permute-start | bytes 36872 | tf_op jit(solution)/shard_map/ppermute | solution.py:320
  72.3 5.7 %collective-permute-start.14 = (f32[24,128]{1,0:T(8,128)S(1)}, f32[24,128]{1,0:T(8,128)S(1)}, u32[]{:S(2)}, u32[]{:S(2)}) collective-permute-start(f32[24,128]{1,0:T(8,128)S(1)} %get-tuple-element.43), channel_id=1, source_target_pairs={{0,12},{1,13},{4,14},{5,15},{8,10},{9,11},{12,6},{13,7},{14,2},{15... | collective-permute-start | bytes 36872 | tf_op jit(solution)/shard_map/ppermute | solution.py:320

commit v3 on v2

--- a/solution.py
+++ b/solution.py
@@ -11,6 +11,7 @@
 CORES = 2
 LANES = 128
 FACT_ROWS = 16
+GROUP = 4
 VMEM_LIMIT = 32 * 1024 * 1024
 
 
@@ -30,7 +31,15 @@
     return high, middle, low
 
 
-def pack_kernel(per_owner, queries, candidates, block):
+def pack_kernel(per_owner, queries_in, candidates_in, block, queries, candidates, sems):
+    loads = [
+        pltpu.make_async_copy(queries_in, queries, sems.at[0]),
+        pltpu.make_async_copy(candidates_in, candidates, sems.at[1]),
+    ]
+    for load in loads:
+        load.start()
+    for load in loads:
+        load.wait()
     query_rows = queries.shape[0]
     for at in range(0, query_rows, LANES):
         block[at : at + LANES, :] = queries[at : at + LANES, :].T
@@ -45,18 +54,44 @@
     return pl.pallas_call(
         functools.partial(pack_kernel, per_owner),
         out_shape=jax.ShapeDtypeStruct((rows + FACT_ROWS, feature), queries.dtype),
-        in_specs=[pl.BlockSpec(memory_space=pltpu.VMEM)] * 2,
+        in_specs=[pl.BlockSpec(memory_space=pl.ANY)] * 2,
         out_specs=pl.BlockSpec(memory_space=pltpu.VMEM),
-        compiler_params=pltpu.CompilerParams(vmem_limit_bytes=VMEM_LIMIT),
+        scratch_shapes=[
+            pltpu.VMEM(queries.shape, queries.dtype),
+            pltpu.VMEM(candidates.shape, candidates.dtype),
+            pltpu.SemaphoreType.DMA((2,)),
+        ],
+        compiler_params=pltpu.CompilerParams(vmem_limit_bytes=56 * 1024 * 1024),
         name="pack",
     )(queries, candidates)
 
 
-def ready_kernel(chips, slots, candidates, passages, slot_of, own, sem):
-    load = pltpu.make_async_copy(passages, own, sem)
-    load.start()
+def fill_tiles(source, source_at, lens, filled, filled_at, first, number):
+    row = lax.broadcasted_iota(jnp.int32, source.shape[1:], 0)
+
+    def some(i, carry):
+        for k in range(4):
+            at = first + 4 * i + k
+            tile = source[source_at + at].astype(jnp.float32)
+            tile = jnp.where(row < lens[at], tile, tile[0:1, :])
+            filled[filled_at + at] = tile.astype(jnp.bfloat16)
+        return carry
+
+    lax.fori_loop(0, number // 4, some, 0)
+
+
+def ready_kernel(chips, slots, parts, lens, candidates, passages, slot_of, filled, sems):
+    per_owner = passages.shape[0]
+    size = per_owner // parts
+    loads = [
+        pltpu.make_async_copy(
+            passages.at[pl.ds(i * size, size)], filled.at[pl.ds(i * size, size)], sems.at[i]
+        )
+        for i in range(parts)
+    ]
+    for load in loads:
+        load.start()
     number = candidates.shape[1]
-    per_owner = passages.shape[0]
     my_place = ring_place(lax.axis_index("corpus") // CORES, chips)
     wide = jnp.broadcast_to(candidates[...], (number, number)) // (CORES * per_owner)
     tall = wide.astype(jnp.float32).T.astype(jnp.int32)
@@ -67,36 +102,62 @@
     ahead = ring_place(tall, chips) - my_place
     ahead = jnp.where(ahead < 0, ahead + chips, ahead)
     slot_of[...] = ahead * slots + rank
-    load.wait()
-
-
-def ready(candidates, passages, chips, slots):
+    for i, load in enumerate(loads):
+        load.wait()
+        fill_tiles(filled, 0, lens, filled, 0, i * size, size)
+
+
+def ready(lengths, candidates, passages, chips, slots):
     number = candidates.shape[1]
+    per_owner = passages.shape[0]
+    parts = 4 if per_owner % 16 == 0 else 1
     return pl.pallas_call(
-        functools.partial(ready_kernel, chips, slots),
+        functools.partial(ready_kernel, chips, slots, parts),
         out_shape=(
             jax.ShapeDtypeStruct((number, number), jnp.int32),
-            jax.ShapeDtypeStruct(passages.shape, passages.dtype),
+            jax.ShapeDtypeStruct((CORES * per_owner,) + passages.shape[1:], passages.dtype),
         ),
         in_specs=[
-            pl.BlockSpec(memory_space=pltpu.VMEM), pl.BlockSpec(memory_space=pl.ANY)
+            pl.BlockSpec(memory_space=pltpu.SMEM),
+            pl.BlockSpec(memory_space=pltpu.VMEM),
+            pl.BlockSpec(memory_space=pl.ANY),
         ],
         out_specs=(pl.BlockSpec(memory_space=pltpu.VMEM),) * 2,
-        scratch_shapes=[pltpu.SemaphoreType.DMA],
+        scratch_shapes=[pltpu.SemaphoreType.DMA((parts,))],
         compiler_params=pltpu.CompilerParams(vmem_limit_bytes=VMEM_LIMIT),
         name="ready",
-    )(candidates, passages)
+    )(lengths, candidates, passages)
+
+
+def join_kernel(lens, other, held, filled):
+    fill_tiles(other, 0, lens, filled, other.shape[0], 0, other.shape[0])
+
+
+def join(lengths, other, filled):
+    return pl.pallas_call(
+        join_kernel,
+        out_shape=jax.ShapeDtypeStruct(filled.shape, filled.dtype),
+        in_specs=[
+            pl.BlockSpec(memory_space=pltpu.SMEM),
+            pl.BlockSpec(memory_space=pltpu.VMEM),
+            pl.BlockSpec(memory_space=pltpu.VMEM),
+        ],
+        out_specs=pl.BlockSpec(memory_space=pltpu.VMEM),
+        input_output_aliases={2: 0},
+        compiler_params=pltpu.CompilerParams(vmem_limit_bytes=VMEM_LIMIT),
+        name="join",
+    )(lengths, other, filled)
 
 
 def score_kernel(pieces, slots, query_tok, *refs):
     blocks = len(pieces)
     arrays = sum(pieces)
-    own_lens, other_lens, own, other = refs[:4]
-    held = refs[4 : 4 + arrays]
-    outs = refs[4 + arrays : 4 + arrays + blocks]
-    mixed, left, nearest, plan_v, plan, sem = refs[4 + arrays + blocks :]
-    per_owner, tile_rows, feature = own.shape
-    query_rows = nearest.shape[1]
+    tiles = refs[0]
+    held = refs[1 : 1 + arrays]
+    outs = refs[1 + arrays : 1 + arrays + blocks]
+    nearest, plan_v, plan, sem = refs[1 + arrays + blocks :]
+    per_chip, tile_rows, feature = tiles.shape
+    per_owner = per_chip // CORES
     me = lax.axis_index("corpus")
     first_owner = me // CORES * CORES
 
@@ -135,41 +196,32 @@
     to_scalar.start()
     to_scalar.wait()
 
-    tile_row = lax.broadcasted_iota(jnp.int32, (tile_rows, feature), 0)
     slot_row = lax.broadcasted_iota(jnp.int32, (slots, LANES), 0)
     slot_lane = lax.broadcasted_iota(jnp.int32, (slots, LANES), 1)
     for b in range(blocks):
         count = plan[b, slots]
 
         def score_group(g, carry, b=b):
-            start = pl.multiple_of(g * 8, 8)
-            for t in range(8):
-                at = plan[b, start + t]
-                here = at < per_owner
-                at_own = jnp.minimum(at, per_owner - 1)
-                at_other = jnp.maximum(at - per_owner, 0)
-                length = jnp.where(here, own_lens[at_own], other_lens[at_other])
-                tile = jnp.where(
-                    here, own[at_own].astype(jnp.float32), other[at_other].astype(jnp.float32)
-                )
-                tile = jnp.where(tile_row < length, tile, tile[0:1, :])
-                mixed[pl.ds(t, tile_rows, stride=8), :] = tile
-            left[...] = mixed[...].astype(jnp.bfloat16)
+            left = jnp.concatenate([tiles[plan[b, g * GROUP + t]] for t in range(GROUP)], axis=0)
+            start = pl.multiple_of(g * (8 * GROUP), 8 * GROUP)
             for c in range(0, len(chunks[b]), 2):
                 pair = [ref[r : r + LANES, :] for ref, r in chunks[b][c : c + 2]]
                 similar = jnp.dot(
-                    left[...], jnp.concatenate(pair, axis=1), preferred_element_type=jnp.float32
+                    left, jnp.concatenate(pair, axis=1), preferred_element_type=jnp.float32
                 )
                 width = similar.shape[1]
-                nearest[pl.ds(start, 8), c * LANES : c * LANES + width] = jnp.max(
-                    similar.reshape(tile_rows, 8, width), axis=0
-                )
+                rows = jnp.max(similar.reshape(GROUP, tile_rows // 8, 8, width), axis=1)
+                rows = rows.reshape(8 * GROUP, width)
+                for k in range(width // LANES):
+                    nearest[c + k, pl.ds(start, 8 * GROUP), :] = rows[:, k * LANES : (k + 1) * LANES]
             return carry
 
-        lax.fori_loop(0, pl.cdiv(count, 8), score_group, 0)
+        lax.fori_loop(0, pl.cdiv(count, GROUP), score_group, 0)
         total = jnp.zeros((slots, LANES), jnp.float32)
-        for k in range(query_rows // LANES):
-            x = nearest[:, k * LANES : (k + 1) * LANES]
+        for k in range(nearest.shape[0]):
+            x = nearest[k, pl.ds(0, slots, stride=8), :]
+            for sublane in range(1, 8):
+                x = jnp.maximum(x, nearest[k, pl.ds(sublane, slots, stride=8), :])
             shift = query_tok // 2
             while shift >= 1:
                 x = x + pltpu.roll(x, LANES - shift, 1)
@@ -180,23 +232,20 @@
         outs[b][...] = jnp.where(slot_row < count, total / float(query_tok), 0.0)
 
 
-def score(held, slots, query_tok, own_lens, other_lens, own, other):
+def score(held, slots, query_tok, tiles):
     pieces = tuple(len(arrays) for arrays in held)
     flat = [x for arrays in held for x in arrays]
     blocks = len(pieces)
-    _, tile_rows, feature = own.shape
+    _, tile_rows, feature = tiles.shape
     query_rows = sum(x.shape[0] for x in held[0]) - FACT_ROWS
     flops = 2 * blocks * slots * tile_rows * feature * query_rows
     return pl.pallas_call(
         functools.partial(score_kernel, pieces, slots, query_tok),
         out_shape=(jax.ShapeDtypeStruct((slots, LANES), jnp.float32),) * blocks,
-        in_specs=[pl.BlockSpec(memory_space=pltpu.SMEM)] * 2
-        + [pl.BlockSpec(memory_space=pltpu.VMEM)] * (2 + len(flat)),
+        in_specs=[pl.BlockSpec(memory_space=pltpu.VMEM)] * (1 + len(flat)),
         out_specs=(pl.BlockSpec(memory_space=pltpu.VMEM),) * blocks,
         scratch_shapes=[
-            pltpu.VMEM((8 * tile_rows, feature), jnp.float32),
-            pltpu.VMEM((8 * tile_rows, feature), jnp.bfloat16),
-            pltpu.VMEM((slots, query_rows), jnp.float32),
+            pltpu.VMEM((query_rows // LANES, 8 * slots, LANES), jnp.float32),
             pltpu.VMEM((8, LANES), jnp.int32),
             pltpu.SMEM((8, LANES), jnp.int32),
             pltpu.SemaphoreType.DMA,
@@ -208,7 +257,7 @@
             transcendentals=0,
         ),
         name="score",
-    )(own_lens, other_lens, own, other, *flat)
+    )(tiles, *flat)
 
 
 def sort_descending(parts, lanes):
@@ -322,7 +371,8 @@
     swap = [(i, i ^ 1) for i in range(peers)]
     other = lax.ppermute(passages, "corpus", swap)
     other_lengths = lax.ppermute(lengths, "corpus", swap)
-    slot_of, own = ready(candidates, passages, chips, slots)
+    slot_of, own = ready(lengths, candidates, passages, chips, slots)
+    tiles = join(other_lengths, other, own)
 
     block = pack(queries.reshape(per_device * query_tok, feature), candidates, per_owner)
     half = per_device * query_tok // LANES // 2 * LANES
@@ -344,14 +394,15 @@
         if step < middle:
             send_on(step + 1)
         offsets = (0, 1, -1) if step == 1 else (middle,) if step == middle else (step, -step)
-        fresh = score(
-            [arrived[offset] for offset in offsets], slots, query_tok,
-            lengths, other_lengths, own, other,
-        )
+        fresh = score([arrived[offset] for offset in offsets], slots, query_tok, tiles)
         if step < middle:
             names = [step + 1, -step - 1] if step + 1 < middle else [middle]
-            held, fresh = lax.optimization_barrier(([arrived[name] for name in names], fresh))
+            earlier = [(1 - step) % chips, (step - 1) % chips] if step > 1 else []
+            held, fresh, came = lax.optimization_barrier(
+                ([arrived[name] for name in names], fresh, [back[j] for j in earlier])
+            )
             arrived.update(zip(names, held))
+            back.update(zip(earlier, came))
         for offset, result in zip(offsets, fresh):
             back[offset % chips] = moved(result, -offset) if offset else result
     return finish(per_device, query_tok, slot_of, [back[j] for j in range(chips)])

time: 78.2 us -> 80.1 us (1.024)
  the two profiles are of different devices: /device:TPU:0 before, /device:TPU:2 now
where the time goes in v3:
time: 80.1 us; the launch traced here: 79.4 us
  Pallas kernels  37.5 us (47%)
  starting transfers between devices  23.3 us (29%)
  waiting for transfers between devices  14.3 us (18%)
  local copies, waits for them, and re-layouts  3.53 us (4%)
    pallas_call x4, Pallas kernels, score(): pl.pallas_call(functools.partial(score_kernel, pieces, slots, query_tok),...  30.4 us
    ppermute x15, starting transfers between devices, moved(): return lax.ppermute(x, 'corpus', pairs)  23.2 us
    ppermute x15, waiting for transfers between devices, moved(): return lax.ppermute(x, 'corpus', pairs)  14.3 us
    unnamed x8, local copies, waits for them, and re-layouts  3.5 us
    pallas_call x1, Pallas kernels, ready(): pl.pallas_call(functools.partial(ready_kernel, chips, slots, parts), out_...  2.36 us
    pallas_call x1, Pallas kernels, pack(): pl.pallas_call(functools.partial(pack_kernel, per_owner), out_shape=jax.S...  1.99 us
    pallas_call x1, Pallas kernels, join(): pl.pallas_call(join_kernel, out_shape=jax.ShapeDtypeStruct(filled.shape,...  1.64 us
  transfers between devices with their start and end apart: 17, of which 5 were waited for; matrix products, arithmetic and copies ran while one was open for 0% of the time, Pallas kernels for 40%

profile of v3, /device:TPU:2, one launch (start us, length us, event | category | flops | bytes accessed | tf_op | source)
XLA Modules:
  0.0 79.4 jit_solution(5941417618053630629)
XLA Ops:
  0.6 0.1 collective-permute-start.5
  0.7 2.0 %pack.1.refs_1_ = bf16[1808,128]{1,0:T(8,128)(2,1)} custom-call(bf16[1792,128]{1,0:T(8,128)(2,1)} %bitcast.1, s32[1,128]{1,0:T(1,128)} %candidates_in.1), custom_call_target="tpu_custom_call" | custom-call | tf_op jit(solution)/shard_map/pack/pallas_call | solution.py:54
  2.7 1.6 %collective-permute-start = (bf16[1808,128]{1,0:T(8,128)(2,1)}, bf16[1808,128]{1,0:T(8,128)(2,1)S(1)}, u32[]{:S(2)}, u32[]{:S(2)}) collective-permute-start(bf16[1808,128]{1,0:T(8,128)(2,1)} %pack.1.refs_1_), channel_id=1, source_target_pairs={{0,4},{1,5},{4,8},{5,9},{8,12},{9,13},{12,14},{13,15},{14,10},{15,... | collective-permute-start | bytes 1388552 | tf_op jit(solution)/shard_map/ppermute | solution.py:369
  4.3 0.4 collective-permute-start.2
  4.8 0.0 collective-permute-start.4
  4.8 0.0 copy-start
  4.8 2.2 %copy-done = bf16[128,128,128]{2,1,0:T(8,128)(2,1)S(1)} copy-done((bf16[128,128,128]{2,1,0:T(8,128)(2,1)S(1)}, bf16[128,128,128]{2,1,0:T(8,128)(2,1)}, u32[]{:S(2)}) %copy-start) | copy-done | bytes 4194328
  7.0 0.0 copy-start.2
  7.0 0.7 copy-done.2
  7.6 0.0 copy-start.3
  7.6 0.7 copy-done.3
  8.3 2.4 %ready.1 = (s32[128,128]{1,0:T(8,128)S(1)}, bf16[256,128,128]{2,1,0:T(8,128)(2,1)S(1)}) custom-call(s32[128]{0:T(128)S(1)} %copy-done.3, s32[1,128]{1,0:T(1,128)S(1)} %copy-done.2, bf16[128,128,128]{2,1,0:T(8,128)(2,1)S(1)} %copy-done), custom_call_target="tpu_custom_call" | custom-call | tf_op jit(solution)/shard_map/ready/pallas_call | solution.py:114
  10.7 5.3 %collective-permute-done.refs_2_ = bf16[1808,128]{1,0:T(8,128)(2,1)S(1)} collective-permute-done((bf16[1808,128]{1,0:T(8,128)(2,1)}, bf16[1808,128]{1,0:T(8,128)(2,1)S(1)}, u32[]{:S(2)}, u32[]{:S(2)}) %collective-permute-start) | collective-permute-done | bytes 462880 | tf_op jit(solution)/shard_map/ppermute | solution.py:369
  16.0 1.6 %collective-permute-start.1 = (bf16[1808,128]{1,0:T(8,128)(2,1)S(1)}, bf16[1808,128]{1,0:T(8,128)(2,1)S(1)}, u32[]{:S(2)}, u32[]{:S(2)}) collective-permute-start(bf16[1808,128]{1,0:T(8,128)(2,1)S(1)} %collective-permute-done.refs_2_), channel_id=1, source_target_pairs={{0,4},{1,5},{4,8},{5,9},{8,12},{9,13},{12,14},{13,15},{14,10},{15,... | collective-permute-start | bytes 1388552 | tf_op jit(solution)/shard_map/ppermute | solution.py:369
  17.6 0.0 collective-permute-done.2.refs_3_
  17.6 0.5 collective-permute-start.3
  18.0 0.0 collective-permute-done.4.lens
  18.0 0.0 collective-permute-done.5.other
  18.0 0.0 copy-start.1
  18.0 1.6 %join.1.refs_0_ = bf16[256,128,128]{2,1,0:T(8,128)(2,1)S(1)} custom-call(s32[128]{0:T(128)S(1)} %collective-permute-done.4.lens, bf16[128,128,128]{2,1,0:T(8,128)(2,1)S(1)} %collective-permute-done.5.other, bf16[256,128,128]{2,1,0:T(8,128)(2,1)S(1)} %get-tuple-element.29.held), custom_call_target="tpu_custom_call", output_to_operand_aliasing={{}: (2, {})} | custom-call | tf_op jit(solution)/shard_map/join/pallas_call | solution.py:137
  19.7 0.0 copy-done.1
  19.7 11.8 %score.4 = (f32[24,128]{1,0:T(8,128)S(1)}, f32[24,128]{1,0:T(8,128)S(1)}, f32[24,128]{1,0:T(8,128)S(1)}) custom-call(bf16[256,128,128]{2,1,0:T(8,128)(2,1)S(1)} %join.1.refs_0_, bf16[1808,128]{1,0:T(8,128)(2,1)S(1)} %copy-done.1, bf16[1808,128]{1,0:T(8,128)(2,1)S(1)} %collective-permute-done.refs_2_, bf16[1808,128]{1,0:T(8,128)(2,1)S(1)} %collective-permute-done.2.refs_3_), custom_call_target="tpu_custom_call" | custom-call | flops 12683575296 | bytes 3735552 | tf_op jit(solution)/shard_map/score/pallas_call | solution.py:242
  31.5 0.0 collective-permute-done.1.refs_1_
  31.5 0.0 collective-permute-done.3.refs_2_
  31.5 4.1 %collective-permute-start.6 = (bf16[1808,128]{1,0:T(8,128)(2,1)S(1)}, bf16[1808,128]{1,0:T(8,128)(2,1)S(1)}, u32[]{:S(2)}, u32[]{:S(2)}) collective-permute-start(bf16[1808,128]{1,0:T(8,128)(2,1)S(1)} %collective-permute-done.1.refs_1_), channel_id=1, source_target_pairs={{0,4},{1,5},{4,8},{5,9},{8,12},{9,13},{12,14},{13,15},{14,10},{15,... | collective-permute-start | bytes 1388552 | tf_op jit(solution)/shard_map/ppermute | solution.py:369
  35.7 0.0 collective-permute-start.7
  35.7 2.0 %collective-permute-start.8 = (f32[24,128]{1,0:T(8,128)S(1)}, f32[24,128]{1,0:T(8,128)S(1)}, u32[]{:S(2)}, u32[]{:S(2)}) collective-permute-start(f32[24,128]{1,0:T(8,128)S(1)} %get-tuple-element.38), channel_id=1, source_target_pairs={{0,4},{1,5},{4,8},{5,9},{8,12},{9,13},{12,14},{13,15},{14,10},{15,... | collective-permute-start | bytes 36872 | tf_op jit(solution)/shard_map/ppermute | solution.py:369
  37.7 0.0 collective-permute-start.9
  37.7 6.2 %score.5 = (f32[24,128]{1,0:T(8,128)S(1)}, f32[24,128]{1,0:T(8,128)S(1)}) custom-call(bf16[256,128,128]{2,1,0:T(8,128)(2,1)S(1)} %join.1.refs_0_, bf16[1808,128]{1,0:T(8,128)(2,1)S(1)} %collective-permute-done.1.refs_1_, bf16[1808,128]{1,0:T(8,128)(2,1)S(1)} %collective-permute-done.3.refs_2_), custom_call_target="tpu_custom_call" | custom-call | flops 8455716864 | bytes 2490368 | tf_op jit(solution)/shard_map/score/pallas_call | solution.py:242
  43.9 1.3 %collective-permute-done.8.refs_7_ = f32[24,128]{1,0:T(8,128)S(1)} collective-permute-done((f32[24,128]{1,0:T(8,128)S(1)}, f32[24,128]{1,0:T(8,128)S(1)}, u32[]{:S(2)}, u32[]{:S(2)}) %collective-permute-start.8) | collective-permute-done | bytes 12320 | tf_op jit(solution)/shard_map/ppermute | solution.py:369
  45.1 2.2 %collective-permute-done.9.refs_1_ = f32[24,128]{1,0:T(8,128)S(1)} collective-permute-done((f32[24,128]{1,0:T(8,128)S(1)}, f32[24,128]{1,0:T(8,128)S(1)}, u32[]{:S(2)}, u32[]{:S(2)}) %collective-permute-start.9) | collective-permute-done | bytes 12320 | tf_op jit(solution)/shard_map/ppermute | solution.py:369
  47.3 0.0 collective-permute-done.6.refs_1_
  47.3 0.0 collective-permute-done.7.refs_2_
  47.4 0.3 collective-permute-start.11
  47.7 2.1 %collective-permute-start.10 = (bf16[896,128]{1,0:T(8,128)(2,1)S(1)}, bf16[896,128]{1,0:T(8,128)(2,1)S(1)}, u32[]{:S(2)}, u32[]{:S(2)}) collective-permute-start(bf16[896,128]{1,0:T(8,128)(2,1)S(1)} %slice.6), channel_id=1, source_target_pairs={{0,4},{1,5},{4,8},{5,9},{8,12},{9,13},{12,14},{13,15},{14,10},{15,... | collective-permute-start | bytes 688136 | tf_op jit(solution)/shard_map/ppermute | solution.py:369
  49.8 1.5 %collective-permute-start.12 = (f32[24,128]{1,0:T(8,128)S(1)}, f32[24,128]{1,0:T(8,128)S(1)}, u32[]{:S(2)}, u32[]{:S(2)}) collective-permute-start(f32[24,128]{1,0:T(8,128)S(1)} %get-tuple-element.45), channel_id=1, source_target_pairs={{0,8},{1,9},{4,12},{5,13},{8,14},{9,15},{12,10},{13,11},{14,6},{15... | collective-permute-start | bytes 36872 | tf_op jit(solution)/shard_map/ppermute | solution.py:369
  51.4 1.4 %collective-permute-start.13 = (f32[24,128]{1,0:T(8,128)S(1)}, f32[24,128]{1,0:T(8,128)S(1)}, u32[]{:S(2)}, u32[]{:S(2)}) collective-permute-start(f32[24,128]{1,0:T(8,128)S(1)} %get-tuple-element.46), channel_id=1, source_target_pairs={{0,6},{1,7},{4,2},{5,3},{8,0},{9,1},{12,4},{13,5},{14,8},{15,9},{1... | collective-permute-start | bytes 36872 | tf_op jit(solution)/shard_map/ppermute | solution.py:369
  52.8 8.0 %score.6 = (f32[24,128]{1,0:T(8,128)S(1)}, f32[24,128]{1,0:T(8,128)S(1)}) custom-call(bf16[256,128,128]{2,1,0:T(8,128)(2,1)S(1)} %join.1.refs_0_, bf16[1808,128]{1,0:T(8,128)(2,1)S(1)} %collective-permute-done.6.refs_1_, bf16[1808,128]{1,0:T(8,128)(2,1)S(1)} %collective-permute-done.7.refs_2_), custom_call_target="tpu_custom_call" | custom-call | flops 8455716864 | bytes 2490368 | tf_op jit(solution)/shard_map/score/pallas_call | solution.py:242
  60.8 0.0 collective-permute-done.12.refs_6_
  60.8 0.0 collective-permute-done.13.refs_2_
  60.9 0.0 collective-permute-done.10.refs_1_
  60.9 0.0 collective-permute-done.11.refs_2_
  60.9 4.3 %score.7 = f32[24,128]{1,0:T(8,128)S(1)} custom-call(bf16[256,128,128]{2,1,0:T(8,128)(2,1)S(1)} %join.1.refs_0_, bf16[896,128]{1,0:T(8,128)(2,1)S(1)} %collective-permute-done.10.refs_1_, bf16[912,128]{1,0:T(8,128)(2,1)S(1)} %collective-permute-done.11.refs_2_), custom_call_target="tpu_custom_call" | custom-call | flops 4227858432 | bytes 1245184 | tf_op jit(solution)/shard_map/score/pallas_call | solution.py:242
  65.2 0.6 collective-permute-start.15
  65.8 7.0 %collective-permute-start.14 = (f32[24,128]{1,0:T(8,128)S(1)}, f32[24,128]{1,0:T(8,128)S(1)}, u32[]{:S(2)}, u32[]{:S(2)}) collective-permute-start(f32[24,128]{1,0:T(8,128)S(1)} %get-tuple-element.48), channel_id=1, source_target_pairs={{0,10},{1,11},{4,6},{5,7},{8,2},{9,3},{12,0},{13,1},{14,4},{15,5},... | collective-permute-start | bytes 36872 | tf_op jit(solution)/shard_map/ppermute | solution.py:369
  72.8 0.0 collective-permute-start.16
  72.8 0.0 collective-permute-done.15.refs_4_
  72.8 1.4 %collective-permute-done.14.refs_3_ = f32[24,128]{1,0:T(8,128)S(1)} collective-permute-done((f32[24,128]{1,0:T(8,128)S(1)}, f32[24,128]{1,0:T(8,128)S(1)}, u32[]{:S(2)}, u32[]{:S(2)}) %collective-permute-start.14) | collective-permute-done | bytes 12320 | tf_op jit(solution)/shard_map/ppermute | solution.py:369
  74.2 4.1 %collective-permute-done.16.refs_5_ = f32[24,128]{1,0:T(8,128)S(1)} collective-permute-done((f32[24,128]{1,0:T(8,128)S(1)}, f32[24,128]{1,0:T(8,128)S(1)}, u32[]{:S(2)}, u32[]{:S(2)}) %collective-permute-start.16) | collective-permute-done | bytes 12320 | tf_op jit(solution)/shard_map/ppermute | solution.py:369
  78.3 1.1 %finish.1 = (f32[56,128]{1,0:T(8,128)}, f32[56,100]{1,0:T(8,128)}) custom-call(s32[128,128]{1,0:T(8,128)S(1)} %get-tuple-element.28.slot_of, f32[24,128]{1,0:T(8,128)S(1)} %get-tuple-element.33.refs_0_, f32[24,128]{1,0:T(8,128)S(1)} %collective-permute-done.9.refs_1_, f32[24,128]{1,0:T(8,128)S(1)} %collective-permute-done.13.refs_2_, ...), custom_call_target="tpu_custom_call" | custom-call | tf_op jit(solution)/shard_map/finish/pallas_call | solution.py:335
  (2 shorter events, 0.0 us)
Async XLA Ops:
  0.6 17.4 %collective-permute-start.5 = (bf16[128,128,128]{2,1,0:T(8,128)(2,1)}, bf16[128,128,128]{2,1,0:T(8,128)(2,1)S(1)}, u32[]{:S(2)}, u32[]{:S(2)}) collective-permute-start(bf16[128,128,128]{2,1,0:T(8,128)(2,1)} %passages.1), channel_id=1, source_target_pairs={{0,1},{1,0},{2,3},{3,2},{4,5},{5,4},{6,7},{7,6},{8,9},{9,8},{10,11... | collective-permute-start | bytes 12582920 | tf_op jit(solution)/shard_map/ppermute | solution.py:372
  2.7 13.3 %collective-permute-start = (bf16[1808,128]{1,0:T(8,128)(2,1)}, bf16[1808,128]{1,0:T(8,128)(2,1)S(1)}, u32[]{:S(2)}, u32[]{:S(2)}) collective-permute-start(bf16[1808,128]{1,0:T(8,128)(2,1)} %pack.1.refs_1_), channel_id=1, source_target_pairs={{0,4},{1,5},{4,8},{5,9},{8,12},{9,13},{12,14},{13,15},{14,10},{15,... | collective-permute-start | bytes 1388552 | tf_op jit(solution)/shard_map/ppermute | solution.py:369
  4.3 13.2 %collective-permute-start.2 = (bf16[1808,128]{1,0:T(8,128)(2,1)}, bf16[1808,128]{1,0:T(8,128)(2,1)S(1)}, u32[]{:S(2)}, u32[]{:S(2)}) collective-permute-start(bf16[1808,128]{1,0:T(8,128)(2,1)} %pack.1.refs_1_), channel_id=1, source_target_pairs={{0,2},{1,3},{4,0},{5,1},{8,4},{9,5},{12,8},{13,9},{14,12},{15,13},... | collective-permute-start | bytes 1388552 | tf_op jit(solution)/shard_map/ppermute | solution.py:369
  4.8 13.2 %collective-permute-start.4 = (s32[128]{0:T(128)}, s32[128]{0:T(128)S(1)}, u32[]{:S(2)}, u32[]{:S(2)}) collective-permute-start(s32[128]{0:T(128)} %lens.1), channel_id=1, source_target_pairs={{0,1},{1,0},{2,3},{3,2},{4,5},{5,4},{6,7},{7,6},{8,9},{9,8},{10,11... | collective-permute-start | bytes 1544 | tf_op jit(solution)/shard_map/ppermute | solution.py:373
  4.8 2.2 %copy-start = (bf16[128,128,128]{2,1,0:T(8,128)(2,1)S(1)}, bf16[128,128,128]{2,1,0:T(8,128)(2,1)}, u32[]{:S(2)}) copy-start(bf16[128,128,128]{2,1,0:T(8,128)(2,1)} %passages.1) | copy-start | bytes 12582916
  7.0 0.7 copy-start.2
  7.6 0.7 copy-start.3
  16.0 15.6 %collective-permute-start.1 = (bf16[1808,128]{1,0:T(8,128)(2,1)S(1)}, bf16[1808,128]{1,0:T(8,128)(2,1)S(1)}, u32[]{:S(2)}, u32[]{:S(2)}) collective-permute-start(bf16[1808,128]{1,0:T(8,128)(2,1)S(1)} %collective-permute-done.refs_2_), channel_id=1, source_target_pairs={{0,4},{1,5},{4,8},{5,9},{8,12},{9,13},{12,14},{13,15},{14,10},{15,... | collective-permute-start | bytes 1388552 | tf_op jit(solution)/shard_map/ppermute | solution.py:369
  17.6 14.0 %collective-permute-start.3 = (bf16[1808,128]{1,0:T(8,128)(2,1)S(1)}, bf16[1808,128]{1,0:T(8,128)(2,1)S(1)}, u32[]{:S(2)}, u32[]{:S(2)}) collective-permute-start(bf16[1808,128]{1,0:T(8,128)(2,1)S(1)} %collective-permute-done.2.refs_3_), channel_id=1, source_target_pairs={{0,2},{1,3},{4,0},{5,1},{8,4},{9,5},{12,8},{13,9},{14,12},{15,13},... | collective-permute-start | bytes 1388552 | tf_op jit(solution)/shard_map/ppermute | solution.py:369
  18.0 1.7 %copy-start.1 = (bf16[1808,128]{1,0:T(8,128)(2,1)S(1)}, bf16[1808,128]{1,0:T(8,128)(2,1)}, u32[]{:S(2)}) copy-start(bf16[1808,128]{1,0:T(8,128)(2,1)} %pack.1.refs_1_) | copy-start | bytes 1388548
  31.5 15.8 %collective-permute-start.6 = (bf16[1808,128]{1,0:T(8,128)(2,1)S(1)}, bf16[1808,128]{1,0:T(8,128)(2,1)S(1)}, u32[]{:S(2)}, u32[]{:S(2)}) collective-permute-start(bf16[1808,128]{1,0:T(8,128)(2,1)S(1)} %collective-permute-done.1.refs_1_), channel_id=1, source_target_pairs={{0,4},{1,5},{4,8},{5,9},{8,12},{9,13},{12,14},{13,15},{14,10},{15,... | collective-permute-start | bytes 1388552 | tf_op jit(solution)/shard_map/ppermute | solution.py:369
  35.7 11.7 %collective-permute-start.7 = (bf16[1808,128]{1,0:T(8,128)(2,1)S(1)}, bf16[1808,128]{1,0:T(8,128)(2,1)S(1)}, u32[]{:S(2)}, u32[]{:S(2)}) collective-permute-start(bf16[1808,128]{1,0:T(8,128)(2,1)S(1)} %collective-permute-done.3.refs_2_), channel_id=1, source_target_pairs={{0,2},{1,3},{4,0},{5,1},{8,4},{9,5},{12,8},{13,9},{14,12},{15,13},... | collective-permute-start | bytes 1388552 | tf_op jit(solution)/shard_map/ppermute | solution.py:369
  35.7 9.4 %collective-permute-start.8 = (f32[24,128]{1,0:T(8,128)S(1)}, f32[24,128]{1,0:T(8,128)S(1)}, u32[]{:S(2)}, u32[]{:S(2)}) collective-permute-start(f32[24,128]{1,0:T(8,128)S(1)} %get-tuple-element.38), channel_id=1, source_target_pairs={{0,4},{1,5},{4,8},{5,9},{8,12},{9,13},{12,14},{13,15},{14,10},{15,... | collective-permute-start | bytes 36872 | tf_op jit(solution)/shard_map/ppermute | solution.py:369
  37.7 9.6 %collective-permute-start.9 = (f32[24,128]{1,0:T(8,128)S(1)}, f32[24,128]{1,0:T(8,128)S(1)}, u32[]{:S(2)}, u32[]{:S(2)}) collective-permute-start(f32[24,128]{1,0:T(8,128)S(1)} %get-tuple-element.39), channel_id=1, source_target_pairs={{0,2},{1,3},{4,0},{5,1},{8,4},{9,5},{12,8},{13,9},{14,12},{15,13},... | collective-permute-start | bytes 36872 | tf_op jit(solution)/shard_map/ppermute | solution.py:369
  47.4 13.5 %collective-permute-start.11 = (bf16[912,128]{1,0:T(8,128)(2,1)S(1)}, bf16[912,128]{1,0:T(8,128)(2,1)S(1)}, u32[]{:S(2)}, u32[]{:S(2)}) collective-permute-start(bf16[912,128]{1,0:T(8,128)(2,1)S(1)} %slice.7), channel_id=1, source_target_pairs={{0,2},{1,3},{4,0},{5,1},{8,4},{9,5},{12,8},{13,9},{14,12},{15,13},... | collective-permute-start | bytes 700424 | tf_op jit(solution)/shard_map/ppermute | solution.py:369
  47.7 13.1 %collective-permute-start.10 = (bf16[896,128]{1,0:T(8,128)(2,1)S(1)}, bf16[896,128]{1,0:T(8,128)(2,1)S(1)}, u32[]{:S(2)}, u32[]{:S(2)}) collective-permute-start(bf16[896,128]{1,0:T(8,128)(2,1)S(1)} %slice.6), channel_id=1, source_target_pairs={{0,4},{1,5},{4,8},{5,9},{8,12},{9,13},{12,14},{13,15},{14,10},{15,... | collective-permute-start | bytes 688136 | tf_op jit(solution)/shard_map/ppermute | solution.py:369
  49.8 11.0 %collective-permute-start.12 = (f32[24,128]{1,0:T(8,128)S(1)}, f32[24,128]{1,0:T(8,128)S(1)}, u32[]{:S(2)}, u32[]{:S(2)}) collective-permute-start(f32[24,128]{1,0:T(8,128)S(1)} %get-tuple-element.45), channel_id=1, source_target_pairs={{0,8},{1,9},{4,12},{5,13},{8,14},{9,15},{12,10},{13,11},{14,6},{15... | collective-permute-start | bytes 36872 | tf_op jit(solution)/shard_map/ppermute | solution.py:369
  51.4 9.5 %collective-permute-start.13 = (f32[24,128]{1,0:T(8,128)S(1)}, f32[24,128]{1,0:T(8,128)S(1)}, u32[]{:S(2)}, u32[]{:S(2)}) collective-permute-start(f32[24,128]{1,0:T(8,128)S(1)} %get-tuple-element.46), channel_id=1, source_target_pairs={{0,6},{1,7},{4,2},{5,3},{8,0},{9,1},{12,4},{13,5},{14,8},{15,9},{1... | collective-permute-start | bytes 36872 | tf_op jit(solution)/shard_map/ppermute | solution.py:369
  65.2 7.6 %collective-permute-start.15 = (f32[24,128]{1,0:T(8,128)S(1)}, f32[24,128]{1,0:T(8,128)S(1)}, u32[]{:S(2)}, u32[]{:S(2)}) collective-permute-start(f32[24,128]{1,0:T(8,128)S(1)} %score.7), channel_id=1, source_target_pairs={{0,14},{1,15},{4,10},{5,11},{8,6},{9,7},{12,2},{13,3},{14,0},{15,1... | collective-permute-start | bytes 36872 | tf_op jit(solution)/shard_map/ppermute | solution.py:369
  65.8 8.4 %collective-permute-start.14 = (f32[24,128]{1,0:T(8,128)S(1)}, f32[24,128]{1,0:T(8,128)S(1)}, u32[]{:S(2)}, u32[]{:S(2)}) collective-permute-start(f32[24,128]{1,0:T(8,128)S(1)} %get-tuple-element.48), channel_id=1, source_target_pairs={{0,10},{1,11},{4,6},{5,7},{8,2},{9,3},{12,0},{13,1},{14,4},{15,5},... | collective-permute-start | bytes 36872 | tf_op jit(solution)/shard_map/ppermute | solution.py:369
  72.8 5.5 %collective-permute-start.16 = (f32[24,128]{1,0:T(8,128)S(1)}, f32[24,128]{1,0:T(8,128)S(1)}, u32[]{:S(2)}, u32[]{:S(2)}) collective-permute-start(f32[24,128]{1,0:T(8,128)S(1)} %get-tuple-element.51), channel_id=1, source_target_pairs={{0,12},{1,13},{4,14},{5,15},{8,10},{9,11},{12,6},{13,7},{14,2},{15... | collective-permute-start | bytes 36872 | tf_op jit(solution)/shard_map/ppermute | solution.py:369

commit v4 on v3

--- a/solution.py
+++ b/solution.py
@@ -92,16 +92,13 @@
     for load in loads:
         load.start()
     number = candidates.shape[1]
-    my_place = ring_place(lax.axis_index("corpus") // CORES, chips)
     wide = jnp.broadcast_to(candidates[...], (number, number)) // (CORES * per_owner)
     tall = wide.astype(jnp.float32).T.astype(jnp.int32)
     row = lax.broadcasted_iota(jnp.int32, (number, number), 0)
     lane = lax.broadcasted_iota(jnp.int32, (number, number), 1)
     earlier = jnp.where((wide == tall) & (lane < row), 1.0, 0.0)
     rank = jnp.sum(earlier, axis=1, keepdims=True).astype(jnp.int32)
-    ahead = ring_place(tall, chips) - my_place
-    ahead = jnp.where(ahead < 0, ahead + chips, ahead)
-    slot_of[...] = ahead * slots + rank
+    slot_of[...] = ring_place(tall, chips) * slots + rank
     for i, load in enumerate(loads):
         load.wait()
         fill_tiles(filled, 0, lens, filled, 0, i * size, size)
@@ -149,24 +146,33 @@
     )(lengths, other, filled)
 
 
-def score_kernel(pieces, slots, query_tok, *refs):
+def score_kernel(pieces, offsets, slots, query_tok, has_earlier, *refs):
     blocks = len(pieces)
     arrays = sum(pieces)
     tiles = refs[0]
     held = refs[1 : 1 + arrays]
-    outs = refs[1 + arrays : 1 + arrays + blocks]
-    nearest, plan_v, plan, sem = refs[1 + arrays + blocks :]
+    out, weights, nearest, plan_v, plan, sem, weight_sems = refs[1 + arrays + has_earlier :]
     per_chip, tile_rows, feature = tiles.shape
     per_owner = per_chip // CORES
+    chips = out.shape[0]
     me = lax.axis_index("corpus")
     first_owner = me // CORES * CORES
-
-    chunks, facts = [], []
+    my_place = ring_place(me // CORES, chips)
+
+    loads, facts = [], []
     at = 0
-    for count in pieces:
-        where = [(ref, r) for ref in held[at : at + count] for r in range(0, ref.shape[0], LANES)]
-        facts.append(where[-1])
-        chunks.append(where[:-1])
+    for b, count in enumerate(pieces):
+        row = 0
+        for ref in held[at : at + count]:
+            rows = min(ref.shape[0], weights.shape[1] - row)
+            loads.append(
+                pltpu.make_async_copy(
+                    ref.at[pl.ds(0, rows)], weights.at[b, pl.ds(row, rows)], weight_sems.at[len(loads)]
+                )
+            )
+            loads[-1].start()
+            row += rows
+        facts.append((ref, rows))
         at += count
 
     sub = lax.broadcasted_iota(jnp.int32, (8, LANES), 0)
@@ -180,12 +186,11 @@
     owner = owner.astype(jnp.int32)
     mine = (owner >= first_owner) & (owner < first_owner + CORES)
     ones = jnp.where(mine, 1.0, 0.0)
-    rank = ones
-    shift = 1
-    while shift < LANES:
-        rank = rank + jnp.where(lane >= shift, pltpu.roll(rank, shift, 1), 0.0)
-        shift *= 2
-    rank = jnp.where(mine, rank - 1.0, -1.0)
+    tri_row = lax.broadcasted_iota(jnp.int32, (LANES, LANES), 0)
+    tri_lane = lax.broadcasted_iota(jnp.int32, (LANES, LANES), 1)
+    before = jnp.where(tri_row < tri_lane, 1.0, 0.0).astype(jnp.bfloat16)
+    rank = jnp.dot(ones.astype(jnp.bfloat16), before, preferred_element_type=jnp.float32)
+    rank = jnp.where(mine, rank, -1.0)
     tile = local_id + jnp.where(owner == me, 0.0, float(per_owner))
     wanted = jnp.where(lane == slots, jnp.sum(ones, axis=1, keepdims=True), 0.0)
     for s in range(slots):
@@ -195,28 +200,40 @@
     to_scalar = pltpu.make_async_copy(plan_v, plan, sem)
     to_scalar.start()
     to_scalar.wait()
+    for load in loads:
+        load.wait()
 
     slot_row = lax.broadcasted_iota(jnp.int32, (slots, LANES), 0)
     slot_lane = lax.broadcasted_iota(jnp.int32, (slots, LANES), 1)
-    for b in range(blocks):
+    most = slots // GROUP
+    least = max(1, most // 2)
+
+    def score_block(b, carry):
         count = plan[b, slots]
-
-        def score_group(g, carry, b=b):
-            left = jnp.concatenate([tiles[plan[b, g * GROUP + t]] for t in range(GROUP)], axis=0)
-            start = pl.multiple_of(g * (8 * GROUP), 8 * GROUP)
-            for c in range(0, len(chunks[b]), 2):
-                pair = [ref[r : r + LANES, :] for ref, r in chunks[b][c : c + 2]]
+        groups = pl.cdiv(count, GROUP)
+
+        def score_groups(number):
+            rows = number * GROUP * 8
+
+            def columns(c, carry):
+                left = jnp.concatenate([tiles[plan[b, t]] for t in range(number * GROUP)], axis=0)
+                at = pl.multiple_of(c * (2 * LANES), 2 * LANES)
+                pair = [weights[b, pl.ds(at + k * LANES, LANES), :] for k in range(2)]
                 similar = jnp.dot(
                     left, jnp.concatenate(pair, axis=1), preferred_element_type=jnp.float32
                 )
-                width = similar.shape[1]
-                rows = jnp.max(similar.reshape(GROUP, tile_rows // 8, 8, width), axis=1)
-                rows = rows.reshape(8 * GROUP, width)
-                for k in range(width // LANES):
-                    nearest[c + k, pl.ds(start, 8 * GROUP), :] = rows[:, k * LANES : (k + 1) * LANES]
-            return carry
-
-        lax.fori_loop(0, pl.cdiv(count, GROUP), score_group, 0)
+                best = jnp.max(similar.reshape(number * GROUP, tile_rows // 8, 8, 2 * LANES), axis=1)
+                best = best.reshape(rows, 2 * LANES)
+                for k in range(2):
+                    nearest[2 * c + k, 0:rows, :] = best[:, k * LANES : (k + 1) * LANES]
+                return carry
+
+            lax.fori_loop(0, weights.shape[1] // (2 * LANES), columns, 0)
+
+        for number in range(least, most + 1):
+            wanted_now = (groups <= number) if number == least else (groups == number)
+            pl.when(wanted_now)(functools.partial(score_groups, number))
+
         total = jnp.zeros((slots, LANES), jnp.float32)
         for k in range(nearest.shape[0]):
             x = nearest[k, pl.ds(0, slots, stride=8), :]
@@ -229,26 +246,38 @@
             if k:
                 x = pltpu.roll(x, k, 1)
             total = jnp.where(slot_lane % query_tok == k, x, total)
-        outs[b][...] = jnp.where(slot_row < count, total / float(query_tok), 0.0)
-
-
-def score(held, slots, query_tok, tiles):
+        offset = offsets[-1]
+        for k in range(blocks - 1):
+            offset = jnp.where(b == k, offsets[k], offset)
+        place = my_place - offset
+        place = jnp.where(place < 0, place + chips, place)
+        out[place] = jnp.where(slot_row < count, total / float(query_tok), 0.0)
+        return carry
+
+    lax.fori_loop(0, blocks, score_block, 0)
+
+
+def score(held, offsets, slots, query_tok, chips, tiles, earlier):
     pieces = tuple(len(arrays) for arrays in held)
     flat = [x for arrays in held for x in arrays]
     blocks = len(pieces)
     _, tile_rows, feature = tiles.shape
     query_rows = sum(x.shape[0] for x in held[0]) - FACT_ROWS
     flops = 2 * blocks * slots * tile_rows * feature * query_rows
+    kept = [] if earlier is None else [earlier]
     return pl.pallas_call(
-        functools.partial(score_kernel, pieces, slots, query_tok),
-        out_shape=(jax.ShapeDtypeStruct((slots, LANES), jnp.float32),) * blocks,
-        in_specs=[pl.BlockSpec(memory_space=pltpu.VMEM)] * (1 + len(flat)),
-        out_specs=(pl.BlockSpec(memory_space=pltpu.VMEM),) * blocks,
+        functools.partial(score_kernel, pieces, offsets, slots, query_tok, len(kept)),
+        out_shape=jax.ShapeDtypeStruct((chips, slots, LANES), jnp.float32),
+        in_specs=[pl.BlockSpec(memory_space=pltpu.VMEM)] * (1 + len(flat) + len(kept)),
+        out_specs=pl.BlockSpec(memory_space=pltpu.VMEM),
+        input_output_aliases={1 + len(flat): 0} if kept else {},
         scratch_shapes=[
+            pltpu.VMEM((blocks, query_rows, feature), tiles.dtype),
             pltpu.VMEM((query_rows // LANES, 8 * slots, LANES), jnp.float32),
             pltpu.VMEM((8, LANES), jnp.int32),
             pltpu.SMEM((8, LANES), jnp.int32),
             pltpu.SemaphoreType.DMA,
+            pltpu.SemaphoreType.DMA((len(flat),)),
         ],
         compiler_params=pltpu.CompilerParams(vmem_limit_bytes=VMEM_LIMIT),
         cost_estimate=pl.CostEstimate(
@@ -257,7 +286,7 @@
             transcendentals=0,
         ),
         name="score",
-    )(tiles, *flat)
+    )(tiles, *flat, *kept)
 
 
 def sort_descending(parts, lanes):
@@ -300,18 +329,14 @@
     return parts
 
 
-def finish_kernel(arrays, per_device, query_tok, topk, slot_of, *refs):
-    returned = refs[:arrays]
-    scores, best_scores, spread, ranked, rows = refs[arrays:]
+def finish_kernel(per_device, query_tok, topk, slot_of, returned, scores, best_scores, ranked, rows):
     number = slot_of.shape[0]
-    step = returned[0].shape[0]
-    for at, ref in enumerate(returned):
-        spread[at * step : (at + 1) * step, :] = ref[...]
+    spread = returned[...].reshape(returned.shape[0] * returned.shape[1], LANES)
     total = spread.shape[0]
     lane = lax.broadcasted_iota(jnp.int32, (number, total), 1)
     choose = (slot_of[:, 0:1] == lane).astype(jnp.float32).astype(jnp.bfloat16)
     by_candidate = jnp.zeros((number, LANES), jnp.float32)
-    for part in split_exact(spread[...]):
+    for part in split_exact(spread):
         by_candidate += jnp.dot(choose, part, preferred_element_type=jnp.float32)
 
     def in_order(x):
@@ -331,23 +356,21 @@
 
 def finish(per_device, query_tok, slot_of, returned):
     number = slot_of.shape[0]
-    total = sum(r.shape[0] for r in returned)
     return pl.pallas_call(
-        functools.partial(finish_kernel, len(returned), per_device, query_tok, TOPK),
+        functools.partial(finish_kernel, per_device, query_tok, TOPK),
         out_shape=(
             jax.ShapeDtypeStruct((per_device, number), jnp.float32),
             jax.ShapeDtypeStruct((per_device, TOPK), jnp.float32),
         ),
-        in_specs=[pl.BlockSpec(memory_space=pltpu.VMEM)] * (1 + len(returned)),
+        in_specs=[pl.BlockSpec(memory_space=pltpu.VMEM)] * 2,
         out_specs=(pl.BlockSpec(memory_space=pltpu.VMEM),) * 2,
         scratch_shapes=[
-            pltpu.VMEM((total, LANES), jnp.float32),
             pltpu.VMEM((number, LANES), jnp.float32),
             pltpu.VMEM((LANES, number), jnp.float32),
         ],
         compiler_params=pltpu.CompilerParams(vmem_limit_bytes=VMEM_LIMIT),
         name="finish",
-    )(slot_of, *returned)
+    )(slot_of, returned)
 
 
 def local(queries, passages, lengths, candidates):
@@ -389,23 +412,24 @@
             ]
 
     send_on(1)
-    back = {}
+    fresh = None
     for step in range(1, middle + 1):
         if step < middle:
             send_on(step + 1)
         offsets = (0, 1, -1) if step == 1 else (middle,) if step == middle else (step, -step)
-        fresh = score([arrived[offset] for offset in offsets], slots, query_tok, tiles)
+        fresh = score(
+            [arrived[offset] for offset in offsets], tuple(offset % chips for offset in offsets),
+            slots, query_tok, chips, tiles, fresh,
+        )
         if step < middle:
             names = [step + 1, -step - 1] if step + 1 < middle else [middle]
-            earlier = [(1 - step) % chips, (step - 1) % chips] if step > 1 else []
-            held, fresh, came = lax.optimization_barrier(
-                ([arrived[name] for name in names], fresh, [back[j] for j in earlier])
-            )
+            held, fresh = lax.optimization_barrier(([arrived[name] for name in names], fresh))
             arrived.update(zip(names, held))
-            back.update(zip(earlier, came))
-        for offset, result in zip(offsets, fresh):
-            back[offset % chips] = moved(result, -offset) if offset else result
-    return finish(per_device, query_tok, slot_of, [back[j] for j in range(chips)])
+    by_place = [[order[i] * CORES + k for i in range(chips)] for k in range(CORES)]
+    returned = lax.all_to_all(
+        fresh, "corpus", split_axis=0, concat_axis=0, tiled=True, axis_index_groups=by_place
+    )
+    return finish(per_device, query_tok, slot_of, returned)
 
 
 def solution(mesh):

time: 80.1 us -> 78.6 us (0.981)
  the two profiles are of different devices: /device:TPU:2 before, /device:TPU:0 now
where the time goes in v4:
time: 78.6 us
  Pallas kernels  40.8 us (52%)
  blocking collectives  15.5 us (20%)
  starting transfers between devices  10.4 us (13%)
  waiting for transfers between devices  7.65 us (10%)
  local copies, waits for them, and re-layouts  3.53 us (4%)
    pallas_call x4, Pallas kernels, score(): pl.pallas_call(functools.partial(score_kernel, pieces, offsets, slots, qu...  33.8 us
    all_to_all x1, blocking collectives, local(): lax.all_to_all(fresh, 'corpus', split_axis=0, concat_axis=0, tiled=True,...  15.5 us
    ppermute x8, starting transfers between devices, moved(): return lax.ppermute(x, 'corpus', pairs)  9.64 us
    ppermute x8, waiting for transfers between devices, moved(): return lax.ppermute(x, 'corpus', pairs)  7.64 us
    unnamed x8, local copies, waits for them, and re-layouts  3.5 us
    pallas_call x1, Pallas kernels, ready(): pl.pallas_call(functools.partial(ready_kernel, chips, slots, parts), out_...  2.27 us
    pallas_call x1, Pallas kernels, pack(): pl.pallas_call(functools.partial(pack_kernel, per_owner), out_shape=jax.S...  1.98 us
    pallas_call x1, Pallas kernels, join(): pl.pallas_call(join_kernel, out_shape=jax.ShapeDtypeStruct(filled.shape,...  1.64 us
  transfers between devices with their start and end apart: 10, of which 3 were waited for; matrix products, arithmetic and copies ran while one was open for 0% of the time, Pallas kernels for 45%

profile of v4, /device:TPU:0, one launch (start us, length us, event | category | flops | bytes accessed | tf_op | source)
XLA Modules:
  0.0 78.6 jit_solution(17823433184058503050)
XLA Ops:
  0.6 0.5 collective-permute-start.1
  1.1 2.0 %pack.1.refs_1_ = bf16[1808,128]{1,0:T(8,128)(2,1)} custom-call(bf16[1792,128]{1,0:T(8,128)(2,1)} %bitcast.1, s32[1,128]{1,0:T(1,128)} %candidates_in.1), custom_call_target="tpu_custom_call" | custom-call | tf_op jit(solution)/shard_map/pack/pallas_call | solution.py:54
  3.1 2.6 %collective-permute-start.2 = (bf16[1808,128]{1,0:T(8,128)(2,1)}, bf16[1808,128]{1,0:T(8,128)(2,1)S(1)}, u32[]{:S(2)}, u32[]{:S(2)}) collective-permute-start(bf16[1808,128]{1,0:T(8,128)(2,1)} %pack.1.refs_1_), channel_id=1, source_target_pairs={{0,4},{1,5},{4,8},{5,9},{8,12},{9,13},{12,14},{13,15},{14,10},{15,... | collective-permute-start | bytes 1388552 | tf_op jit(solution)/shard_map/ppermute | solution.py:392
  5.8 0.0 collective-permute-start.4
  5.8 0.2 collective-permute-start
  6.0 0.0 copy-start
  6.0 2.2 %copy-done = bf16[128,128,128]{2,1,0:T(8,128)(2,1)S(1)} copy-done((bf16[128,128,128]{2,1,0:T(8,128)(2,1)S(1)}, bf16[128,128,128]{2,1,0:T(8,128)(2,1)}, u32[]{:S(2)}) %copy-start) | copy-done | bytes 4194328
  8.2 0.0 copy-start.2
  8.2 0.7 copy-done.2
  8.8 0.0 copy-start.3
  8.8 0.7 copy-done.3
  9.5 2.3 %ready.1 = (s32[128,128]{1,0:T(8,128)S(1)}, bf16[256,128,128]{2,1,0:T(8,128)(2,1)S(1)}) custom-call(s32[128]{0:T(128)S(1)} %copy-done.3, s32[1,128]{1,0:T(1,128)S(1)} %copy-done.2, bf16[128,128,128]{2,1,0:T(8,128)(2,1)S(1)} %copy-done), custom_call_target="tpu_custom_call" | custom-call | tf_op jit(solution)/shard_map/ready/pallas_call | solution.py:111
  11.8 5.4 %collective-permute-done.2.refs_2_ = bf16[1808,128]{1,0:T(8,128)(2,1)S(1)} collective-permute-done((bf16[1808,128]{1,0:T(8,128)(2,1)}, bf16[1808,128]{1,0:T(8,128)(2,1)S(1)}, u32[]{:S(2)}, u32[]{:S(2)}) %collective-permute-start.2) | collective-permute-done | bytes 462880 | tf_op jit(solution)/shard_map/ppermute | solution.py:392
  17.2 1.8 %collective-permute-start.3 = (bf16[1808,128]{1,0:T(8,128)(2,1)S(1)}, bf16[1808,128]{1,0:T(8,128)(2,1)S(1)}, u32[]{:S(2)}, u32[]{:S(2)}) collective-permute-start(bf16[1808,128]{1,0:T(8,128)(2,1)S(1)} %collective-permute-done.2.refs_2_), channel_id=1, source_target_pairs={{0,4},{1,5},{4,8},{5,9},{8,12},{9,13},{12,14},{13,15},{14,10},{15,... | collective-permute-start | bytes 1388552 | tf_op jit(solution)/shard_map/ppermute | solution.py:392
  19.0 0.0 collective-permute-done.4.refs_3_
  19.0 0.2 collective-permute-start.5
  19.2 0.0 collective-permute-done.lens
  19.2 0.0 collective-permute-done.1.other
  19.2 0.0 copy-start.1
  19.2 1.6 %join.1.refs_0_ = bf16[256,128,128]{2,1,0:T(8,128)(2,1)S(1)} custom-call(s32[128]{0:T(128)S(1)} %collective-permute-done.lens, bf16[128,128,128]{2,1,0:T(8,128)(2,1)S(1)} %collective-permute-done.1.other, bf16[256,128,128]{2,1,0:T(8,128)(2,1)S(1)} %get-tuple-element.14.held), custom_call_target="tpu_custom_call", output_to_operand_aliasing={{}: (2, {})} | custom-call | tf_op jit(solution)/shard_map/join/pallas_call | solution.py:134
  20.9 0.0 copy-done.1
  20.9 12.8 %score.4.refs_3_ = f32[8,24,128]{2,1,0:T(8,128)S(1)} custom-call(bf16[256,128,128]{2,1,0:T(8,128)(2,1)S(1)} %join.1.refs_0_, bf16[1808,128]{1,0:T(8,128)(2,1)S(1)} %copy-done.1, bf16[1808,128]{1,0:T(8,128)(2,1)S(1)} %collective-permute-done.2.refs_2_, bf16[1808,128]{1,0:T(8,128)(2,1)S(1)} %collective-permute-done.4.refs_3_), custom_call_target="tpu_custom_call" | custom-call | flops 12683575296 | bytes 3735552 | tf_op jit(solution)/shard_map/score/pallas_call | solution.py:268
  33.7 0.0 collective-permute-done.3.refs_1_
  33.7 0.0 collective-permute-done.5.refs_2_
  33.7 0.9 %collective-permute-start.6 = (bf16[1808,128]{1,0:T(8,128)(2,1)S(1)}, bf16[1808,128]{1,0:T(8,128)(2,1)S(1)}, u32[]{:S(2)}, u32[]{:S(2)}) collective-permute-start(bf16[1808,128]{1,0:T(8,128)(2,1)S(1)} %collective-permute-done.3.refs_1_), channel_id=1, source_target_pairs={{0,4},{1,5},{4,8},{5,9},{8,12},{9,13},{12,14},{13,15},{14,10},{15,... | collective-permute-start | bytes 1388552 | tf_op jit(solution)/shard_map/ppermute | solution.py:392
  34.6 1.9 %collective-permute-start.7 = (bf16[1808,128]{1,0:T(8,128)(2,1)S(1)}, bf16[1808,128]{1,0:T(8,128)(2,1)S(1)}, u32[]{:S(2)}, u32[]{:S(2)}) collective-permute-start(bf16[1808,128]{1,0:T(8,128)(2,1)S(1)} %collective-permute-done.5.refs_2_), channel_id=1, source_target_pairs={{0,2},{1,3},{4,0},{5,1},{8,4},{9,5},{12,8},{13,9},{14,12},{15,13},... | collective-permute-start | bytes 1388552 | tf_op jit(solution)/shard_map/ppermute | solution.py:392
  36.5 8.0 %score.5.refs_3_ = f32[8,24,128]{2,1,0:T(8,128)S(1)} custom-call(bf16[256,128,128]{2,1,0:T(8,128)(2,1)S(1)} %join.1.refs_0_, bf16[1808,128]{1,0:T(8,128)(2,1)S(1)} %collective-permute-done.3.refs_1_, bf16[1808,128]{1,0:T(8,128)(2,1)S(1)} %collective-permute-done.5.refs_2_, f32[8,24,128]{2,1,0:T(8,128)S(1)} %score.4.refs_3_), custom_call_target="tpu_custom_call", output_to_operand_aliasing={{}: (3, {})} | custom-call | flops 8455716864 | bytes 2490368 | tf_op jit(solution)/shard_map/score/pallas_call | solution.py:268
  44.6 0.9 %collective-permute-done.6.refs_1_ = bf16[1808,128]{1,0:T(8,128)(2,1)S(1)} collective-permute-done((bf16[1808,128]{1,0:T(8,128)(2,1)S(1)}, bf16[1808,128]{1,0:T(8,128)(2,1)S(1)}, u32[]{:S(2)}, u32[]{:S(2)}) %collective-permute-start.6) | collective-permute-done | bytes 462880 | tf_op jit(solution)/shard_map/ppermute | solution.py:392
  45.4 1.4 %collective-permute-done.7.refs_2_ = bf16[1808,128]{1,0:T(8,128)(2,1)S(1)} collective-permute-done((bf16[1808,128]{1,0:T(8,128)(2,1)S(1)}, bf16[1808,128]{1,0:T(8,128)(2,1)S(1)}, u32[]{:S(2)}, u32[]{:S(2)}) %collective-permute-start.7) | collective-permute-done | bytes 462880 | tf_op jit(solution)/shard_map/ppermute | solution.py:392
  46.8 1.8 %collective-permute-start.8 = (bf16[896,128]{1,0:T(8,128)(2,1)S(1)}, bf16[896,128]{1,0:T(8,128)(2,1)S(1)}, u32[]{:S(2)}, u32[]{:S(2)}) collective-permute-start(bf16[896,128]{1,0:T(8,128)(2,1)S(1)} %slice.6), channel_id=1, source_target_pairs={{0,4},{1,5},{4,8},{5,9},{8,12},{9,13},{12,14},{13,15},{14,10},{15,... | collective-permute-start | bytes 688136 | tf_op jit(solution)/shard_map/ppermute | solution.py:392
  48.6 0.3 collective-permute-start.9
  49.0 8.5 %score.6.refs_3_ = f32[8,24,128]{2,1,0:T(8,128)S(1)} custom-call(bf16[256,128,128]{2,1,0:T(8,128)(2,1)S(1)} %join.1.refs_0_, bf16[1808,128]{1,0:T(8,128)(2,1)S(1)} %collective-permute-done.6.refs_1_, bf16[1808,128]{1,0:T(8,128)(2,1)S(1)} %collective-permute-done.7.refs_2_, f32[8,24,128]{2,1,0:T(8,128)S(1)} %score.5.refs_3_), custom_call_target="tpu_custom_call", output_to_operand_aliasing={{}: (3, {})} | custom-call | flops 8455716864 | bytes 2490368 | tf_op jit(solution)/shard_map/score/pallas_call | solution.py:268
  57.4 0.0 collective-permute-done.8.refs_1_
  57.4 0.0 collective-permute-done.9.refs_2_
  57.5 4.5 %score.7 = f32[8,24,128]{2,1,0:T(8,128)S(1)} custom-call(bf16[256,128,128]{2,1,0:T(8,128)(2,1)S(1)} %join.1.refs_0_, bf16[896,128]{1,0:T(8,128)(2,1)S(1)} %collective-permute-done.8.refs_1_, bf16[912,128]{1,0:T(8,128)(2,1)S(1)} %collective-permute-done.9.refs_2_, f32[8,24,128]{2,1,0:T(8,128)S(1)} %score.6.refs_3_), custom_call_target="tpu_custom_call", output_to_operand_aliasing={{}: (3, {})} | custom-call | flops 4227858432 | bytes 1245184 | tf_op jit(solution)/shard_map/score/pallas_call | solution.py:268
  62.0 15.5 %all_to_all.5.returned = f32[8,24,128]{2,1,0:T(8,128)S(1)} all-to-all(f32[8,24,128]{2,1,0:T(8,128)S(1)} %score.7), channel_id=1, replica_groups={{0,4,8,12,14,10,6,2},{1,5,9,13,15,11,7,3},{16,20,24,28,30,26,22,18},{17..., dimensions={0} | all-to-all | bytes 196608 | tf_op jit(solution)/shard_map/all_to_all | solution.py:429
  77.5 1.1 %finish.1 = (f32[56,128]{1,0:T(8,128)}, f32[56,100]{1,0:T(8,128)}) custom-call(s32[128,128]{1,0:T(8,128)S(1)} %get-tuple-element.13.slot_of, f32[8,24,128]{2,1,0:T(8,128)S(1)} %all_to_all.5.returned), custom_call_target="tpu_custom_call" | custom-call | tf_op jit(solution)/shard_map/finish/pallas_call | solution.py:359
  (2 shorter events, 0.0 us)
Async XLA Ops:
  0.6 18.6 %collective-permute-start.1 = (bf16[128,128,128]{2,1,0:T(8,128)(2,1)}, bf16[128,128,128]{2,1,0:T(8,128)(2,1)S(1)}, u32[]{:S(2)}, u32[]{:S(2)}) collective-permute-start(bf16[128,128,128]{2,1,0:T(8,128)(2,1)} %passages.1), channel_id=1, source_target_pairs={{0,1},{1,0},{2,3},{3,2},{4,5},{5,4},{6,7},{7,6},{8,9},{9,8},{10,11... | collective-permute-start | bytes 12582920 | tf_op jit(solution)/shard_map/ppermute | solution.py:395
  3.1 14.1 %collective-permute-start.2 = (bf16[1808,128]{1,0:T(8,128)(2,1)}, bf16[1808,128]{1,0:T(8,128)(2,1)S(1)}, u32[]{:S(2)}, u32[]{:S(2)}) collective-permute-start(bf16[1808,128]{1,0:T(8,128)(2,1)} %pack.1.refs_1_), channel_id=1, source_target_pairs={{0,4},{1,5},{4,8},{5,9},{8,12},{9,13},{12,14},{13,15},{14,10},{15,... | collective-permute-start | bytes 1388552 | tf_op jit(solution)/shard_map/ppermute | solution.py:392
  5.8 13.2 %collective-permute-start.4 = (bf16[1808,128]{1,0:T(8,128)(2,1)}, bf16[1808,128]{1,0:T(8,128)(2,1)S(1)}, u32[]{:S(2)}, u32[]{:S(2)}) collective-permute-start(bf16[1808,128]{1,0:T(8,128)(2,1)} %pack.1.refs_1_), channel_id=1, source_target_pairs={{0,2},{1,3},{4,0},{5,1},{8,4},{9,5},{12,8},{13,9},{14,12},{15,13},... | collective-permute-start | bytes 1388552 | tf_op jit(solution)/shard_map/ppermute | solution.py:392
  5.8 13.4 %collective-permute-start = (s32[128]{0:T(128)}, s32[128]{0:T(128)S(1)}, u32[]{:S(2)}, u32[]{:S(2)}) collective-permute-start(s32[128]{0:T(128)} %lens.1), channel_id=1, source_target_pairs={{0,1},{1,0},{2,3},{3,2},{4,5},{5,4},{6,7},{7,6},{8,9},{9,8},{10,11... | collective-permute-start | bytes 1544 | tf_op jit(solution)/shard_map/ppermute | solution.py:396
  6.0 2.2 %copy-start = (bf16[128,128,128]{2,1,0:T(8,128)(2,1)S(1)}, bf16[128,128,128]{2,1,0:T(8,128)(2,1)}, u32[]{:S(2)}) copy-start(bf16[128,128,128]{2,1,0:T(8,128)(2,1)} %passages.1) | copy-start | bytes 12582916
  8.2 0.7 copy-start.2
  8.8 0.7 copy-start.3
  17.2 16.5 %collective-permute-start.3 = (bf16[1808,128]{1,0:T(8,128)(2,1)S(1)}, bf16[1808,128]{1,0:T(8,128)(2,1)S(1)}, u32[]{:S(2)}, u32[]{:S(2)}) collective-permute-start(bf16[1808,128]{1,0:T(8,128)(2,1)S(1)} %collective-permute-done.2.refs_2_), channel_id=1, source_target_pairs={{0,4},{1,5},{4,8},{5,9},{8,12},{9,13},{12,14},{13,15},{14,10},{15,... | collective-permute-start | bytes 1388552 | tf_op jit(solution)/shard_map/ppermute | solution.py:392
  19.0 14.7 %collective-permute-start.5 = (bf16[1808,128]{1,0:T(8,128)(2,1)S(1)}, bf16[1808,128]{1,0:T(8,128)(2,1)S(1)}, u32[]{:S(2)}, u32[]{:S(2)}) collective-permute-start(bf16[1808,128]{1,0:T(8,128)(2,1)S(1)} %collective-permute-done.4.refs_3_), channel_id=1, source_target_pairs={{0,2},{1,3},{4,0},{5,1},{8,4},{9,5},{12,8},{13,9},{14,12},{15,13},... | collective-permute-start | bytes 1388552 | tf_op jit(solution)/shard_map/ppermute | solution.py:392
  19.2 1.7 %copy-start.1 = (bf16[1808,128]{1,0:T(8,128)(2,1)S(1)}, bf16[1808,128]{1,0:T(8,128)(2,1)}, u32[]{:S(2)}) copy-start(bf16[1808,128]{1,0:T(8,128)(2,1)} %pack.1.refs_1_) | copy-start | bytes 1388548
  33.7 11.7 %collective-permute-start.6 = (bf16[1808,128]{1,0:T(8,128)(2,1)S(1)}, bf16[1808,128]{1,0:T(8,128)(2,1)S(1)}, u32[]{:S(2)}, u32[]{:S(2)}) collective-permute-start(bf16[1808,128]{1,0:T(8,128)(2,1)S(1)} %collective-permute-done.3.refs_1_), channel_id=1, source_target_pairs={{0,4},{1,5},{4,8},{5,9},{8,12},{9,13},{12,14},{13,15},{14,10},{15,... | collective-permute-start | bytes 1388552 | tf_op jit(solution)/shard_map/ppermute | solution.py:392
  34.6 12.2 %collective-permute-start.7 = (bf16[1808,128]{1,0:T(8,128)(2,1)S(1)}, bf16[1808,128]{1,0:T(8,128)(2,1)S(1)}, u32[]{:S(2)}, u32[]{:S(2)}) collective-permute-start(bf16[1808,128]{1,0:T(8,128)(2,1)S(1)} %collective-permute-done.5.refs_2_), channel_id=1, source_target_pairs={{0,2},{1,3},{4,0},{5,1},{8,4},{9,5},{12,8},{13,9},{14,12},{15,13},... | collective-permute-start | bytes 1388552 | tf_op jit(solution)/shard_map/ppermute | solution.py:392
  46.8 10.6 %collective-permute-start.8 = (bf16[896,128]{1,0:T(8,128)(2,1)S(1)}, bf16[896,128]{1,0:T(8,128)(2,1)S(1)}, u32[]{:S(2)}, u32[]{:S(2)}) collective-permute-start(bf16[896,128]{1,0:T(8,128)(2,1)S(1)} %slice.6), channel_id=1, source_target_pairs={{0,4},{1,5},{4,8},{5,9},{8,12},{9,13},{12,14},{13,15},{14,10},{15,... | collective-permute-start | bytes 688136 | tf_op jit(solution)/shard_map/ppermute | solution.py:392
  48.6 8.8 %collective-permute-start.9 = (bf16[912,128]{1,0:T(8,128)(2,1)S(1)}, bf16[912,128]{1,0:T(8,128)(2,1)S(1)}, u32[]{:S(2)}, u32[]{:S(2)}) collective-permute-start(bf16[912,128]{1,0:T(8,128)(2,1)S(1)} %slice.7), channel_id=1, source_target_pairs={{0,2},{1,3},{4,0},{5,1},{8,4},{9,5},{12,8},{13,9},{14,12},{15,13},... | collective-permute-start | bytes 700424 | tf_op jit(solution)/shard_map/ppermute | solution.py:392

commit v5 on v3

--- a/solution.py
+++ b/solution.py
@@ -10,8 +10,7 @@
 TOPK = 100
 CORES = 2
 LANES = 128
-FACT_ROWS = 16
-GROUP = 4
+GROUP = 8
 VMEM_LIMIT = 32 * 1024 * 1024
 
 
@@ -31,7 +30,7 @@
     return high, middle, low
 
 
-def pack_kernel(per_owner, queries_in, candidates_in, block, queries, candidates, sems):
+def pack_kernel(per_owner, chips, slots, queries_in, candidates_in, block, queries, candidates, sems):
     loads = [
         pltpu.make_async_copy(queries_in, queries, sems.at[0]),
         pltpu.make_async_copy(candidates_in, candidates, sems.at[1]),
@@ -43,17 +42,39 @@
     query_rows = queries.shape[0]
     for at in range(0, query_rows, LANES):
         block[at : at + LANES, :] = queries[at : at + LANES, :].T
-    ids = jnp.broadcast_to(candidates[...], (FACT_ROWS, candidates.shape[1]))
+    fact_rows = block.shape[0] - query_rows
+    number = candidates.shape[1]
+    per_chip = CORES * per_owner
+    ids = jnp.broadcast_to(candidates[...], (fact_rows, number))
     row = lax.broadcasted_iota(jnp.int32, ids.shape, 0)
-    facts = jnp.where(row == 0, ids // per_owner, jnp.where(row == 1, ids % per_owner, 0))
-    block[query_rows:, :] = facts.astype(jnp.float32).astype(jnp.bfloat16)
-
-
-def pack(queries, candidates, per_owner):
+    lane = lax.broadcasted_iota(jnp.int32, ids.shape, 1)
+    chosen = ring_place(ids // per_chip, chips) == row
+    ones = jnp.where(chosen, 1.0, 0.0)
+    before = jnp.where(
+        lax.broadcasted_iota(jnp.int32, (number, number), 0)
+        < lax.broadcasted_iota(jnp.int32, (number, number), 1), 1.0, 0.0,
+    )
+    rank = jnp.dot(
+        ones.astype(jnp.bfloat16), before.astype(jnp.bfloat16), preferred_element_type=jnp.float32
+    )
+    rank = jnp.where(chosen, rank, -1.0)
+    tile = (ids % per_chip).astype(jnp.float32)
+    wanted = jnp.where(lane == slots, jnp.sum(ones, axis=1, keepdims=True), 0.0)
+    for s in range(slots):
+        found = jnp.sum(jnp.where(rank == float(s), tile, 0.0), axis=1, keepdims=True)
+        wanted = jnp.where(lane == s, found, wanted)
+    block[query_rows:, :] = wanted.astype(jnp.bfloat16)
+
+
+def fact_rows_of(chips):
+    return -(-chips // 16) * 16
+
+
+def pack(queries, candidates, per_owner, chips, slots):
     rows, feature = queries.shape
     return pl.pallas_call(
-        functools.partial(pack_kernel, per_owner),
-        out_shape=jax.ShapeDtypeStruct((rows + FACT_ROWS, feature), queries.dtype),
+        functools.partial(pack_kernel, per_owner, chips, slots),
+        out_shape=jax.ShapeDtypeStruct((rows + fact_rows_of(chips), feature), queries.dtype),
         in_specs=[pl.BlockSpec(memory_space=pl.ANY)] * 2,
         out_specs=pl.BlockSpec(memory_space=pltpu.VMEM),
         scratch_shapes=[
@@ -83,9 +104,10 @@
 def ready_kernel(chips, slots, parts, lens, candidates, passages, slot_of, filled, sems):
     per_owner = passages.shape[0]
     size = per_owner // parts
+    base = lax.axis_index("corpus") % CORES * per_owner
     loads = [
         pltpu.make_async_copy(
-            passages.at[pl.ds(i * size, size)], filled.at[pl.ds(i * size, size)], sems.at[i]
+            passages.at[pl.ds(i * size, size)], filled.at[pl.ds(base + i * size, size)], sems.at[i]
         )
         for i in range(parts)
     ]
@@ -104,7 +126,7 @@
     slot_of[...] = ahead * slots + rank
     for i, load in enumerate(loads):
         load.wait()
-        fill_tiles(filled, 0, lens, filled, 0, i * size, size)
+        fill_tiles(filled, base, lens, filled, base, i * size, size)
 
 
 def ready(lengths, candidates, passages, chips, slots):
@@ -130,7 +152,9 @@
 
 
 def join_kernel(lens, other, held, filled):
-    fill_tiles(other, 0, lens, filled, other.shape[0], 0, other.shape[0])
+    per_owner = other.shape[0]
+    base = (1 - lax.axis_index("corpus") % CORES) * per_owner
+    fill_tiles(other, 0, lens, filled, base, 0, per_owner)
 
 
 def join(lengths, other, filled):
@@ -149,74 +173,73 @@
     )(lengths, other, filled)
 
 
-def score_kernel(pieces, slots, query_tok, *refs):
+def score_kernel(pieces, slots, query_tok, chips, *refs):
     blocks = len(pieces)
     arrays = sum(pieces)
     tiles = refs[0]
     held = refs[1 : 1 + arrays]
     outs = refs[1 + arrays : 1 + arrays + blocks]
-    nearest, plan_v, plan, sem = refs[1 + arrays + blocks :]
-    per_chip, tile_rows, feature = tiles.shape
-    per_owner = per_chip // CORES
-    me = lax.axis_index("corpus")
-    first_owner = me // CORES * CORES
-
-    chunks, facts = [], []
+    weights, nearest, plan_v, plan, sem, weight_sems = refs[1 + arrays + blocks :]
+    tile_rows = tiles.shape[1]
+    my_place = ring_place(lax.axis_index("corpus") // CORES, chips)
+    fact_rows = fact_rows_of(chips)
+
+    loads = []
+    fact_row = lax.broadcasted_iota(jnp.int32, (fact_rows, LANES), 0)
     at = 0
-    for count in pieces:
-        where = [(ref, r) for ref in held[at : at + count] for r in range(0, ref.shape[0], LANES)]
-        facts.append(where[-1])
-        chunks.append(where[:-1])
+    for b, count in enumerate(pieces):
+        row = 0
+        for ref in held[at : at + count]:
+            rows = min(ref.shape[0], weights.shape[1] - row)
+            loads.append(
+                pltpu.make_async_copy(
+                    ref.at[pl.ds(0, rows)], weights.at[b, pl.ds(row, rows)], weight_sems.at[len(loads)]
+                )
+            )
+            row += rows
+        fact = ref[rows : rows + fact_rows, :].astype(jnp.float32)
+        fact = jnp.sum(jnp.where(fact_row == my_place, fact, 0.0), axis=0, keepdims=True)
+        plan_v[b : b + 1, :] = fact.astype(jnp.int32)
         at += count
-
-    sub = lax.broadcasted_iota(jnp.int32, (8, LANES), 0)
-    lane = lax.broadcasted_iota(jnp.int32, (8, LANES), 1)
-    owner = jnp.full((8, LANES), -1.0, jnp.float32)
-    local_id = jnp.zeros((8, LANES), jnp.float32)
-    for b, (ref, r) in enumerate(facts):
-        fact = ref[r : r + FACT_ROWS, :].astype(jnp.float32)
-        owner = jnp.where(sub == b, fact[0:1, :], owner)
-        local_id = jnp.where(sub == b, fact[1:2, :], local_id)
-    owner = owner.astype(jnp.int32)
-    mine = (owner >= first_owner) & (owner < first_owner + CORES)
-    ones = jnp.where(mine, 1.0, 0.0)
-    rank = ones
-    shift = 1
-    while shift < LANES:
-        rank = rank + jnp.where(lane >= shift, pltpu.roll(rank, shift, 1), 0.0)
-        shift *= 2
-    rank = jnp.where(mine, rank - 1.0, -1.0)
-    tile = local_id + jnp.where(owner == me, 0.0, float(per_owner))
-    wanted = jnp.where(lane == slots, jnp.sum(ones, axis=1, keepdims=True), 0.0)
-    for s in range(slots):
-        found = jnp.sum(jnp.where(rank == float(s), tile, 0.0), axis=1, keepdims=True)
-        wanted = jnp.where(lane == s, found, wanted)
-    plan_v[...] = wanted.astype(jnp.int32)
     to_scalar = pltpu.make_async_copy(plan_v, plan, sem)
     to_scalar.start()
+    for load in loads:
+        load.start()
     to_scalar.wait()
+    for load in loads:
+        load.wait()
 
     slot_row = lax.broadcasted_iota(jnp.int32, (slots, LANES), 0)
     slot_lane = lax.broadcasted_iota(jnp.int32, (slots, LANES), 1)
-    for b in range(blocks):
+
+    def score_block(b, carry):
         count = plan[b, slots]
 
-        def score_group(g, carry, b=b):
-            left = jnp.concatenate([tiles[plan[b, g * GROUP + t]] for t in range(GROUP)], axis=0)
-            start = pl.multiple_of(g * (8 * GROUP), 8 * GROUP)
-            for c in range(0, len(chunks[b]), 2):
-                pair = [ref[r : r + LANES, :] for ref, r in chunks[b][c : c + 2]]
+        def score_tiles(first, number):
+            left = jnp.concatenate([tiles[plan[b, first + t]] for t in range(number)], axis=0)
+            start = pl.multiple_of(first * 8, 8 * number)
+            for c in range(0, nearest.shape[0], 2):
+                pair = [weights[b, k * LANES : (k + 1) * LANES, :] for k in (c, c + 1)]
                 similar = jnp.dot(
                     left, jnp.concatenate(pair, axis=1), preferred_element_type=jnp.float32
                 )
-                width = similar.shape[1]
-                rows = jnp.max(similar.reshape(GROUP, tile_rows // 8, 8, width), axis=1)
-                rows = rows.reshape(8 * GROUP, width)
-                for k in range(width // LANES):
-                    nearest[c + k, pl.ds(start, 8 * GROUP), :] = rows[:, k * LANES : (k + 1) * LANES]
+                best = jnp.max(similar.reshape(number, tile_rows // 8, 8, 2 * LANES), axis=1)
+                best = best.reshape(number * 8, 2 * LANES)
+                for k in range(2):
+                    nearest[c + k, pl.ds(start, number * 8), :] = best[:, k * LANES : (k + 1) * LANES]
+
+        whole = count // GROUP
+        rest = count - whole * GROUP
+        small = (rest > 0) & (rest <= GROUP // 2)
+        turns = pl.cdiv(count, GROUP) - small.astype(jnp.int32)
+
+        def turn(g, carry):
+            score_tiles(pl.multiple_of(g * GROUP, GROUP), GROUP)
             return carry
 
-        lax.fori_loop(0, pl.cdiv(count, GROUP), score_group, 0)
+        lax.fori_loop(0, turns, turn, 0)
+        pl.when(small)(lambda: score_tiles(pl.multiple_of(whole * GROUP, GROUP), GROUP // 2))
+
         total = jnp.zeros((slots, LANES), jnp.float32)
         for k in range(nearest.shape[0]):
             x = nearest[k, pl.ds(0, slots, stride=8), :]
@@ -229,26 +252,37 @@
             if k:
                 x = pltpu.roll(x, k, 1)
             total = jnp.where(slot_lane % query_tok == k, x, total)
-        outs[b][...] = jnp.where(slot_row < count, total / float(query_tok), 0.0)
-
-
-def score(held, slots, query_tok, tiles):
+        total = jnp.where(slot_row < count, total / float(query_tok), 0.0)
+        for k in range(blocks):
+
+            @pl.when(b == k)
+            def _(k=k):
+                outs[k][...] = total
+
+        return carry
+
+    lax.fori_loop(0, blocks, score_block, 0)
+
+
+def score(held, slots, query_tok, chips, tiles):
     pieces = tuple(len(arrays) for arrays in held)
     flat = [x for arrays in held for x in arrays]
     blocks = len(pieces)
     _, tile_rows, feature = tiles.shape
-    query_rows = sum(x.shape[0] for x in held[0]) - FACT_ROWS
+    query_rows = sum(x.shape[0] for x in held[0]) - fact_rows_of(chips)
     flops = 2 * blocks * slots * tile_rows * feature * query_rows
     return pl.pallas_call(
-        functools.partial(score_kernel, pieces, slots, query_tok),
+        functools.partial(score_kernel, pieces, slots, query_tok, chips),
         out_shape=(jax.ShapeDtypeStruct((slots, LANES), jnp.float32),) * blocks,
         in_specs=[pl.BlockSpec(memory_space=pltpu.VMEM)] * (1 + len(flat)),
         out_specs=(pl.BlockSpec(memory_space=pltpu.VMEM),) * blocks,
         scratch_shapes=[
+            pltpu.VMEM((blocks, query_rows, feature), tiles.dtype),
             pltpu.VMEM((query_rows // LANES, 8 * slots, LANES), jnp.float32),
             pltpu.VMEM((8, LANES), jnp.int32),
             pltpu.SMEM((8, LANES), jnp.int32),
             pltpu.SemaphoreType.DMA,
+            pltpu.SemaphoreType.DMA((len(flat),)),
         ],
         compiler_params=pltpu.CompilerParams(vmem_limit_bytes=VMEM_LIMIT),
         cost_estimate=pl.CostEstimate(
@@ -374,7 +408,9 @@
     slot_of, own = ready(lengths, candidates, passages, chips, slots)
     tiles = join(other_lengths, other, own)
 
-    block = pack(queries.reshape(per_device * query_tok, feature), candidates, per_owner)
+    block = pack(
+        queries.reshape(per_device * query_tok, feature), candidates, per_owner, chips, slots
+    )
     half = per_device * query_tok // LANES // 2 * LANES
     middle = chips // 2
     arrived = {0: [block]}
@@ -390,19 +426,18 @@
 
     send_on(1)
     back = {}
-    for step in range(1, middle + 1):
-        if step < middle:
+    for step in range(middle + 1):
+        if 0 < step < middle:
             send_on(step + 1)
-        offsets = (0, 1, -1) if step == 1 else (middle,) if step == middle else (step, -step)
-        fresh = score([arrived[offset] for offset in offsets], slots, query_tok, tiles)
-        if step < middle:
-            names = [step + 1, -step - 1] if step + 1 < middle else [middle]
-            earlier = [(1 - step) % chips, (step - 1) % chips] if step > 1 else []
-            held, fresh, came = lax.optimization_barrier(
-                ([arrived[name] for name in names], fresh, [back[j] for j in earlier])
-            )
-            arrived.update(zip(names, held))
-            back.update(zip(earlier, came))
+        offsets = (step,) if step in (0, middle) else (step, -step)
+        fresh = score([arrived[offset] for offset in offsets], slots, query_tok, chips, tiles)
+        earlier = [(step - 1) % chips, (1 - step) % chips] if step > 1 else []
+        names = [] if step == middle else [step + 1, -step - 1] if step + 1 < middle else [middle]
+        held, fresh, came = lax.optimization_barrier(
+            ([arrived[name] for name in names], fresh, [back[j] for j in earlier])
+        )
+        arrived.update(zip(names, held))
+        back.update(zip(earlier, came))
         for offset, result in zip(offsets, fresh):
             back[offset % chips] = moved(result, -offset) if offset else result
     return finish(per_device, query_tok, slot_of, [back[j] for j in range(chips)])

time: 80.1 us -> 73.4 us (0.916)
  the two profiles are of different devices: /device:TPU:2 before, /device:TPU:0 now
where the time goes in v5:
time: 73.4 us; the launch traced here: 73.2 us
  Pallas kernels  30.7 us (42%)
  starting transfers between devices  23.3 us (32%)
  waiting for transfers between devices  14.9 us (20%)
  local copies, waits for them, and re-layouts  3.53 us (5%)
  between operations  0.79 us (1%)
    pallas_call x5, Pallas kernels, score(): pl.pallas_call(functools.partial(score_kernel, pieces, slots, query_tok,...  23.5 us
    ppermute x15, starting transfers between devices, moved(): return lax.ppermute(x, 'corpus', pairs)  22.6 us
    ppermute x15, waiting for transfers between devices, moved(): return lax.ppermute(x, 'corpus', pairs)  14.9 us
    unnamed x8, local copies, waits for them, and re-layouts  3.5 us
    pallas_call x1, Pallas kernels, ready(): pl.pallas_call(functools.partial(ready_kernel, chips, slots, parts), out_...  2.38 us
    pallas_call x1, Pallas kernels, pack(): pl.pallas_call(functools.partial(pack_kernel, per_owner, chips, slots), o...  2.08 us
    pallas_call x1, Pallas kernels, join(): pl.pallas_call(join_kernel, out_shape=jax.ShapeDtypeStruct(filled.shape,...  1.65 us
  transfers between devices with their start and end apart: 17, of which 7 were waited for; matrix products, arithmetic and copies ran while one was open for 0% of the time, Pallas kernels for 40%

profile of v5, /device:TPU:0, one launch (start us, length us, event | category | flops | bytes accessed | tf_op | source)
XLA Modules:
  0.0 73.2 jit_solution(16210330688759251418)
XLA Ops:
  0.6 0.5 collective-permute-start.3
  1.1 2.1 %pack.1.refs_1_ = bf16[1808,128]{1,0:T(8,128)(2,1)} custom-call(bf16[1792,128]{1,0:T(8,128)(2,1)} %bitcast.1, s32[1,128]{1,0:T(1,128)} %candidates_in.1), custom_call_target="tpu_custom_call" | custom-call | tf_op jit(solution)/shard_map/pack/pallas_call | solution.py:75
  3.2 2.6 %collective-permute-start = (bf16[1808,128]{1,0:T(8,128)(2,1)}, bf16[1808,128]{1,0:T(8,128)(2,1)S(1)}, u32[]{:S(2)}, u32[]{:S(2)}) collective-permute-start(bf16[1808,128]{1,0:T(8,128)(2,1)} %pack.1.refs_1_), channel_id=1, source_target_pairs={{0,4},{1,5},{4,8},{5,9},{8,12},{9,13},{12,14},{13,15},{14,10},{15,... | collective-permute-start | bytes 1388552 | tf_op jit(solution)/shard_map/ppermute | solution.py:403
  5.9 0.0 collective-permute-start.1
  5.9 0.2 collective-permute-start.2
  6.1 0.0 copy-start
  6.1 2.2 %copy-done = bf16[128,128,128]{2,1,0:T(8,128)(2,1)S(1)} copy-done((bf16[128,128,128]{2,1,0:T(8,128)(2,1)S(1)}, bf16[128,128,128]{2,1,0:T(8,128)(2,1)}, u32[]{:S(2)}) %copy-start) | copy-done | bytes 4194328
  8.3 0.0 copy-start.2
  8.3 0.7 copy-done.2
  8.9 0.0 copy-start.3
  8.9 0.7 copy-done.3
  9.6 2.4 %ready.1 = (s32[128,128]{1,0:T(8,128)S(1)}, bf16[256,128,128]{2,1,0:T(8,128)(2,1)S(1)}) custom-call(s32[128]{0:T(128)S(1)} %copy-done.3, s32[1,128]{1,0:T(1,128)S(1)} %copy-done.2, bf16[128,128,128]{2,1,0:T(8,128)(2,1)S(1)} %copy-done), custom_call_target="tpu_custom_call" | custom-call | tf_op jit(solution)/shard_map/ready/pallas_call | solution.py:136
  12.0 0.0 collective-permute-done.2.lens
  12.0 0.0 collective-permute-done.3.other
  12.0 0.0 copy-start.1
  12.0 1.6 %join.1.refs_0_ = bf16[256,128,128]{2,1,0:T(8,128)(2,1)S(1)} custom-call(s32[128]{0:T(128)S(1)} %collective-permute-done.2.lens, bf16[128,128,128]{2,1,0:T(8,128)(2,1)S(1)} %collective-permute-done.3.other, bf16[256,128,128]{2,1,0:T(8,128)(2,1)S(1)} %get-tuple-element.33.held), custom_call_target="tpu_custom_call", output_to_operand_aliasing={{}: (2, {})} | custom-call | tf_op jit(solution)/shard_map/join/pallas_call | solution.py:161
  13.7 0.0 copy-done.1
  13.7 3.5 %score.5.refs_0_ = f32[24,128]{1,0:T(8,128)S(1)} custom-call(bf16[256,128,128]{2,1,0:T(8,128)(2,1)S(1)} %join.1.refs_0_, bf16[1808,128]{1,0:T(8,128)(2,1)S(1)} %copy-done.1), custom_call_target="tpu_custom_call" | custom-call | flops 4227858432 | bytes 1245184 | tf_op jit(solution)/shard_map/score/pallas_call | solution.py:274
  17.2 0.1 collective-permute-done.refs_1_
  17.3 1.5 %collective-permute-done.1.refs_2_ = bf16[1808,128]{1,0:T(8,128)(2,1)S(1)} collective-permute-done((bf16[1808,128]{1,0:T(8,128)(2,1)}, bf16[1808,128]{1,0:T(8,128)(2,1)S(1)}, u32[]{:S(2)}, u32[]{:S(2)}) %collective-permute-start.1) | collective-permute-done | bytes 462880 | tf_op jit(solution)/shard_map/ppermute | solution.py:403
  18.8 1.6 %collective-permute-start.4 = (bf16[1808,128]{1,0:T(8,128)(2,1)S(1)}, bf16[1808,128]{1,0:T(8,128)(2,1)S(1)}, u32[]{:S(2)}, u32[]{:S(2)}) collective-permute-start(bf16[1808,128]{1,0:T(8,128)(2,1)S(1)} %collective-permute-done.refs_1_), channel_id=1, source_target_pairs={{0,4},{1,5},{4,8},{5,9},{8,12},{9,13},{12,14},{13,15},{14,10},{15,... | collective-permute-start | bytes 1388552 | tf_op jit(solution)/shard_map/ppermute | solution.py:403
  20.4 0.4 collective-permute-start.5
  20.8 5.4 %score.6 = (f32[24,128]{1,0:T(8,128)S(1)}, f32[24,128]{1,0:T(8,128)S(1)}) custom-call(bf16[256,128,128]{2,1,0:T(8,128)(2,1)S(1)} %join.1.refs_0_, bf16[1808,128]{1,0:T(8,128)(2,1)S(1)} %collective-permute-done.refs_1_, bf16[1808,128]{1,0:T(8,128)(2,1)S(1)} %collective-permute-done.1.refs_2_), custom_call_target="tpu_custom_call" | custom-call | flops 8455716864 | bytes 2490368 | tf_op jit(solution)/shard_map/score/pallas_call | solution.py:274
  26.2 4.5 %collective-permute-done.4.refs_1_ = bf16[1808,128]{1,0:T(8,128)(2,1)S(1)} collective-permute-done((bf16[1808,128]{1,0:T(8,128)(2,1)S(1)}, bf16[1808,128]{1,0:T(8,128)(2,1)S(1)}, u32[]{:S(2)}, u32[]{:S(2)}) %collective-permute-start.4) | collective-permute-done | bytes 462880 | tf_op jit(solution)/shard_map/ppermute | solution.py:403
  30.7 2.2 %collective-permute-done.5.refs_2_ = bf16[1808,128]{1,0:T(8,128)(2,1)S(1)} collective-permute-done((bf16[1808,128]{1,0:T(8,128)(2,1)S(1)}, bf16[1808,128]{1,0:T(8,128)(2,1)S(1)}, u32[]{:S(2)}, u32[]{:S(2)}) %collective-permute-start.5) | collective-permute-done | bytes 462880 | tf_op jit(solution)/shard_map/ppermute | solution.py:403
  32.9 1.1 %collective-permute-start.6 = (bf16[1808,128]{1,0:T(8,128)(2,1)S(1)}, bf16[1808,128]{1,0:T(8,128)(2,1)S(1)}, u32[]{:S(2)}, u32[]{:S(2)}) collective-permute-start(bf16[1808,128]{1,0:T(8,128)(2,1)S(1)} %collective-permute-done.4.refs_1_), channel_id=1, source_target_pairs={{0,4},{1,5},{4,8},{5,9},{8,12},{9,13},{12,14},{13,15},{14,10},{15,... | collective-permute-start | bytes 1388552 | tf_op jit(solution)/shard_map/ppermute | solution.py:403
  34.0 0.9 %collective-permute-start.7 = (bf16[1808,128]{1,0:T(8,128)(2,1)S(1)}, bf16[1808,128]{1,0:T(8,128)(2,1)S(1)}, u32[]{:S(2)}, u32[]{:S(2)}) collective-permute-start(bf16[1808,128]{1,0:T(8,128)(2,1)S(1)} %collective-permute-done.5.refs_2_), channel_id=1, source_target_pairs={{0,2},{1,3},{4,0},{5,1},{8,4},{9,5},{12,8},{13,9},{14,12},{15,13},... | collective-permute-start | bytes 1388552 | tf_op jit(solution)/shard_map/ppermute | solution.py:403
  34.9 0.3 collective-permute-start.8
  35.2 1.7 %collective-permute-start.9 = (f32[24,128]{1,0:T(8,128)S(1)}, f32[24,128]{1,0:T(8,128)S(1)}, u32[]{:S(2)}, u32[]{:S(2)}) collective-permute-start(f32[24,128]{1,0:T(8,128)S(1)} %get-tuple-element.44), channel_id=1, source_target_pairs={{0,4},{1,5},{4,8},{5,9},{8,12},{9,13},{12,14},{13,15},{14,10},{15,... | collective-permute-start | bytes 36872 | tf_op jit(solution)/shard_map/ppermute | solution.py:403
  37.0 5.8 %score.7 = (f32[24,128]{1,0:T(8,128)S(1)}, f32[24,128]{1,0:T(8,128)S(1)}) custom-call(bf16[256,128,128]{2,1,0:T(8,128)(2,1)S(1)} %join.1.refs_0_, bf16[1808,128]{1,0:T(8,128)(2,1)S(1)} %collective-permute-done.4.refs_1_, bf16[1808,128]{1,0:T(8,128)(2,1)S(1)} %collective-permute-done.5.refs_2_), custom_call_target="tpu_custom_call" | custom-call | flops 8455716864 | bytes 2490368 | tf_op jit(solution)/shard_map/score/pallas_call | solution.py:274
  42.8 2.4 %collective-permute-done.8.refs_1_ = f32[24,128]{1,0:T(8,128)S(1)} collective-permute-done((f32[24,128]{1,0:T(8,128)S(1)}, f32[24,128]{1,0:T(8,128)S(1)}, u32[]{:S(2)}, u32[]{:S(2)}) %collective-permute-start.8) | collective-permute-done | bytes 12320 | tf_op jit(solution)/shard_map/ppermute | solution.py:403
  45.1 0.0 collective-permute-done.9.refs_7_
  45.1 0.0 collective-permute-done.6.refs_1_
  45.1 0.0 collective-permute-done.7.refs_2_
  45.2 1.5 %collective-permute-start.11 = (bf16[912,128]{1,0:T(8,128)(2,1)S(1)}, bf16[912,128]{1,0:T(8,128)(2,1)S(1)}, u32[]{:S(2)}, u32[]{:S(2)}) collective-permute-start(bf16[912,128]{1,0:T(8,128)(2,1)S(1)} %slice.7), channel_id=1, source_target_pairs={{0,2},{1,3},{4,0},{5,1},{8,4},{9,5},{12,8},{13,9},{14,12},{15,13},... | collective-permute-start | bytes 700424 | tf_op jit(solution)/shard_map/ppermute | solution.py:403
  46.7 0.7 collective-permute-start.10
  47.3 1.2 %collective-permute-start.12 = (f32[24,128]{1,0:T(8,128)S(1)}, f32[24,128]{1,0:T(8,128)S(1)}, u32[]{:S(2)}, u32[]{:S(2)}) collective-permute-start(f32[24,128]{1,0:T(8,128)S(1)} %get-tuple-element.50), channel_id=1, source_target_pairs={{0,6},{1,7},{4,2},{5,3},{8,0},{9,1},{12,4},{13,5},{14,8},{15,9},{1... | collective-permute-start | bytes 36872 | tf_op jit(solution)/shard_map/ppermute | solution.py:403
  48.6 1.7 %collective-permute-start.13 = (f32[24,128]{1,0:T(8,128)S(1)}, f32[24,128]{1,0:T(8,128)S(1)}, u32[]{:S(2)}, u32[]{:S(2)}) collective-permute-start(f32[24,128]{1,0:T(8,128)S(1)} %get-tuple-element.51), channel_id=1, source_target_pairs={{0,8},{1,9},{4,12},{5,13},{8,14},{9,15},{12,10},{13,11},{14,6},{15... | collective-permute-start | bytes 36872 | tf_op jit(solution)/shard_map/ppermute | solution.py:403
  50.3 5.3 %score.8 = (f32[24,128]{1,0:T(8,128)S(1)}, f32[24,128]{1,0:T(8,128)S(1)}) custom-call(bf16[256,128,128]{2,1,0:T(8,128)(2,1)S(1)} %join.1.refs_0_, bf16[1808,128]{1,0:T(8,128)(2,1)S(1)} %collective-permute-done.6.refs_1_, bf16[1808,128]{1,0:T(8,128)(2,1)S(1)} %collective-permute-done.7.refs_2_), custom_call_target="tpu_custom_call" | custom-call | flops 8455716864 | bytes 2490368 | tf_op jit(solution)/shard_map/score/pallas_call | solution.py:274
  55.6 0.0 collective-permute-done.12.refs_2_
  55.6 0.0 collective-permute-done.13.refs_6_
  55.6 0.0 collective-permute-done.10.refs_1_
  55.6 0.0 collective-permute-done.11.refs_2_
  55.6 4.5 %collective-permute-start.14 = (f32[24,128]{1,0:T(8,128)S(1)}, f32[24,128]{1,0:T(8,128)S(1)}, u32[]{:S(2)}, u32[]{:S(2)}) collective-permute-start(f32[24,128]{1,0:T(8,128)S(1)} %get-tuple-element.55), channel_id=1, source_target_pairs={{0,10},{1,11},{4,6},{5,7},{8,2},{9,3},{12,0},{13,1},{14,4},{15,5},... | collective-permute-start | bytes 36872 | tf_op jit(solution)/shard_map/ppermute | solution.py:403
  60.2 0.3 collective-permute-start.15
  60.5 3.5 %score.9 = f32[24,128]{1,0:T(8,128)S(1)} custom-call(bf16[256,128,128]{2,1,0:T(8,128)(2,1)S(1)} %join.1.refs_0_, bf16[896,128]{1,0:T(8,128)(2,1)S(1)} %collective-permute-done.10.refs_1_, bf16[912,128]{1,0:T(8,128)(2,1)S(1)} %collective-permute-done.11.refs_2_), custom_call_target="tpu_custom_call" | custom-call | flops 4227858432 | bytes 1245184 | tf_op jit(solution)/shard_map/score/pallas_call | solution.py:274
  64.0 0.0 collective-permute-done.14.refs_3_
  64.0 1.7 %collective-permute-done.15.refs_5_ = f32[24,128]{1,0:T(8,128)S(1)} collective-permute-done((f32[24,128]{1,0:T(8,128)S(1)}, f32[24,128]{1,0:T(8,128)S(1)}, u32[]{:S(2)}, u32[]{:S(2)}) %collective-permute-start.15) | collective-permute-done | bytes 12320 | tf_op jit(solution)/shard_map/ppermute | solution.py:403
  65.7 3.9 %collective-permute-start.16 = (f32[24,128]{1,0:T(8,128)S(1)}, f32[24,128]{1,0:T(8,128)S(1)}, u32[]{:S(2)}, u32[]{:S(2)}) collective-permute-start(f32[24,128]{1,0:T(8,128)S(1)} %score.9), channel_id=1, source_target_pairs={{0,14},{1,15},{4,10},{5,11},{8,6},{9,7},{12,2},{13,3},{14,0},{15,1... | collective-permute-start | bytes 36872 | tf_op jit(solution)/shard_map/ppermute | solution.py:403
  69.6 2.5 %collective-permute-done.16.refs_4_ = f32[24,128]{1,0:T(8,128)S(1)} collective-permute-done((f32[24,128]{1,0:T(8,128)S(1)}, f32[24,128]{1,0:T(8,128)S(1)}, u32[]{:S(2)}, u32[]{:S(2)}) %collective-permute-start.16) | collective-permute-done | bytes 12320 | tf_op jit(solution)/shard_map/ppermute | solution.py:403
  72.1 1.1 %finish.1 = (f32[56,128]{1,0:T(8,128)}, f32[56,100]{1,0:T(8,128)}) custom-call(s32[128,128]{1,0:T(8,128)S(1)} %get-tuple-element.32.slot_of, f32[24,128]{1,0:T(8,128)S(1)} %score.5.refs_0_, f32[24,128]{1,0:T(8,128)S(1)} %collective-permute-done.8.refs_1_, f32[24,128]{1,0:T(8,128)S(1)} %collective-permute-done.12.refs_2_, ...), custom_call_target="tpu_custom_call" | custom-call | tf_op jit(solution)/shard_map/finish/pallas_call | solution.py:369
  (2 shorter events, 0.0 us)
Async XLA Ops:
  0.6 11.4 %collective-permute-start.3 = (bf16[128,128,128]{2,1,0:T(8,128)(2,1)}, bf16[128,128,128]{2,1,0:T(8,128)(2,1)S(1)}, u32[]{:S(2)}, u32[]{:S(2)}) collective-permute-start(bf16[128,128,128]{2,1,0:T(8,128)(2,1)} %passages.1), channel_id=1, source_target_pairs={{0,1},{1,0},{2,3},{3,2},{4,5},{5,4},{6,7},{7,6},{8,9},{9,8},{10,11... | collective-permute-start | bytes 12582920 | tf_op jit(solution)/shard_map/ppermute | solution.py:406
  3.2 14.1 %collective-permute-start = (bf16[1808,128]{1,0:T(8,128)(2,1)}, bf16[1808,128]{1,0:T(8,128)(2,1)S(1)}, u32[]{:S(2)}, u32[]{:S(2)}) collective-permute-start(bf16[1808,128]{1,0:T(8,128)(2,1)} %pack.1.refs_1_), channel_id=1, source_target_pairs={{0,4},{1,5},{4,8},{5,9},{8,12},{9,13},{12,14},{13,15},{14,10},{15,... | collective-permute-start | bytes 1388552 | tf_op jit(solution)/shard_map/ppermute | solution.py:403
  5.9 12.9 %collective-permute-start.1 = (bf16[1808,128]{1,0:T(8,128)(2,1)}, bf16[1808,128]{1,0:T(8,128)(2,1)S(1)}, u32[]{:S(2)}, u32[]{:S(2)}) collective-permute-start(bf16[1808,128]{1,0:T(8,128)(2,1)} %pack.1.refs_1_), channel_id=1, source_target_pairs={{0,2},{1,3},{4,0},{5,1},{8,4},{9,5},{12,8},{13,9},{14,12},{15,13},... | collective-permute-start | bytes 1388552 | tf_op jit(solution)/shard_map/ppermute | solution.py:403
  5.9 6.1 %collective-permute-start.2 = (s32[128]{0:T(128)}, s32[128]{0:T(128)S(1)}, u32[]{:S(2)}, u32[]{:S(2)}) collective-permute-start(s32[128]{0:T(128)} %lens.1), channel_id=1, source_target_pairs={{0,1},{1,0},{2,3},{3,2},{4,5},{5,4},{6,7},{7,6},{8,9},{9,8},{10,11... | collective-permute-start | bytes 1544 | tf_op jit(solution)/shard_map/ppermute | solution.py:407
  6.1 2.2 %copy-start = (bf16[128,128,128]{2,1,0:T(8,128)(2,1)S(1)}, bf16[128,128,128]{2,1,0:T(8,128)(2,1)}, u32[]{:S(2)}) copy-start(bf16[128,128,128]{2,1,0:T(8,128)(2,1)} %passages.1) | copy-start | bytes 12582916
  8.3 0.7 copy-start.2
  8.9 0.7 copy-start.3
  12.0 1.7 %copy-start.1 = (bf16[1808,128]{1,0:T(8,128)(2,1)S(1)}, bf16[1808,128]{1,0:T(8,128)(2,1)}, u32[]{:S(2)}) copy-start(bf16[1808,128]{1,0:T(8,128)(2,1)} %pack.1.refs_1_) | copy-start | bytes 1388548
  18.8 11.9 %collective-permute-start.4 = (bf16[1808,128]{1,0:T(8,128)(2,1)S(1)}, bf16[1808,128]{1,0:T(8,128)(2,1)S(1)}, u32[]{:S(2)}, u32[]{:S(2)}) collective-permute-start(bf16[1808,128]{1,0:T(8,128)(2,1)S(1)} %collective-permute-done.refs_1_), channel_id=1, source_target_pairs={{0,4},{1,5},{4,8},{5,9},{8,12},{9,13},{12,14},{13,15},{14,10},{15,... | collective-permute-start | bytes 1388552 | tf_op jit(solution)/shard_map/ppermute | solution.py:403
  20.4 12.5 %collective-permute-start.5 = (bf16[1808,128]{1,0:T(8,128)(2,1)S(1)}, bf16[1808,128]{1,0:T(8,128)(2,1)S(1)}, u32[]{:S(2)}, u32[]{:S(2)}) collective-permute-start(bf16[1808,128]{1,0:T(8,128)(2,1)S(1)} %collective-permute-done.1.refs_2_), channel_id=1, source_target_pairs={{0,2},{1,3},{4,0},{5,1},{8,4},{9,5},{12,8},{13,9},{14,12},{15,13},... | collective-permute-start | bytes 1388552 | tf_op jit(solution)/shard_map/ppermute | solution.py:403
  32.9 12.2 %collective-permute-start.6 = (bf16[1808,128]{1,0:T(8,128)(2,1)S(1)}, bf16[1808,128]{1,0:T(8,128)(2,1)S(1)}, u32[]{:S(2)}, u32[]{:S(2)}) collective-permute-start(bf16[1808,128]{1,0:T(8,128)(2,1)S(1)} %collective-permute-done.4.refs_1_), channel_id=1, source_target_pairs={{0,4},{1,5},{4,8},{5,9},{8,12},{9,13},{12,14},{13,15},{14,10},{15,... | collective-permute-start | bytes 1388552 | tf_op jit(solution)/shard_map/ppermute | solution.py:403
  34.0 11.2 %collective-permute-start.7 = (bf16[1808,128]{1,0:T(8,128)(2,1)S(1)}, bf16[1808,128]{1,0:T(8,128)(2,1)S(1)}, u32[]{:S(2)}, u32[]{:S(2)}) collective-permute-start(bf16[1808,128]{1,0:T(8,128)(2,1)S(1)} %collective-permute-done.5.refs_2_), channel_id=1, source_target_pairs={{0,2},{1,3},{4,0},{5,1},{8,4},{9,5},{12,8},{13,9},{14,12},{15,13},... | collective-permute-start | bytes 1388552 | tf_op jit(solution)/shard_map/ppermute | solution.py:403
  34.9 10.2 %collective-permute-start.8 = (f32[24,128]{1,0:T(8,128)S(1)}, f32[24,128]{1,0:T(8,128)S(1)}, u32[]{:S(2)}, u32[]{:S(2)}) collective-permute-start(f32[24,128]{1,0:T(8,128)S(1)} %get-tuple-element.43), channel_id=1, source_target_pairs={{0,2},{1,3},{4,0},{5,1},{8,4},{9,5},{12,8},{13,9},{14,12},{15,13},... | collective-permute-start | bytes 36872 | tf_op jit(solution)/shard_map/ppermute | solution.py:403
  35.2 9.9 %collective-permute-start.9 = (f32[24,128]{1,0:T(8,128)S(1)}, f32[24,128]{1,0:T(8,128)S(1)}, u32[]{:S(2)}, u32[]{:S(2)}) collective-permute-start(f32[24,128]{1,0:T(8,128)S(1)} %get-tuple-element.44), channel_id=1, source_target_pairs={{0,4},{1,5},{4,8},{5,9},{8,12},{9,13},{12,14},{13,15},{14,10},{15,... | collective-permute-start | bytes 36872 | tf_op jit(solution)/shard_map/ppermute | solution.py:403
  45.2 10.5 %collective-permute-start.11 = (bf16[912,128]{1,0:T(8,128)(2,1)S(1)}, bf16[912,128]{1,0:T(8,128)(2,1)S(1)}, u32[]{:S(2)}, u32[]{:S(2)}) collective-permute-start(bf16[912,128]{1,0:T(8,128)(2,1)S(1)} %slice.7), channel_id=1, source_target_pairs={{0,2},{1,3},{4,0},{5,1},{8,4},{9,5},{12,8},{13,9},{14,12},{15,13},... | collective-permute-start | bytes 700424 | tf_op jit(solution)/shard_map/ppermute | solution.py:403
  46.7 9.0 %collective-permute-start.10 = (bf16[896,128]{1,0:T(8,128)(2,1)S(1)}, bf16[896,128]{1,0:T(8,128)(2,1)S(1)}, u32[]{:S(2)}, u32[]{:S(2)}) collective-permute-start(bf16[896,128]{1,0:T(8,128)(2,1)S(1)} %slice.6), channel_id=1, source_target_pairs={{0,4},{1,5},{4,8},{5,9},{8,12},{9,13},{12,14},{13,15},{14,10},{15,... | collective-permute-start | bytes 688136 | tf_op jit(solution)/shard_map/ppermute | solution.py:403
  47.3 8.3 %collective-permute-start.12 = (f32[24,128]{1,0:T(8,128)S(1)}, f32[24,128]{1,0:T(8,128)S(1)}, u32[]{:S(2)}, u32[]{:S(2)}) collective-permute-start(f32[24,128]{1,0:T(8,128)S(1)} %get-tuple-element.50), channel_id=1, source_target_pairs={{0,6},{1,7},{4,2},{5,3},{8,0},{9,1},{12,4},{13,5},{14,8},{15,9},{1... | collective-permute-start | bytes 36872 | tf_op jit(solution)/shard_map/ppermute | solution.py:403
  48.6 7.1 %collective-permute-start.13 = (f32[24,128]{1,0:T(8,128)S(1)}, f32[24,128]{1,0:T(8,128)S(1)}, u32[]{:S(2)}, u32[]{:S(2)}) collective-permute-start(f32[24,128]{1,0:T(8,128)S(1)} %get-tuple-element.51), channel_id=1, source_target_pairs={{0,8},{1,9},{4,12},{5,13},{8,14},{9,15},{12,10},{13,11},{14,6},{15... | collective-permute-start | bytes 36872 | tf_op jit(solution)/shard_map/ppermute | solution.py:403
  55.6 8.4 %collective-permute-start.14 = (f32[24,128]{1,0:T(8,128)S(1)}, f32[24,128]{1,0:T(8,128)S(1)}, u32[]{:S(2)}, u32[]{:S(2)}) collective-permute-start(f32[24,128]{1,0:T(8,128)S(1)} %get-tuple-element.55), channel_id=1, source_target_pairs={{0,10},{1,11},{4,6},{5,7},{8,2},{9,3},{12,0},{13,1},{14,4},{15,5},... | collective-permute-start | bytes 36872 | tf_op jit(solution)/shard_map/ppermute | solution.py:403
  60.2 5.5 %collective-permute-start.15 = (f32[24,128]{1,0:T(8,128)S(1)}, f32[24,128]{1,0:T(8,128)S(1)}, u32[]{:S(2)}, u32[]{:S(2)}) collective-permute-start(f32[24,128]{1,0:T(8,128)S(1)} %get-tuple-element.56), channel_id=1, source_target_pairs={{0,12},{1,13},{4,14},{5,15},{8,10},{9,11},{12,6},{13,7},{14,2},{15... | collective-permute-start | bytes 36872 | tf_op jit(solution)/shard_map/ppermute | solution.py:403
  65.7 6.4 %collective-permute-start.16 = (f32[24,128]{1,0:T(8,128)S(1)}, f32[24,128]{1,0:T(8,128)S(1)}, u32[]{:S(2)}, u32[]{:S(2)}) collective-permute-start(f32[24,128]{1,0:T(8,128)S(1)} %score.9), channel_id=1, source_target_pairs={{0,14},{1,15},{4,10},{5,11},{8,6},{9,7},{12,2},{13,3},{14,0},{15,1... | collective-permute-start | bytes 36872 | tf_op jit(solution)/shard_map/ppermute | solution.py:403

commit v6 on v5

--- a/solution.py
+++ b/solution.py
@@ -87,13 +87,13 @@
     )(queries, candidates)
 
 
-def fill_tiles(source, source_at, lens, filled, filled_at, first, number):
+def fill_tiles(source, lens, filled, filled_at, first, number):
     row = lax.broadcasted_iota(jnp.int32, source.shape[1:], 0)
 
     def some(i, carry):
         for k in range(4):
             at = first + 4 * i + k
-            tile = source[source_at + at].astype(jnp.float32)
+            tile = source[at].astype(jnp.float32)
             tile = jnp.where(row < lens[at], tile, tile[0:1, :])
             filled[filled_at + at] = tile.astype(jnp.bfloat16)
         return carry
@@ -104,10 +104,9 @@
 def ready_kernel(chips, slots, parts, lens, candidates, passages, slot_of, filled, sems):
     per_owner = passages.shape[0]
     size = per_owner // parts
-    base = lax.axis_index("corpus") % CORES * per_owner
     loads = [
         pltpu.make_async_copy(
-            passages.at[pl.ds(i * size, size)], filled.at[pl.ds(base + i * size, size)], sems.at[i]
+            passages.at[pl.ds(i * size, size)], filled.at[pl.ds(i * size, size)], sems.at[i]
         )
         for i in range(parts)
     ]
@@ -126,7 +125,7 @@
     slot_of[...] = ahead * slots + rank
     for i, load in enumerate(loads):
         load.wait()
-        fill_tiles(filled, base, lens, filled, base, i * size, size)
+        fill_tiles(filled, lens, filled, 0, i * size, size)
 
 
 def ready(lengths, candidates, passages, chips, slots):
@@ -137,7 +136,7 @@
         functools.partial(ready_kernel, chips, slots, parts),
         out_shape=(
             jax.ShapeDtypeStruct((number, number), jnp.int32),
-            jax.ShapeDtypeStruct((CORES * per_owner,) + passages.shape[1:], passages.dtype),
+            jax.ShapeDtypeStruct(passages.shape, passages.dtype),
         ),
         in_specs=[
             pl.BlockSpec(memory_space=pltpu.SMEM),
@@ -151,26 +150,57 @@
     )(lengths, candidates, passages)
 
 
-def join_kernel(lens, other, held, filled):
+def join_kernel(lens, other, own, filled, sem):
     per_owner = other.shape[0]
-    base = (1 - lax.axis_index("corpus") % CORES) * per_owner
-    fill_tiles(other, 0, lens, filled, base, 0, per_owner)
-
-
-def join(lengths, other, filled):
+    core = lax.axis_index("corpus") % CORES
+    keep = pltpu.make_async_copy(own, filled.at[pl.ds(core * per_owner, per_owner)], sem)
+    keep.start()
+    fill_tiles(other, lens, filled, (1 - core) * per_owner, 0, per_owner)
+    keep.wait()
+
+
+def join(lengths, other, own):
     return pl.pallas_call(
         join_kernel,
-        out_shape=jax.ShapeDtypeStruct(filled.shape, filled.dtype),
+        out_shape=jax.ShapeDtypeStruct((CORES * own.shape[0],) + own.shape[1:], own.dtype),
         in_specs=[
             pl.BlockSpec(memory_space=pltpu.SMEM),
             pl.BlockSpec(memory_space=pltpu.VMEM),
             pl.BlockSpec(memory_space=pltpu.VMEM),
         ],
         out_specs=pl.BlockSpec(memory_space=pltpu.VMEM),
-        input_output_aliases={2: 0},
+        scratch_shapes=[pltpu.SemaphoreType.DMA],
         compiler_params=pltpu.CompilerParams(vmem_limit_bytes=VMEM_LIMIT),
         name="join",
-    )(lengths, other, filled)
+    )(lengths, other, own)
+
+
+def lane_step(chunks, query_tok):
+    return query_tok // pl.next_power_of_2(chunks)
+
+
+def token_sums(parts, query_tok):
+    lane = lax.broadcasted_iota(jnp.int32, parts[0].shape, 1)
+    parts = list(parts)
+    parts += [None] * (pl.next_power_of_2(len(parts)) - len(parts))
+    shift = query_tok // 2
+    while shift >= 1:
+        low = (lane & shift) == 0
+        half = max(1, len(parts) // 2)
+        merged = []
+        for k in range(half):
+            a = parts[k]
+            b = parts[k + half] if len(parts) > 1 else None
+            if a is None:
+                merged.append(None)
+                continue
+            x = a + pltpu.roll(a, LANES - shift, 1)
+            if b is not None:
+                x = jnp.where(low, x, b + pltpu.roll(b, shift, 1))
+            merged.append(x)
+        parts = merged
+        shift //= 2
+    return parts[0]
 
 
 def score_kernel(pieces, slots, query_tok, chips, *refs):
@@ -210,7 +240,6 @@
         load.wait()
 
     slot_row = lax.broadcasted_iota(jnp.int32, (slots, LANES), 0)
-    slot_lane = lax.broadcasted_iota(jnp.int32, (slots, LANES), 1)
 
     def score_block(b, carry):
         count = plan[b, slots]
@@ -240,18 +269,13 @@
         lax.fori_loop(0, turns, turn, 0)
         pl.when(small)(lambda: score_tiles(pl.multiple_of(whole * GROUP, GROUP), GROUP // 2))
 
-        total = jnp.zeros((slots, LANES), jnp.float32)
+        parts = []
         for k in range(nearest.shape[0]):
             x = nearest[k, pl.ds(0, slots, stride=8), :]
             for sublane in range(1, 8):
                 x = jnp.maximum(x, nearest[k, pl.ds(sublane, slots, stride=8), :])
-            shift = query_tok // 2
-            while shift >= 1:
-                x = x + pltpu.roll(x, LANES - shift, 1)
-                shift //= 2
-            if k:
-                x = pltpu.roll(x, k, 1)
-            total = jnp.where(slot_lane % query_tok == k, x, total)
+            parts.append(x)
+        total = token_sums(parts, query_tok)
         total = jnp.where(slot_row < count, total / float(query_tok), 0.0)
         for k in range(blocks):
 
@@ -336,7 +360,7 @@
 
 def finish_kernel(arrays, per_device, query_tok, topk, slot_of, *refs):
     returned = refs[:arrays]
-    scores, best_scores, spread, ranked, rows = refs[arrays:]
+    scores, best_scores, spread, ranked, rows, turned = refs[arrays:]
     number = slot_of.shape[0]
     step = returned[0].shape[0]
     for at, ref in enumerate(returned):
@@ -348,11 +372,16 @@
     for part in split_exact(spread[...]):
         by_candidate += jnp.dot(choose, part, preferred_element_type=jnp.float32)
 
+    each = LANES // query_tok
+    step = lane_step(-(-per_device // each), query_tok)
+    many_rows = query_tok // step
+
     def in_order(x):
-        x = x.T
-        each = LANES // query_tok
+        turned[...] = x.T
         for m in range(each):
-            rows[pl.ds(m, query_tok, stride=each), :] = x[m * query_tok : (m + 1) * query_tok, :]
+            rows[pl.ds(m, many_rows, stride=each), :] = turned[
+                pl.ds(m * query_tok, many_rows, stride=step), :
+            ]
         return rows[...]
 
     scores[...] = in_order(by_candidate)[:per_device, :]
@@ -378,6 +407,7 @@
             pltpu.VMEM((total, LANES), jnp.float32),
             pltpu.VMEM((number, LANES), jnp.float32),
             pltpu.VMEM((LANES, number), jnp.float32),
+            pltpu.VMEM((LANES, number), jnp.float32),
         ],
         compiler_params=pltpu.CompilerParams(vmem_limit_bytes=VMEM_LIMIT),
         name="finish",
@@ -431,15 +461,16 @@
             send_on(step + 1)
         offsets = (step,) if step in (0, middle) else (step, -step)
         fresh = score([arrived[offset] for offset in offsets], slots, query_tok, chips, tiles)
-        earlier = [(step - 1) % chips, (1 - step) % chips] if step > 1 else []
+        for offset, result in zip(offsets, fresh):
+            back[offset % chips] = moved(result, -offset) if offset else result
         names = [] if step == middle else [step + 1, -step - 1] if step + 1 < middle else [middle]
-        held, fresh, came = lax.optimization_barrier(
-            ([arrived[name] for name in names], fresh, [back[j] for j in earlier])
+        earlier = [1, -1] if step == 1 else [step - 1, 1 - step] if 2 < step < middle else []
+        earlier = [offset % chips for offset in earlier]
+        held, came, _ = lax.optimization_barrier(
+            ([arrived[name] for name in names], [back[j] for j in earlier], fresh)
         )
         arrived.update(zip(names, held))
         back.update(zip(earlier, came))
-        for offset, result in zip(offsets, fresh):
-            back[offset % chips] = moved(result, -offset) if offset else result
     return finish(per_device, query_tok, slot_of, [back[j] for j in range(chips)])
 
 

time: 73.4 us -> 70.8 us (0.965); the launches traced: 73.2 us -> 71.4 us
  waiting for transfers between devices: 14.9 us -> 5.84 us
  Pallas kernels: 30.7 us -> 38.4 us
    ppermute x15, waiting for transfers between devices: 14.9 us -> 5.84 us  [moved(): return lax.ppermute(x, 'corpus', pairs)]
    pallas_call x5, Pallas kernels: 23.5 us -> 30.8 us  [score(): pl.pallas_call(functools.partial(score_kernel, pieces, slots, query_tok,...]
  transfers between devices with their start and end apart: 17 -> 17, of which waited for: 7 -> 4; matrix products, arithmetic and copies ran while one was open for 0% -> 0% of each run, Pallas kernels for 40% -> 52%
where the time goes in v6:
time: 70.8 us; the launch traced here: 71.4 us
  Pallas kernels  38.4 us (54%)
  starting transfers between devices  22.9 us (32%)
  waiting for transfers between devices  5.84 us (8%)
  local copies, waits for them, and re-layouts  3.53 us (5%)
  between operations  0.78 us (1%)
    pallas_call x5, Pallas kernels, score(): pl.pallas_call(functools.partial(score_kernel, pieces, slots, query_tok,...  30.8 us
    ppermute x15, starting transfers between devices, moved(): return lax.ppermute(x, 'corpus', pairs)  22.2 us
    ppermute x15, waiting for transfers between devices, moved(): return lax.ppermute(x, 'corpus', pairs)  5.84 us
    unnamed x8, local copies, waits for them, and re-layouts  3.5 us
    pallas_call x1, Pallas kernels, ready(): pl.pallas_call(functools.partial(ready_kernel, chips, slots, parts), out_...  2.36 us
    pallas_call x1, Pallas kernels, pack(): pl.pallas_call(functools.partial(pack_kernel, per_owner, chips, slots), o...  2.08 us
    pallas_call x1, Pallas kernels, join(): pl.pallas_call(join_kernel, out_shape=jax.ShapeDtypeStruct((CORES * own.s...  1.94 us
  transfers between devices with their start and end apart: 17, of which 4 were waited for; matrix products, arithmetic and copies ran while one was open for 0% of the time, Pallas kernels for 52%

profile of v6, /device:TPU:0, one launch (start us, length us, event | category | flops | bytes accessed | tf_op | source)
XLA Modules:
  0.0 71.4 jit_solution(3892803341159619187)
XLA Ops:
  0.6 0.5 collective-permute-start.1
  1.1 2.1 %pack.1.refs_1_ = bf16[1808,128]{1,0:T(8,128)(2,1)} custom-call(bf16[1792,128]{1,0:T(8,128)(2,1)} %bitcast.1, s32[1,128]{1,0:T(1,128)} %candidates_in.1), custom_call_target="tpu_custom_call" | custom-call | tf_op jit(solution)/shard_map/pack/pallas_call | solution.py:75
  3.2 2.6 %collective-permute-start.2 = (bf16[1808,128]{1,0:T(8,128)(2,1)}, bf16[1808,128]{1,0:T(8,128)(2,1)S(1)}, u32[]{:S(2)}, u32[]{:S(2)}) collective-permute-start(bf16[1808,128]{1,0:T(8,128)(2,1)} %pack.1.refs_1_), channel_id=1, source_target_pairs={{0,4},{1,5},{4,8},{5,9},{8,12},{9,13},{12,14},{13,15},{14,10},{15,... | collective-permute-start | bytes 1388552 | tf_op jit(solution)/shard_map/ppermute | solution.py:433
  5.9 0.0 collective-permute-start.3
  5.9 0.2 collective-permute-start
  6.1 0.0 copy-start
  6.1 2.2 %copy-done = bf16[128,128,128]{2,1,0:T(8,128)(2,1)S(1)} copy-done((bf16[128,128,128]{2,1,0:T(8,128)(2,1)S(1)}, bf16[128,128,128]{2,1,0:T(8,128)(2,1)}, u32[]{:S(2)}) %copy-start) | copy-done | bytes 4194328
  8.3 0.0 copy-start.2
  8.3 0.7 copy-done.2
  8.9 0.0 copy-start.3
  8.9 0.7 copy-done.3
  9.6 2.4 %ready.1 = (s32[128,128]{1,0:T(8,128)S(1)}, bf16[128,128,128]{2,1,0:T(8,128)(2,1)S(1)}) custom-call(s32[128]{0:T(128)S(1)} %copy-done.3, s32[1,128]{1,0:T(1,128)S(1)} %copy-done.2, bf16[128,128,128]{2,1,0:T(8,128)(2,1)S(1)} %copy-done), custom_call_target="tpu_custom_call" | custom-call | tf_op jit(solution)/shard_map/ready/pallas_call | solution.py:135
  12.0 0.0 collective-permute-done.lens
  12.0 0.0 collective-permute-done.1.other
  12.0 0.0 copy-start.1
  12.0 1.9 %join.1.refs_0_ = bf16[256,128,128]{2,1,0:T(8,128)(2,1)S(1)} custom-call(s32[128]{0:T(128)S(1)} %collective-permute-done.lens, bf16[128,128,128]{2,1,0:T(8,128)(2,1)S(1)} %collective-permute-done.1.other, bf16[128,128,128]{2,1,0:T(8,128)(2,1)S(1)} %get-tuple-element.23.own), custom_call_target="tpu_custom_call" | custom-call | tf_op jit(solution)/shard_map/join/pallas_call | solution.py:163
  13.9 0.0 copy-done.1
  14.0 4.0 %score.5.refs_0_ = f32[24,128]{1,0:T(8,128)S(1)} custom-call(bf16[256,128,128]{2,1,0:T(8,128)(2,1)S(1)} %join.1.refs_0_, bf16[1808,128]{1,0:T(8,128)(2,1)S(1)} %copy-done.1), custom_call_target="tpu_custom_call" | custom-call | flops 4227858432 | bytes 1245184 | tf_op jit(solution)/shard_map/score/pallas_call | solution.py:298
  18.0 0.0 collective-permute-done.2.refs_1_
  18.0 0.8 %collective-permute-done.3.refs_2_ = bf16[1808,128]{1,0:T(8,128)(2,1)S(1)} collective-permute-done((bf16[1808,128]{1,0:T(8,128)(2,1)}, bf16[1808,128]{1,0:T(8,128)(2,1)S(1)}, u32[]{:S(2)}, u32[]{:S(2)}) %collective-permute-start.3) | collective-permute-done | bytes 462880 | tf_op jit(solution)/shard_map/ppermute | solution.py:433
  18.8 1.6 %collective-permute-start.4 = (bf16[1808,128]{1,0:T(8,128)(2,1)S(1)}, bf16[1808,128]{1,0:T(8,128)(2,1)S(1)}, u32[]{:S(2)}, u32[]{:S(2)}) collective-permute-start(bf16[1808,128]{1,0:T(8,128)(2,1)S(1)} %collective-permute-done.2.refs_1_), channel_id=1, source_target_pairs={{0,4},{1,5},{4,8},{5,9},{8,12},{9,13},{12,14},{13,15},{14,10},{15,... | collective-permute-start | bytes 1388552 | tf_op jit(solution)/shard_map/ppermute | solution.py:433
  20.4 0.4 collective-permute-start.5
  20.8 7.4 %score.6 = (f32[24,128]{1,0:T(8,128)S(1)}, f32[24,128]{1,0:T(8,128)S(1)}) custom-call(bf16[256,128,128]{2,1,0:T(8,128)(2,1)S(1)} %join.1.refs_0_, bf16[1808,128]{1,0:T(8,128)(2,1)S(1)} %collective-permute-done.2.refs_1_, bf16[1808,128]{1,0:T(8,128)(2,1)S(1)} %collective-permute-done.3.refs_2_), custom_call_target="tpu_custom_call" | custom-call | flops 8455716864 | bytes 2490368 | tf_op jit(solution)/shard_map/score/pallas_call | solution.py:298
  28.3 0.1 collective-permute-start.6
  28.3 2.0 %collective-permute-start.7 = (f32[24,128]{1,0:T(8,128)S(1)}, f32[24,128]{1,0:T(8,128)S(1)}, u32[]{:S(2)}, u32[]{:S(2)}) collective-permute-start(f32[24,128]{1,0:T(8,128)S(1)} %get-tuple-element.27), channel_id=1, source_target_pairs={{0,4},{1,5},{4,8},{5,9},{8,12},{9,13},{12,14},{13,15},{14,10},{15,... | collective-permute-start | bytes 36872 | tf_op jit(solution)/shard_map/ppermute | solution.py:433
  30.3 1.9 %collective-permute-done.6.refs_1_ = f32[24,128]{1,0:T(8,128)S(1)} collective-permute-done((f32[24,128]{1,0:T(8,128)S(1)}, f32[24,128]{1,0:T(8,128)S(1)}, u32[]{:S(2)}, u32[]{:S(2)}) %collective-permute-start.6) | collective-permute-done | bytes 12320 | tf_op jit(solution)/shard_map/ppermute | solution.py:433
  32.3 0.0 collective-permute-done.7.refs_7_
  32.3 0.0 collective-permute-done.4.refs_1_
  32.3 0.0 collective-permute-done.5.refs_2_
  32.3 1.7 %collective-permute-start.8 = (bf16[1808,128]{1,0:T(8,128)(2,1)S(1)}, bf16[1808,128]{1,0:T(8,128)(2,1)S(1)}, u32[]{:S(2)}, u32[]{:S(2)}) collective-permute-start(bf16[1808,128]{1,0:T(8,128)(2,1)S(1)} %collective-permute-done.4.refs_1_), channel_id=1, source_target_pairs={{0,4},{1,5},{4,8},{5,9},{8,12},{9,13},{12,14},{13,15},{14,10},{15,... | collective-permute-start | bytes 1388552 | tf_op jit(solution)/shard_map/ppermute | solution.py:433
  34.0 0.3 collective-permute-start.9
  34.4 7.4 %score.7 = (f32[24,128]{1,0:T(8,128)S(1)}, f32[24,128]{1,0:T(8,128)S(1)}) custom-call(bf16[256,128,128]{2,1,0:T(8,128)(2,1)S(1)} %join.1.refs_0_, bf16[1808,128]{1,0:T(8,128)(2,1)S(1)} %collective-permute-done.4.refs_1_, bf16[1808,128]{1,0:T(8,128)(2,1)S(1)} %collective-permute-done.5.refs_2_), custom_call_target="tpu_custom_call" | custom-call | flops 8455716864 | bytes 2490368 | tf_op jit(solution)/shard_map/score/pallas_call | solution.py:298
  41.8 2.2 %collective-permute-start.12 = (f32[24,128]{1,0:T(8,128)S(1)}, f32[24,128]{1,0:T(8,128)S(1)}, u32[]{:S(2)}, u32[]{:S(2)}) collective-permute-start(f32[24,128]{1,0:T(8,128)S(1)} %get-tuple-element.31), channel_id=1, source_target_pairs={{0,6},{1,7},{4,2},{5,3},{8,0},{9,1},{12,4},{13,5},{14,8},{15,9},{1... | collective-permute-start | bytes 36872 | tf_op jit(solution)/shard_map/ppermute | solution.py:433
  44.0 0.8 %collective-permute-start.13 = (f32[24,128]{1,0:T(8,128)S(1)}, f32[24,128]{1,0:T(8,128)S(1)}, u32[]{:S(2)}, u32[]{:S(2)}) collective-permute-start(f32[24,128]{1,0:T(8,128)S(1)} %get-tuple-element.32), channel_id=1, source_target_pairs={{0,8},{1,9},{4,12},{5,13},{8,14},{9,15},{12,10},{13,11},{14,6},{15... | collective-permute-start | bytes 36872 | tf_op jit(solution)/shard_map/ppermute | solution.py:433
  44.8 0.0 collective-permute-done.8.refs_1_
  44.8 0.5 collective-permute-done.9.refs_2_
  45.3 2.6 %collective-permute-start.10 = (bf16[896,128]{1,0:T(8,128)(2,1)S(1)}, bf16[896,128]{1,0:T(8,128)(2,1)S(1)}, u32[]{:S(2)}, u32[]{:S(2)}) collective-permute-start(bf16[896,128]{1,0:T(8,128)(2,1)S(1)} %slice.6), channel_id=1, source_target_pairs={{0,4},{1,5},{4,8},{5,9},{8,12},{9,13},{12,14},{13,15},{14,10},{15,... | collective-permute-start | bytes 688136 | tf_op jit(solution)/shard_map/ppermute | solution.py:433
  47.9 0.1 collective-permute-start.11
  48.0 7.9 %score.8 = (f32[24,128]{1,0:T(8,128)S(1)}, f32[24,128]{1,0:T(8,128)S(1)}) custom-call(bf16[256,128,128]{2,1,0:T(8,128)(2,1)S(1)} %join.1.refs_0_, bf16[1808,128]{1,0:T(8,128)(2,1)S(1)} %collective-permute-done.8.refs_1_, bf16[1808,128]{1,0:T(8,128)(2,1)S(1)} %collective-permute-done.9.refs_2_), custom_call_target="tpu_custom_call" | custom-call | flops 8455716864 | bytes 2490368 | tf_op jit(solution)/shard_map/score/pallas_call | solution.py:298
  55.9 0.5 collective-permute-start.14
  56.4 0.0 collective-permute-done.12.refs_2_
  56.4 3.4 %collective-permute-start.16 = (f32[24,128]{1,0:T(8,128)S(1)}, f32[24,128]{1,0:T(8,128)S(1)}, u32[]{:S(2)}, u32[]{:S(2)}) collective-permute-start(f32[24,128]{1,0:T(8,128)S(1)} %get-tuple-element.36), channel_id=1, source_target_pairs={{0,12},{1,13},{4,14},{5,15},{8,10},{9,11},{12,6},{13,7},{14,2},{15... | collective-permute-start | bytes 36872 | tf_op jit(solution)/shard_map/ppermute | solution.py:433
  59.8 0.0 collective-permute-done.13.refs_6_
  59.8 0.0 collective-permute-done.10.refs_1_
  59.8 0.0 collective-permute-done.11.refs_2_
  59.8 4.1 %score.9 = f32[24,128]{1,0:T(8,128)S(1)} custom-call(bf16[256,128,128]{2,1,0:T(8,128)(2,1)S(1)} %join.1.refs_0_, bf16[896,128]{1,0:T(8,128)(2,1)S(1)} %collective-permute-done.10.refs_1_, bf16[912,128]{1,0:T(8,128)(2,1)S(1)} %collective-permute-done.11.refs_2_), custom_call_target="tpu_custom_call" | custom-call | flops 4227858432 | bytes 1245184 | tf_op jit(solution)/shard_map/score/pallas_call | solution.py:298
  63.8 3.8 %collective-permute-start.15 = (f32[24,128]{1,0:T(8,128)S(1)}, f32[24,128]{1,0:T(8,128)S(1)}, u32[]{:S(2)}, u32[]{:S(2)}) collective-permute-start(f32[24,128]{1,0:T(8,128)S(1)} %score.9), channel_id=1, source_target_pairs={{0,14},{1,15},{4,10},{5,11},{8,6},{9,7},{12,2},{13,3},{14,0},{15,1... | collective-permute-start | bytes 36872 | tf_op jit(solution)/shard_map/ppermute | solution.py:433
  67.7 0.0 collective-permute-done.14.refs_3_
  67.7 0.0 collective-permute-done.16.refs_5_
  67.7 2.6 %collective-permute-done.15.refs_4_ = f32[24,128]{1,0:T(8,128)S(1)} collective-permute-done((f32[24,128]{1,0:T(8,128)S(1)}, f32[24,128]{1,0:T(8,128)S(1)}, u32[]{:S(2)}, u32[]{:S(2)}) %collective-permute-start.15) | collective-permute-done | bytes 12320 | tf_op jit(solution)/shard_map/ppermute | solution.py:433
  70.3 1.1 %finish.1 = (f32[56,128]{1,0:T(8,128)}, f32[56,100]{1,0:T(8,128)}) custom-call(s32[128,128]{1,0:T(8,128)S(1)} %get-tuple-element.22.slot_of, f32[24,128]{1,0:T(8,128)S(1)} %score.5.refs_0_, f32[24,128]{1,0:T(8,128)S(1)} %collective-permute-done.6.refs_1_, f32[24,128]{1,0:T(8,128)S(1)} %collective-permute-done.12.refs_2_, ...), custom_call_target="tpu_custom_call" | custom-call | tf_op jit(solution)/shard_map/finish/pallas_call | solution.py:398
  (2 shorter events, 0.0 us)
Async XLA Ops:
  0.6 11.3 %collective-permute-start.1 = (bf16[128,128,128]{2,1,0:T(8,128)(2,1)}, bf16[128,128,128]{2,1,0:T(8,128)(2,1)S(1)}, u32[]{:S(2)}, u32[]{:S(2)}) collective-permute-start(bf16[128,128,128]{2,1,0:T(8,128)(2,1)} %passages.1), channel_id=1, source_target_pairs={{0,1},{1,0},{2,3},{3,2},{4,5},{5,4},{6,7},{7,6},{8,9},{9,8},{10,11... | collective-permute-start | bytes 12582920 | tf_op jit(solution)/shard_map/ppermute | solution.py:436
  3.2 14.8 %collective-permute-start.2 = (bf16[1808,128]{1,0:T(8,128)(2,1)}, bf16[1808,128]{1,0:T(8,128)(2,1)S(1)}, u32[]{:S(2)}, u32[]{:S(2)}) collective-permute-start(bf16[1808,128]{1,0:T(8,128)(2,1)} %pack.1.refs_1_), channel_id=1, source_target_pairs={{0,4},{1,5},{4,8},{5,9},{8,12},{9,13},{12,14},{13,15},{14,10},{15,... | collective-permute-start | bytes 1388552 | tf_op jit(solution)/shard_map/ppermute | solution.py:433
  5.9 12.9 %collective-permute-start.3 = (bf16[1808,128]{1,0:T(8,128)(2,1)}, bf16[1808,128]{1,0:T(8,128)(2,1)S(1)}, u32[]{:S(2)}, u32[]{:S(2)}) collective-permute-start(bf16[1808,128]{1,0:T(8,128)(2,1)} %pack.1.refs_1_), channel_id=1, source_target_pairs={{0,2},{1,3},{4,0},{5,1},{8,4},{9,5},{12,8},{13,9},{14,12},{15,13},... | collective-permute-start | bytes 1388552 | tf_op jit(solution)/shard_map/ppermute | solution.py:433
  5.9 6.1 %collective-permute-start = (s32[128]{0:T(128)}, s32[128]{0:T(128)S(1)}, u32[]{:S(2)}, u32[]{:S(2)}) collective-permute-start(s32[128]{0:T(128)} %lens.1), channel_id=1, source_target_pairs={{0,1},{1,0},{2,3},{3,2},{4,5},{5,4},{6,7},{7,6},{8,9},{9,8},{10,11... | collective-permute-start | bytes 1544 | tf_op jit(solution)/shard_map/ppermute | solution.py:437
  6.1 2.2 %copy-start = (bf16[128,128,128]{2,1,0:T(8,128)(2,1)S(1)}, bf16[128,128,128]{2,1,0:T(8,128)(2,1)}, u32[]{:S(2)}) copy-start(bf16[128,128,128]{2,1,0:T(8,128)(2,1)} %passages.1) | copy-start | bytes 12582916
  8.3 0.7 copy-start.2
  8.9 0.7 copy-start.3
  12.0 2.0 %copy-start.1 = (bf16[1808,128]{1,0:T(8,128)(2,1)S(1)}, bf16[1808,128]{1,0:T(8,128)(2,1)}, u32[]{:S(2)}) copy-start(bf16[1808,128]{1,0:T(8,128)(2,1)} %pack.1.refs_1_) | copy-start | bytes 1388548
  18.8 13.5 %collective-permute-start.4 = (bf16[1808,128]{1,0:T(8,128)(2,1)S(1)}, bf16[1808,128]{1,0:T(8,128)(2,1)S(1)}, u32[]{:S(2)}, u32[]{:S(2)}) collective-permute-start(bf16[1808,128]{1,0:T(8,128)(2,1)S(1)} %collective-permute-done.2.refs_1_), channel_id=1, source_target_pairs={{0,4},{1,5},{4,8},{5,9},{8,12},{9,13},{12,14},{13,15},{14,10},{15,... | collective-permute-start | bytes 1388552 | tf_op jit(solution)/shard_map/ppermute | solution.py:433
  20.4 11.9 %collective-permute-start.5 = (bf16[1808,128]{1,0:T(8,128)(2,1)S(1)}, bf16[1808,128]{1,0:T(8,128)(2,1)S(1)}, u32[]{:S(2)}, u32[]{:S(2)}) collective-permute-start(bf16[1808,128]{1,0:T(8,128)(2,1)S(1)} %collective-permute-done.3.refs_2_), channel_id=1, source_target_pairs={{0,2},{1,3},{4,0},{5,1},{8,4},{9,5},{12,8},{13,9},{14,12},{15,13},... | collective-permute-start | bytes 1388552 | tf_op jit(solution)/shard_map/ppermute | solution.py:433
  28.3 4.0 %collective-permute-start.6 = (f32[24,128]{1,0:T(8,128)S(1)}, f32[24,128]{1,0:T(8,128)S(1)}, u32[]{:S(2)}, u32[]{:S(2)}) collective-permute-start(f32[24,128]{1,0:T(8,128)S(1)} %get-tuple-element.26), channel_id=1, source_target_pairs={{0,2},{1,3},{4,0},{5,1},{8,4},{9,5},{12,8},{13,9},{14,12},{15,13},... | collective-permute-start | bytes 36872 | tf_op jit(solution)/shard_map/ppermute | solution.py:433
  28.3 4.0 %collective-permute-start.7 = (f32[24,128]{1,0:T(8,128)S(1)}, f32[24,128]{1,0:T(8,128)S(1)}, u32[]{:S(2)}, u32[]{:S(2)}) collective-permute-start(f32[24,128]{1,0:T(8,128)S(1)} %get-tuple-element.27), channel_id=1, source_target_pairs={{0,4},{1,5},{4,8},{5,9},{8,12},{9,13},{12,14},{13,15},{14,10},{15,... | collective-permute-start | bytes 36872 | tf_op jit(solution)/shard_map/ppermute | solution.py:433
  32.3 12.5 %collective-permute-start.8 = (bf16[1808,128]{1,0:T(8,128)(2,1)S(1)}, bf16[1808,128]{1,0:T(8,128)(2,1)S(1)}, u32[]{:S(2)}, u32[]{:S(2)}) collective-permute-start(bf16[1808,128]{1,0:T(8,128)(2,1)S(1)} %collective-permute-done.4.refs_1_), channel_id=1, source_target_pairs={{0,4},{1,5},{4,8},{5,9},{8,12},{9,13},{12,14},{13,15},{14,10},{15,... | collective-permute-start | bytes 1388552 | tf_op jit(solution)/shard_map/ppermute | solution.py:433
  34.0 11.2 %collective-permute-start.9 = (bf16[1808,128]{1,0:T(8,128)(2,1)S(1)}, bf16[1808,128]{1,0:T(8,128)(2,1)S(1)}, u32[]{:S(2)}, u32[]{:S(2)}) collective-permute-start(bf16[1808,128]{1,0:T(8,128)(2,1)S(1)} %collective-permute-done.5.refs_2_), channel_id=1, source_target_pairs={{0,2},{1,3},{4,0},{5,1},{8,4},{9,5},{12,8},{13,9},{14,12},{15,13},... | collective-permute-start | bytes 1388552 | tf_op jit(solution)/shard_map/ppermute | solution.py:433
  41.8 14.6 %collective-permute-start.12 = (f32[24,128]{1,0:T(8,128)S(1)}, f32[24,128]{1,0:T(8,128)S(1)}, u32[]{:S(2)}, u32[]{:S(2)}) collective-permute-start(f32[24,128]{1,0:T(8,128)S(1)} %get-tuple-element.31), channel_id=1, source_target_pairs={{0,6},{1,7},{4,2},{5,3},{8,0},{9,1},{12,4},{13,5},{14,8},{15,9},{1... | collective-permute-start | bytes 36872 | tf_op jit(solution)/shard_map/ppermute | solution.py:433
  44.0 15.8 %collective-permute-start.13 = (f32[24,128]{1,0:T(8,128)S(1)}, f32[24,128]{1,0:T(8,128)S(1)}, u32[]{:S(2)}, u32[]{:S(2)}) collective-permute-start(f32[24,128]{1,0:T(8,128)S(1)} %get-tuple-element.32), channel_id=1, source_target_pairs={{0,8},{1,9},{4,12},{5,13},{8,14},{9,15},{12,10},{13,11},{14,6},{15... | collective-permute-start | bytes 36872 | tf_op jit(solution)/shard_map/ppermute | solution.py:433
  45.3 14.5 %collective-permute-start.10 = (bf16[896,128]{1,0:T(8,128)(2,1)S(1)}, bf16[896,128]{1,0:T(8,128)(2,1)S(1)}, u32[]{:S(2)}, u32[]{:S(2)}) collective-permute-start(bf16[896,128]{1,0:T(8,128)(2,1)S(1)} %slice.6), channel_id=1, source_target_pairs={{0,4},{1,5},{4,8},{5,9},{8,12},{9,13},{12,14},{13,15},{14,10},{15,... | collective-permute-start | bytes 688136 | tf_op jit(solution)/shard_map/ppermute | solution.py:433
  47.9 11.9 %collective-permute-start.11 = (bf16[912,128]{1,0:T(8,128)(2,1)S(1)}, bf16[912,128]{1,0:T(8,128)(2,1)S(1)}, u32[]{:S(2)}, u32[]{:S(2)}) collective-permute-start(bf16[912,128]{1,0:T(8,128)(2,1)S(1)} %slice.7), channel_id=1, source_target_pairs={{0,2},{1,3},{4,0},{5,1},{8,4},{9,5},{12,8},{13,9},{14,12},{15,13},... | collective-permute-start | bytes 700424 | tf_op jit(solution)/shard_map/ppermute | solution.py:433
  55.9 11.8 %collective-permute-start.14 = (f32[24,128]{1,0:T(8,128)S(1)}, f32[24,128]{1,0:T(8,128)S(1)}, u32[]{:S(2)}, u32[]{:S(2)}) collective-permute-start(f32[24,128]{1,0:T(8,128)S(1)} %get-tuple-element.35), channel_id=1, source_target_pairs={{0,10},{1,11},{4,6},{5,7},{8,2},{9,3},{12,0},{13,1},{14,4},{15,5},... | collective-permute-start | bytes 36872 | tf_op jit(solution)/shard_map/ppermute | solution.py:433
  56.4 11.3 %collective-permute-start.16 = (f32[24,128]{1,0:T(8,128)S(1)}, f32[24,128]{1,0:T(8,128)S(1)}, u32[]{:S(2)}, u32[]{:S(2)}) collective-permute-start(f32[24,128]{1,0:T(8,128)S(1)} %get-tuple-element.36), channel_id=1, source_target_pairs={{0,12},{1,13},{4,14},{5,15},{8,10},{9,11},{12,6},{13,7},{14,2},{15... | collective-permute-start | bytes 36872 | tf_op jit(solution)/shard_map/ppermute | solution.py:433
  63.8 6.5 %collective-permute-start.15 = (f32[24,128]{1,0:T(8,128)S(1)}, f32[24,128]{1,0:T(8,128)S(1)}, u32[]{:S(2)}, u32[]{:S(2)}) collective-permute-start(f32[24,128]{1,0:T(8,128)S(1)} %score.9), channel_id=1, source_target_pairs={{0,14},{1,15},{4,10},{5,11},{8,6},{9,7},{12,2},{13,3},{14,0},{15,1... | collective-permute-start | bytes 36872 | tf_op jit(solution)/shard_map/ppermute | solution.py:433

commit v7 on v6

--- a/solution.py
+++ b/solution.py
@@ -12,6 +12,7 @@
 LANES = 128
 GROUP = 8
 VMEM_LIMIT = 32 * 1024 * 1024
+READY_LIMIT = 48 * 1024 * 1024
 
 
 def ring_order(chips):
@@ -30,18 +31,21 @@
     return high, middle, low
 
 
-def pack_kernel(per_owner, chips, slots, queries_in, candidates_in, block, queries, candidates, sems):
+def pack_kernel(per_owner, chips, slots, queries_in, candidates_in, out, queries, candidates, block, in_sems, out_sems):
+    query_rows = queries.shape[0]
+    half = query_rows // LANES // 2 * LANES
+    spans = [(0, half), (half, query_rows - half)]
+    listed = pltpu.make_async_copy(candidates_in, candidates, in_sems.at[2])
+    listed.start()
     loads = [
-        pltpu.make_async_copy(queries_in, queries, sems.at[0]),
-        pltpu.make_async_copy(candidates_in, candidates, sems.at[1]),
+        pltpu.make_async_copy(
+            queries_in.at[pl.ds(at, rows)], queries.at[pl.ds(at, rows)], in_sems.at[i]
+        )
+        for i, (at, rows) in enumerate(spans)
     ]
     for load in loads:
         load.start()
-    for load in loads:
-        load.wait()
-    query_rows = queries.shape[0]
-    for at in range(0, query_rows, LANES):
-        block[at : at + LANES, :] = queries[at : at + LANES, :].T
+    listed.wait()
     fact_rows = block.shape[0] - query_rows
     number = candidates.shape[1]
     per_chip = CORES * per_owner
@@ -64,6 +68,19 @@
         found = jnp.sum(jnp.where(rank == float(s), tile, 0.0), axis=1, keepdims=True)
         wanted = jnp.where(lane == s, found, wanted)
     block[query_rows:, :] = wanted.astype(jnp.bfloat16)
+    stores = []
+    for i, (at, rows) in enumerate(spans):
+        loads[i].wait()
+        for row_at in range(at, at + rows, LANES):
+            block[row_at : row_at + LANES, :] = queries[row_at : row_at + LANES, :].T
+        if i:
+            rows += fact_rows
+        stores.append(
+            pltpu.make_async_copy(block.at[pl.ds(at, rows)], out.at[pl.ds(at, rows)], out_sems.at[i])
+        )
+        stores[-1].start()
+    for store in stores:
+        store.wait()
 
 
 def fact_rows_of(chips):
@@ -76,10 +93,12 @@
         functools.partial(pack_kernel, per_owner, chips, slots),
         out_shape=jax.ShapeDtypeStruct((rows + fact_rows_of(chips), feature), queries.dtype),
         in_specs=[pl.BlockSpec(memory_space=pl.ANY)] * 2,
-        out_specs=pl.BlockSpec(memory_space=pltpu.VMEM),
+        out_specs=pl.BlockSpec(memory_space=pl.ANY),
         scratch_shapes=[
             pltpu.VMEM(queries.shape, queries.dtype),
             pltpu.VMEM(candidates.shape, candidates.dtype),
+            pltpu.VMEM((rows + fact_rows_of(chips), feature), queries.dtype),
+            pltpu.SemaphoreType.DMA((3,)),
             pltpu.SemaphoreType.DMA((2,)),
         ],
         compiler_params=pltpu.CompilerParams(vmem_limit_bytes=56 * 1024 * 1024),
@@ -145,7 +164,7 @@
         ],
         out_specs=(pl.BlockSpec(memory_space=pltpu.VMEM),) * 2,
         scratch_shapes=[pltpu.SemaphoreType.DMA((parts,))],
-        compiler_params=pltpu.CompilerParams(vmem_limit_bytes=VMEM_LIMIT),
+        compiler_params=pltpu.CompilerParams(vmem_limit_bytes=READY_LIMIT),
         name="ready",
     )(lengths, candidates, passages)
 
@@ -236,13 +255,17 @@
     for load in loads:
         load.start()
     to_scalar.wait()
-    for load in loads:
-        load.wait()
 
     slot_row = lax.broadcasted_iota(jnp.int32, (slots, LANES), 0)
 
     def score_block(b, carry):
         count = plan[b, slots]
+        for k in range(blocks):
+
+            @pl.when(b == k)
+            def _(k=k):
+                for load in loads[sum(pieces[:k]) : sum(pieces[: k + 1])]:
+                    load.wait()
 
         def score_tiles(first, number):
             left = jnp.concatenate([tiles[plan[b, first + t]] for t in range(number)], axis=0)

time: 70.8 us -> 69.9 us (0.987); the launches traced: 71.4 us -> 69.7 us
  Pallas kernels: 38.4 us -> 33 us
  starting transfers between devices: 22.9 us -> 27.5 us
  local copies, waits for them, and re-layouts: 3.53 us -> 1.35 us
  waiting for transfers between devices: 5.84 us -> 7.11 us
    pallas_call x5, Pallas kernels: 30.8 us -> 24.9 us  [score(): pl.pallas_call(functools.partial(score_kernel, pieces, slots, query_tok,...]
    ppermute x15, starting transfers between devices: 22.2 us -> 26.7 us  [moved(): return lax.ppermute(x, 'corpus', pairs)]
    unnamed x8 -> x6, local copies, waits for them, and re-layouts: 3.5 us -> 1.31 us
    ppermute x15, waiting for transfers between devices: 5.84 us -> 7.11 us  [moved(): return lax.ppermute(x, 'corpus', pairs)]
    pallas_call x1, Pallas kernels: 2.36 us -> 3.11 us  [ready(): pl.pallas_call(functools.partial(ready_kernel, chips, slots, parts), out_...]
  transfers between devices with their start and end apart: 17 -> 17, of which waited for: 4 -> 5; matrix products, arithmetic and copies ran while one was open for 0% -> 0% of each run, Pallas kernels for 52% -> 46%
where the time goes in v7:
time: 69.9 us; the launch traced here: 69.7 us
  Pallas kernels  33 us (47%)
  starting transfers between devices  27.5 us (39%)
  waiting for transfers between devices  7.11 us (10%)
  local copies, waits for them, and re-layouts  1.35 us (2%)
  between operations  0.77 us (1%)
    ppermute x15, starting transfers between devices, moved(): return lax.ppermute(x, 'corpus', pairs)  26.7 us
    pallas_call x5, Pallas kernels, score(): pl.pallas_call(functools.partial(score_kernel, pieces, slots, query_tok,...  24.9 us
    ppermute x15, waiting for transfers between devices, moved(): return lax.ppermute(x, 'corpus', pairs)  7.11 us
    pallas_call x1, Pallas kernels, ready(): pl.pallas_call(functools.partial(ready_kernel, chips, slots, parts), out_...  3.11 us
    pallas_call x1, Pallas kernels, join(): pl.pallas_call(join_kernel, out_shape=jax.ShapeDtypeStruct((CORES * own.s...  1.94 us
    pallas_call x1, Pallas kernels, pack(): pl.pallas_call(functools.partial(pack_kernel, per_owner, chips, slots), o...  1.93 us
  transfers between devices with their start and end apart: 17, of which 5 were waited for; matrix products, arithmetic and copies ran while one was open for 0% of the time, Pallas kernels for 46%

profile of v7, /device:TPU:0, one launch (start us, length us, event | category | flops | bytes accessed | tf_op | source)
XLA Modules:
  0.0 69.7 jit_solution(7452070677589569346)
XLA Ops:
  0.6 0.5 collective-permute-start.1
  1.1 1.9 %pack.1.refs_1_ = bf16[1808,128]{1,0:T(8,128)(2,1)} custom-call(bf16[1792,128]{1,0:T(8,128)(2,1)} %bitcast.1, s32[1,128]{1,0:T(1,128)} %candidates_in.1), custom_call_target="tpu_custom_call" | custom-call | tf_op jit(solution)/shard_map/pack/pallas_call | solution.py:92
  3.1 2.6 %collective-permute-start.2 = (bf16[1808,128]{1,0:T(8,128)(2,1)}, bf16[1808,128]{1,0:T(8,128)(2,1)S(1)}, u32[]{:S(2)}, u32[]{:S(2)}) collective-permute-start(bf16[1808,128]{1,0:T(8,128)(2,1)} %pack.1.refs_1_), channel_id=1, source_target_pairs={{0,4},{1,5},{4,8},{5,9},{8,12},{9,13},{12,14},{13,15},{14,10},{15,... | collective-permute-start | bytes 1388552 | tf_op jit(solution)/shard_map/ppermute | solution.py:456
  5.7 0.0 collective-permute-start.3
  5.7 0.2 collective-permute-start
  5.9 0.0 copy-start.1
  5.9 0.7 copy-done.1
  6.6 0.0 copy-start.2
  6.6 0.7 copy-done.2
  7.3 3.1 %ready.1 = (s32[128,128]{1,0:T(8,128)S(1)}, bf16[128,128,128]{2,1,0:T(8,128)(2,1)S(1)}) custom-call(s32[128]{0:T(128)S(1)} %copy-done.2, s32[1,128]{1,0:T(1,128)S(1)} %copy-done.1, bf16[128,128,128]{2,1,0:T(8,128)(2,1)} %passages.1), custom_call_target="tpu_custom_call" | custom-call | tf_op jit(solution)/shard_map/ready/pallas_call | solution.py:154
  10.4 0.0 collective-permute-done.lens
  10.4 0.0 collective-permute-done.1.other
  10.4 0.0 copy-start
  10.4 1.9 %join.1.refs_0_ = bf16[256,128,128]{2,1,0:T(8,128)(2,1)S(1)} custom-call(s32[128]{0:T(128)S(1)} %collective-permute-done.lens, bf16[128,128,128]{2,1,0:T(8,128)(2,1)S(1)} %collective-permute-done.1.other, bf16[128,128,128]{2,1,0:T(8,128)(2,1)S(1)} %get-tuple-element.23.own), custom_call_target="tpu_custom_call" | custom-call | tf_op jit(solution)/shard_map/join/pallas_call | solution.py:182
  12.4 0.0 copy-done
  12.4 3.4 %score.5.refs_0_ = f32[24,128]{1,0:T(8,128)S(1)} custom-call(bf16[256,128,128]{2,1,0:T(8,128)(2,1)S(1)} %join.1.refs_0_, bf16[1808,128]{1,0:T(8,128)(2,1)S(1)} %copy-done), custom_call_target="tpu_custom_call" | custom-call | flops 4227858432 | bytes 1245184 | tf_op jit(solution)/shard_map/score/pallas_call | solution.py:321
  15.8 1.3 %collective-permute-done.2.refs_1_ = bf16[1808,128]{1,0:T(8,128)(2,1)S(1)} collective-permute-done((bf16[1808,128]{1,0:T(8,128)(2,1)}, bf16[1808,128]{1,0:T(8,128)(2,1)S(1)}, u32[]{:S(2)}, u32[]{:S(2)}) %collective-permute-start.2) | collective-permute-done | bytes 462880 | tf_op jit(solution)/shard_map/ppermute | solution.py:456
  17.1 1.5 %collective-permute-done.3.refs_2_ = bf16[1808,128]{1,0:T(8,128)(2,1)S(1)} collective-permute-done((bf16[1808,128]{1,0:T(8,128)(2,1)}, bf16[1808,128]{1,0:T(8,128)(2,1)S(1)}, u32[]{:S(2)}, u32[]{:S(2)}) %collective-permute-start.3) | collective-permute-done | bytes 462880 | tf_op jit(solution)/shard_map/ppermute | solution.py:456
  18.7 1.6 %collective-permute-start.4 = (bf16[1808,128]{1,0:T(8,128)(2,1)S(1)}, bf16[1808,128]{1,0:T(8,128)(2,1)S(1)}, u32[]{:S(2)}, u32[]{:S(2)}) collective-permute-start(bf16[1808,128]{1,0:T(8,128)(2,1)S(1)} %collective-permute-done.2.refs_1_), channel_id=1, source_target_pairs={{0,4},{1,5},{4,8},{5,9},{8,12},{9,13},{12,14},{13,15},{14,10},{15,... | collective-permute-start | bytes 1388552 | tf_op jit(solution)/shard_map/ppermute | solution.py:456
  20.2 0.4 collective-permute-start.5
  20.7 6.2 %score.6 = (f32[24,128]{1,0:T(8,128)S(1)}, f32[24,128]{1,0:T(8,128)S(1)}) custom-call(bf16[256,128,128]{2,1,0:T(8,128)(2,1)S(1)} %join.1.refs_0_, bf16[1808,128]{1,0:T(8,128)(2,1)S(1)} %collective-permute-done.2.refs_1_, bf16[1808,128]{1,0:T(8,128)(2,1)S(1)} %collective-permute-done.3.refs_2_), custom_call_target="tpu_custom_call" | custom-call | flops 8455716864 | bytes 2490368 | tf_op jit(solution)/shard_map/score/pallas_call | solution.py:321
  26.9 0.5 collective-permute-start.6
  27.4 2.4 %collective-permute-start.7 = (f32[24,128]{1,0:T(8,128)S(1)}, f32[24,128]{1,0:T(8,128)S(1)}, u32[]{:S(2)}, u32[]{:S(2)}) collective-permute-start(f32[24,128]{1,0:T(8,128)S(1)} %get-tuple-element.27), channel_id=1, source_target_pairs={{0,4},{1,5},{4,8},{5,9},{8,12},{9,13},{12,14},{13,15},{14,10},{15,... | collective-permute-start | bytes 36872 | tf_op jit(solution)/shard_map/ppermute | solution.py:456
  29.8 2.3 %collective-permute-done.6.refs_1_ = f32[24,128]{1,0:T(8,128)S(1)} collective-permute-done((f32[24,128]{1,0:T(8,128)S(1)}, f32[24,128]{1,0:T(8,128)S(1)}, u32[]{:S(2)}, u32[]{:S(2)}) %collective-permute-start.6) | collective-permute-done | bytes 12320 | tf_op jit(solution)/shard_map/ppermute | solution.py:456
  32.1 0.0 collective-permute-done.7.refs_7_
  32.1 0.0 collective-permute-done.4.refs_1_
  32.1 0.0 collective-permute-done.5.refs_2_
  32.1 1.6 %collective-permute-start.8 = (bf16[1808,128]{1,0:T(8,128)(2,1)S(1)}, bf16[1808,128]{1,0:T(8,128)(2,1)S(1)}, u32[]{:S(2)}, u32[]{:S(2)}) collective-permute-start(bf16[1808,128]{1,0:T(8,128)(2,1)S(1)} %collective-permute-done.4.refs_1_), channel_id=1, source_target_pairs={{0,4},{1,5},{4,8},{5,9},{8,12},{9,13},{12,14},{13,15},{14,10},{15,... | collective-permute-start | bytes 1388552 | tf_op jit(solution)/shard_map/ppermute | solution.py:456
  33.8 0.4 collective-permute-start.9
  34.2 6.2 %score.7 = (f32[24,128]{1,0:T(8,128)S(1)}, f32[24,128]{1,0:T(8,128)S(1)}) custom-call(bf16[256,128,128]{2,1,0:T(8,128)(2,1)S(1)} %join.1.refs_0_, bf16[1808,128]{1,0:T(8,128)(2,1)S(1)} %collective-permute-done.4.refs_1_, bf16[1808,128]{1,0:T(8,128)(2,1)S(1)} %collective-permute-done.5.refs_2_), custom_call_target="tpu_custom_call" | custom-call | flops 8455716864 | bytes 2490368 | tf_op jit(solution)/shard_map/score/pallas_call | solution.py:321
  40.4 4.0 %collective-permute-start.12 = (f32[24,128]{1,0:T(8,128)S(1)}, f32[24,128]{1,0:T(8,128)S(1)}, u32[]{:S(2)}, u32[]{:S(2)}) collective-permute-start(f32[24,128]{1,0:T(8,128)S(1)} %get-tuple-element.31), channel_id=1, source_target_pairs={{0,6},{1,7},{4,2},{5,3},{8,0},{9,1},{12,4},{13,5},{14,8},{15,9},{1... | collective-permute-start | bytes 36872 | tf_op jit(solution)/shard_map/ppermute | solution.py:456
  44.4 0.0 collective-permute-start.13
  44.4 0.0 collective-permute-done.8.refs_1_
  44.4 0.2 collective-permute-done.9.refs_2_
  44.7 1.7 %collective-permute-start.10 = (bf16[896,128]{1,0:T(8,128)(2,1)S(1)}, bf16[896,128]{1,0:T(8,128)(2,1)S(1)}, u32[]{:S(2)}, u32[]{:S(2)}) collective-permute-start(bf16[896,128]{1,0:T(8,128)(2,1)S(1)} %slice.6), channel_id=1, source_target_pairs={{0,4},{1,5},{4,8},{5,9},{8,12},{9,13},{12,14},{13,15},{14,10},{15,... | collective-permute-start | bytes 688136 | tf_op jit(solution)/shard_map/ppermute | solution.py:456
  46.4 0.4 collective-permute-start.11
  46.8 5.7 %score.8 = (f32[24,128]{1,0:T(8,128)S(1)}, f32[24,128]{1,0:T(8,128)S(1)}) custom-call(bf16[256,128,128]{2,1,0:T(8,128)(2,1)S(1)} %join.1.refs_0_, bf16[1808,128]{1,0:T(8,128)(2,1)S(1)} %collective-permute-done.8.refs_1_, bf16[1808,128]{1,0:T(8,128)(2,1)S(1)} %collective-permute-done.9.refs_2_), custom_call_target="tpu_custom_call" | custom-call | flops 8455716864 | bytes 2490368 | tf_op jit(solution)/shard_map/score/pallas_call | solution.py:321
  52.5 4.0 %collective-permute-start.14 = (f32[24,128]{1,0:T(8,128)S(1)}, f32[24,128]{1,0:T(8,128)S(1)}, u32[]{:S(2)}, u32[]{:S(2)}) collective-permute-start(f32[24,128]{1,0:T(8,128)S(1)} %get-tuple-element.35), channel_id=1, source_target_pairs={{0,10},{1,11},{4,6},{5,7},{8,2},{9,3},{12,0},{13,1},{14,4},{15,5},... | collective-permute-start | bytes 36872 | tf_op jit(solution)/shard_map/ppermute | solution.py:456
  56.5 0.0 collective-permute-done.12.refs_2_
  56.5 0.0 collective-permute-start.16
  56.5 0.0 collective-permute-done.13.refs_6_
  56.5 0.0 collective-permute-done.10.refs_1_
  56.6 0.0 collective-permute-done.11.refs_2_
  56.6 3.4 %score.9 = f32[24,128]{1,0:T(8,128)S(1)} custom-call(bf16[256,128,128]{2,1,0:T(8,128)(2,1)S(1)} %join.1.refs_0_, bf16[896,128]{1,0:T(8,128)(2,1)S(1)} %collective-permute-done.10.refs_1_, bf16[912,128]{1,0:T(8,128)(2,1)S(1)} %collective-permute-done.11.refs_2_), custom_call_target="tpu_custom_call" | custom-call | flops 4227858432 | bytes 1245184 | tf_op jit(solution)/shard_map/score/pallas_call | solution.py:321
  60.0 6.9 %collective-permute-start.15 = (f32[24,128]{1,0:T(8,128)S(1)}, f32[24,128]{1,0:T(8,128)S(1)}, u32[]{:S(2)}, u32[]{:S(2)}) collective-permute-start(f32[24,128]{1,0:T(8,128)S(1)} %score.9), channel_id=1, source_target_pairs={{0,14},{1,15},{4,10},{5,11},{8,6},{9,7},{12,2},{13,3},{14,0},{15,1... | collective-permute-start | bytes 36872 | tf_op jit(solution)/shard_map/ppermute | solution.py:456
  66.9 0.0 collective-permute-done.14.refs_3_
  66.9 0.0 collective-permute-done.16.refs_5_
  66.9 1.7 %collective-permute-done.15.refs_4_ = f32[24,128]{1,0:T(8,128)S(1)} collective-permute-done((f32[24,128]{1,0:T(8,128)S(1)}, f32[24,128]{1,0:T(8,128)S(1)}, u32[]{:S(2)}, u32[]{:S(2)}) %collective-permute-start.15) | collective-permute-done | bytes 12320 | tf_op jit(solution)/shard_map/ppermute | solution.py:456
  68.5 1.1 %finish.1 = (f32[56,128]{1,0:T(8,128)}, f32[56,100]{1,0:T(8,128)}) custom-call(s32[128,128]{1,0:T(8,128)S(1)} %get-tuple-element.22.slot_of, f32[24,128]{1,0:T(8,128)S(1)} %score.5.refs_0_, f32[24,128]{1,0:T(8,128)S(1)} %collective-permute-done.6.refs_1_, f32[24,128]{1,0:T(8,128)S(1)} %collective-permute-done.12.refs_2_, ...), custom_call_target="tpu_custom_call" | custom-call | tf_op jit(solution)/shard_map/finish/pallas_call | solution.py:421
  (2 shorter events, 0.0 us)
Async XLA Ops:
  0.6 9.8 %collective-permute-start.1 = (bf16[128,128,128]{2,1,0:T(8,128)(2,1)}, bf16[128,128,128]{2,1,0:T(8,128)(2,1)S(1)}, u32[]{:S(2)}, u32[]{:S(2)}) collective-permute-start(bf16[128,128,128]{2,1,0:T(8,128)(2,1)} %passages.1), channel_id=1, source_target_pairs={{0,1},{1,0},{2,3},{3,2},{4,5},{5,4},{6,7},{7,6},{8,9},{9,8},{10,11... | collective-permute-start | bytes 12582920 | tf_op jit(solution)/shard_map/ppermute | solution.py:459
  3.1 14.1 %collective-permute-start.2 = (bf16[1808,128]{1,0:T(8,128)(2,1)}, bf16[1808,128]{1,0:T(8,128)(2,1)S(1)}, u32[]{:S(2)}, u32[]{:S(2)}) collective-permute-start(bf16[1808,128]{1,0:T(8,128)(2,1)} %pack.1.refs_1_), channel_id=1, source_target_pairs={{0,4},{1,5},{4,8},{5,9},{8,12},{9,13},{12,14},{13,15},{14,10},{15,... | collective-permute-start | bytes 1388552 | tf_op jit(solution)/shard_map/ppermute | solution.py:456
  5.7 12.9 %collective-permute-start.3 = (bf16[1808,128]{1,0:T(8,128)(2,1)}, bf16[1808,128]{1,0:T(8,128)(2,1)S(1)}, u32[]{:S(2)}, u32[]{:S(2)}) collective-permute-start(bf16[1808,128]{1,0:T(8,128)(2,1)} %pack.1.refs_1_), channel_id=1, source_target_pairs={{0,2},{1,3},{4,0},{5,1},{8,4},{9,5},{12,8},{13,9},{14,12},{15,13},... | collective-permute-start | bytes 1388552 | tf_op jit(solution)/shard_map/ppermute | solution.py:456
  5.7 4.6 %collective-permute-start = (s32[128]{0:T(128)}, s32[128]{0:T(128)S(1)}, u32[]{:S(2)}, u32[]{:S(2)}) collective-permute-start(s32[128]{0:T(128)} %lens.1), channel_id=1, source_target_pairs={{0,1},{1,0},{2,3},{3,2},{4,5},{5,4},{6,7},{7,6},{8,9},{9,8},{10,11... | collective-permute-start | bytes 1544 | tf_op jit(solution)/shard_map/ppermute | solution.py:460
  5.9 0.7 copy-start.1
  6.6 0.7 copy-start.2
  10.4 2.0 %copy-start = (bf16[1808,128]{1,0:T(8,128)(2,1)S(1)}, bf16[1808,128]{1,0:T(8,128)(2,1)}, u32[]{:S(2)}) copy-start(bf16[1808,128]{1,0:T(8,128)(2,1)} %pack.1.refs_1_) | copy-start | bytes 1388548
  18.7 13.5 %collective-permute-start.4 = (bf16[1808,128]{1,0:T(8,128)(2,1)S(1)}, bf16[1808,128]{1,0:T(8,128)(2,1)S(1)}, u32[]{:S(2)}, u32[]{:S(2)}) collective-permute-start(bf16[1808,128]{1,0:T(8,128)(2,1)S(1)} %collective-permute-done.2.refs_1_), channel_id=1, source_target_pairs={{0,4},{1,5},{4,8},{5,9},{8,12},{9,13},{12,14},{13,15},{14,10},{15,... | collective-permute-start | bytes 1388552 | tf_op jit(solution)/shard_map/ppermute | solution.py:456
  20.2 11.9 %collective-permute-start.5 = (bf16[1808,128]{1,0:T(8,128)(2,1)S(1)}, bf16[1808,128]{1,0:T(8,128)(2,1)S(1)}, u32[]{:S(2)}, u32[]{:S(2)}) collective-permute-start(bf16[1808,128]{1,0:T(8,128)(2,1)S(1)} %collective-permute-done.3.refs_2_), channel_id=1, source_target_pairs={{0,2},{1,3},{4,0},{5,1},{8,4},{9,5},{12,8},{13,9},{14,12},{15,13},... | collective-permute-start | bytes 1388552 | tf_op jit(solution)/shard_map/ppermute | solution.py:456
  26.9 5.3 %collective-permute-start.6 = (f32[24,128]{1,0:T(8,128)S(1)}, f32[24,128]{1,0:T(8,128)S(1)}, u32[]{:S(2)}, u32[]{:S(2)}) collective-permute-start(f32[24,128]{1,0:T(8,128)S(1)} %get-tuple-element.26), channel_id=1, source_target_pairs={{0,2},{1,3},{4,0},{5,1},{8,4},{9,5},{12,8},{13,9},{14,12},{15,13},... | collective-permute-start | bytes 36872 | tf_op jit(solution)/shard_map/ppermute | solution.py:456
  27.4 4.8 %collective-permute-start.7 = (f32[24,128]{1,0:T(8,128)S(1)}, f32[24,128]{1,0:T(8,128)S(1)}, u32[]{:S(2)}, u32[]{:S(2)}) collective-permute-start(f32[24,128]{1,0:T(8,128)S(1)} %get-tuple-element.27), channel_id=1, source_target_pairs={{0,4},{1,5},{4,8},{5,9},{8,12},{9,13},{12,14},{13,15},{14,10},{15,... | collective-permute-start | bytes 36872 | tf_op jit(solution)/shard_map/ppermute | solution.py:456
  32.1 12.3 %collective-permute-start.8 = (bf16[1808,128]{1,0:T(8,128)(2,1)S(1)}, bf16[1808,128]{1,0:T(8,128)(2,1)S(1)}, u32[]{:S(2)}, u32[]{:S(2)}) collective-permute-start(bf16[1808,128]{1,0:T(8,128)(2,1)S(1)} %collective-permute-done.4.refs_1_), channel_id=1, source_target_pairs={{0,4},{1,5},{4,8},{5,9},{8,12},{9,13},{12,14},{13,15},{14,10},{15,... | collective-permute-start | bytes 1388552 | tf_op jit(solution)/shard_map/ppermute | solution.py:456
  33.8 10.9 %collective-permute-start.9 = (bf16[1808,128]{1,0:T(8,128)(2,1)S(1)}, bf16[1808,128]{1,0:T(8,128)(2,1)S(1)}, u32[]{:S(2)}, u32[]{:S(2)}) collective-permute-start(bf16[1808,128]{1,0:T(8,128)(2,1)S(1)} %collective-permute-done.5.refs_2_), channel_id=1, source_target_pairs={{0,2},{1,3},{4,0},{5,1},{8,4},{9,5},{12,8},{13,9},{14,12},{15,13},... | collective-permute-start | bytes 1388552 | tf_op jit(solution)/shard_map/ppermute | solution.py:456
  40.4 16.1 %collective-permute-start.12 = (f32[24,128]{1,0:T(8,128)S(1)}, f32[24,128]{1,0:T(8,128)S(1)}, u32[]{:S(2)}, u32[]{:S(2)}) collective-permute-start(f32[24,128]{1,0:T(8,128)S(1)} %get-tuple-element.31), channel_id=1, source_target_pairs={{0,6},{1,7},{4,2},{5,3},{8,0},{9,1},{12,4},{13,5},{14,8},{15,9},{1... | collective-permute-start | bytes 36872 | tf_op jit(solution)/shard_map/ppermute | solution.py:456
  44.4 12.1 %collective-permute-start.13 = (f32[24,128]{1,0:T(8,128)S(1)}, f32[24,128]{1,0:T(8,128)S(1)}, u32[]{:S(2)}, u32[]{:S(2)}) collective-permute-start(f32[24,128]{1,0:T(8,128)S(1)} %get-tuple-element.32), channel_id=1, source_target_pairs={{0,8},{1,9},{4,12},{5,13},{8,14},{9,15},{12,10},{13,11},{14,6},{15... | collective-permute-start | bytes 36872 | tf_op jit(solution)/shard_map/ppermute | solution.py:456
  44.7 11.9 %collective-permute-start.10 = (bf16[896,128]{1,0:T(8,128)(2,1)S(1)}, bf16[896,128]{1,0:T(8,128)(2,1)S(1)}, u32[]{:S(2)}, u32[]{:S(2)}) collective-permute-start(bf16[896,128]{1,0:T(8,128)(2,1)S(1)} %slice.6), channel_id=1, source_target_pairs={{0,4},{1,5},{4,8},{5,9},{8,12},{9,13},{12,14},{13,15},{14,10},{15,... | collective-permute-start | bytes 688136 | tf_op jit(solution)/shard_map/ppermute | solution.py:456
  46.4 10.1 %collective-permute-start.11 = (bf16[912,128]{1,0:T(8,128)(2,1)S(1)}, bf16[912,128]{1,0:T(8,128)(2,1)S(1)}, u32[]{:S(2)}, u32[]{:S(2)}) collective-permute-start(bf16[912,128]{1,0:T(8,128)(2,1)S(1)} %slice.7), channel_id=1, source_target_pairs={{0,2},{1,3},{4,0},{5,1},{8,4},{9,5},{12,8},{13,9},{14,12},{15,13},... | collective-permute-start | bytes 700424 | tf_op jit(solution)/shard_map/ppermute | solution.py:456
  52.5 14.3 %collective-permute-start.14 = (f32[24,128]{1,0:T(8,128)S(1)}, f32[24,128]{1,0:T(8,128)S(1)}, u32[]{:S(2)}, u32[]{:S(2)}) collective-permute-start(f32[24,128]{1,0:T(8,128)S(1)} %get-tuple-element.35), channel_id=1, source_target_pairs={{0,10},{1,11},{4,6},{5,7},{8,2},{9,3},{12,0},{13,1},{14,4},{15,5},... | collective-permute-start | bytes 36872 | tf_op jit(solution)/shard_map/ppermute | solution.py:456
  56.5 10.3 %collective-permute-start.16 = (f32[24,128]{1,0:T(8,128)S(1)}, f32[24,128]{1,0:T(8,128)S(1)}, u32[]{:S(2)}, u32[]{:S(2)}) collective-permute-start(f32[24,128]{1,0:T(8,128)S(1)} %get-tuple-element.36), channel_id=1, source_target_pairs={{0,12},{1,13},{4,14},{5,15},{8,10},{9,11},{12,6},{13,7},{14,2},{15... | collective-permute-start | bytes 36872 | tf_op jit(solution)/shard_map/ppermute | solution.py:456
  60.0 8.5 %collective-permute-start.15 = (f32[24,128]{1,0:T(8,128)S(1)}, f32[24,128]{1,0:T(8,128)S(1)}, u32[]{:S(2)}, u32[]{:S(2)}) collective-permute-start(f32[24,128]{1,0:T(8,128)S(1)} %score.9), channel_id=1, source_target_pairs={{0,14},{1,15},{4,10},{5,11},{8,6},{9,7},{12,2},{13,3},{14,0},{15,1... | collective-permute-start | bytes 36872 | tf_op jit(solution)/shard_map/ppermute | solution.py:456

commit v8 on v7

--- a/solution.py
+++ b/solution.py
@@ -478,22 +478,24 @@
             ]
 
     send_on(1)
-    back = {}
+    scored, back = {}, {}
+
+    def send_back(offsets):
+        return {offset % chips: moved(scored[offset], -offset) for offset in offsets}
+
     for step in range(middle + 1):
         if 0 < step < middle:
             send_on(step + 1)
         offsets = (step,) if step in (0, middle) else (step, -step)
         fresh = score([arrived[offset] for offset in offsets], slots, query_tok, chips, tiles)
-        for offset, result in zip(offsets, fresh):
-            back[offset % chips] = moved(result, -offset) if offset else result
+        scored.update(zip(offsets, fresh))
         names = [] if step == middle else [step + 1, -step - 1] if step + 1 < middle else [middle]
-        earlier = [1, -1] if step == 1 else [step - 1, 1 - step] if 2 < step < middle else []
-        earlier = [offset % chips for offset in earlier]
-        held, came, _ = lax.optimization_barrier(
-            ([arrived[name] for name in names], [back[j] for j in earlier], fresh)
+        held, scored, back = lax.optimization_barrier(
+            ([arrived[name] for name in names], scored, send_back(offsets) if step == 1 else back)
         )
         arrived.update(zip(names, held))
-        back.update(zip(earlier, came))
+    back.update(send_back([offset for offset in scored if abs(offset) > 1]))
+    back[0] = scored[0]
     return finish(per_device, query_tok, slot_of, [back[j] for j in range(chips)])
 
 

time: 69.9 us -> 71.2 us (1.019); the launches traced: 69.7 us -> 69.9 us
  starting transfers between devices: 27.5 us -> 17.2 us
  Pallas kernels: 33 us -> 39.9 us
  waiting for transfers between devices: 7.11 us -> 10.7 us
    ppermute x15, starting transfers between devices: 26.7 us -> 16.5 us  [moved(): return lax.ppermute(x, 'corpus', pairs)]
    pallas_call x5, Pallas kernels: 24.9 us -> 31.8 us  [score(): pl.pallas_call(functools.partial(score_kernel, pieces, slots, query_tok,...]
    ppermute x15, waiting for transfers between devices: 7.11 us -> 10.7 us  [moved(): return lax.ppermute(x, 'corpus', pairs)]
  transfers between devices with their start and end apart: 17 -> 17, of which waited for: 5 -> 9; matrix products, arithmetic and copies ran while one was open for 0% -> 0% of each run, Pallas kernels for 46% -> 50%
where the time goes in v8:
time: 71.2 us; the launch traced here: 69.9 us
  Pallas kernels  39.9 us (56%)
  starting transfers between devices  17.2 us (24%)
  waiting for transfers between devices  10.7 us (15%)
  local copies, waits for them, and re-layouts  1.35 us (2%)
  between operations  0.78 us (1%)
    pallas_call x5, Pallas kernels, score(): pl.pallas_call(functools.partial(score_kernel, pieces, slots, query_tok,...  31.8 us
    ppermute x15, starting transfers between devices, moved(): return lax.ppermute(x, 'corpus', pairs)  16.5 us
    ppermute x15, waiting for transfers between devices, moved(): return lax.ppermute(x, 'corpus', pairs)  10.7 us
    pallas_call x1, Pallas kernels, ready(): pl.pallas_call(functools.partial(ready_kernel, chips, slots, parts), out_...  3.11 us
    pallas_call x1, Pallas kernels, join(): pl.pallas_call(join_kernel, out_shape=jax.ShapeDtypeStruct((CORES * own.s...  1.94 us
    pallas_call x1, Pallas kernels, pack(): pl.pallas_call(functools.partial(pack_kernel, per_owner, chips, slots), o...  1.93 us
  transfers between devices with their start and end apart: 17, of which 9 were waited for; matrix products, arithmetic and copies ran while one was open for 0% of the time, Pallas kernels for 50%

profile of v8, /device:TPU:0, one launch (start us, length us, event | category | flops | bytes accessed | tf_op | source)
XLA Modules:
  0.0 69.9 jit_solution(10288307110834198431)
XLA Ops:
  0.6 0.5 collective-permute-start.3
  1.1 1.9 %pack.1.refs_1_ = bf16[1808,128]{1,0:T(8,128)(2,1)} custom-call(bf16[1792,128]{1,0:T(8,128)(2,1)} %bitcast.1, s32[1,128]{1,0:T(1,128)} %candidates_in.1), custom_call_target="tpu_custom_call" | custom-call | tf_op jit(solution)/shard_map/pack/pallas_call | solution.py:92
  3.1 2.6 %collective-permute-start = (bf16[1808,128]{1,0:T(8,128)(2,1)}, bf16[1808,128]{1,0:T(8,128)(2,1)S(1)}, u32[]{:S(2)}, u32[]{:S(2)}) collective-permute-start(bf16[1808,128]{1,0:T(8,128)(2,1)} %pack.1.refs_1_), channel_id=1, source_target_pairs={{0,4},{1,5},{4,8},{5,9},{8,12},{9,13},{12,14},{13,15},{14,10},{15,... | collective-permute-start | bytes 1388552 | tf_op jit(solution)/shard_map/ppermute | solution.py:456
  5.7 0.0 collective-permute-start.1
  5.7 0.2 collective-permute-start.2
  5.9 0.0 copy-start.1
  5.9 0.7 copy-done.1
  6.6 0.0 copy-start.2
  6.6 0.7 copy-done.2
  7.3 3.1 %ready.1 = (s32[128,128]{1,0:T(8,128)S(1)}, bf16[128,128,128]{2,1,0:T(8,128)(2,1)S(1)}) custom-call(s32[128]{0:T(128)S(1)} %copy-done.2, s32[1,128]{1,0:T(1,128)S(1)} %copy-done.1, bf16[128,128,128]{2,1,0:T(8,128)(2,1)} %passages.1), custom_call_target="tpu_custom_call" | custom-call | tf_op jit(solution)/shard_map/ready/pallas_call | solution.py:154
  10.4 0.0 collective-permute-done.2.lens
  10.4 0.0 collective-permute-done.3.other
  10.4 0.0 copy-start
  10.4 1.9 %join.1.refs_0_ = bf16[256,128,128]{2,1,0:T(8,128)(2,1)S(1)} custom-call(s32[128]{0:T(128)S(1)} %collective-permute-done.2.lens, bf16[128,128,128]{2,1,0:T(8,128)(2,1)S(1)} %collective-permute-done.3.other, bf16[128,128,128]{2,1,0:T(8,128)(2,1)S(1)} %get-tuple-element.43.own), custom_call_target="tpu_custom_call" | custom-call | tf_op jit(solution)/shard_map/join/pallas_call | solution.py:182
  12.4 0.0 copy-done
  12.4 4.0 %score.5.refs_0_ = f32[24,128]{1,0:T(8,128)S(1)} custom-call(bf16[256,128,128]{2,1,0:T(8,128)(2,1)S(1)} %join.1.refs_0_, bf16[1808,128]{1,0:T(8,128)(2,1)S(1)} %copy-done), custom_call_target="tpu_custom_call" | custom-call | flops 4227858432 | bytes 1245184 | tf_op jit(solution)/shard_map/score/pallas_call | solution.py:321
  16.4 0.7 %collective-permute-done.refs_1_ = bf16[1808,128]{1,0:T(8,128)(2,1)S(1)} collective-permute-done((bf16[1808,128]{1,0:T(8,128)(2,1)}, bf16[1808,128]{1,0:T(8,128)(2,1)S(1)}, u32[]{:S(2)}, u32[]{:S(2)}) %collective-permute-start) | collective-permute-done | bytes 462880 | tf_op jit(solution)/shard_map/ppermute | solution.py:456
  17.1 1.5 %collective-permute-done.1.refs_2_ = bf16[1808,128]{1,0:T(8,128)(2,1)S(1)} collective-permute-done((bf16[1808,128]{1,0:T(8,128)(2,1)}, bf16[1808,128]{1,0:T(8,128)(2,1)S(1)}, u32[]{:S(2)}, u32[]{:S(2)}) %collective-permute-start.1) | collective-permute-done | bytes 462880 | tf_op jit(solution)/shard_map/ppermute | solution.py:456
  18.7 1.6 %collective-permute-start.4 = (bf16[1808,128]{1,0:T(8,128)(2,1)S(1)}, bf16[1808,128]{1,0:T(8,128)(2,1)S(1)}, u32[]{:S(2)}, u32[]{:S(2)}) collective-permute-start(bf16[1808,128]{1,0:T(8,128)(2,1)S(1)} %collective-permute-done.refs_1_), channel_id=1, source_target_pairs={{0,4},{1,5},{4,8},{5,9},{8,12},{9,13},{12,14},{13,15},{14,10},{15,... | collective-permute-start | bytes 1388552 | tf_op jit(solution)/shard_map/ppermute | solution.py:456
  20.2 0.4 collective-permute-start.5
  20.7 7.9 %score.6 = (f32[24,128]{1,0:T(8,128)S(1)}, f32[24,128]{1,0:T(8,128)S(1)}) custom-call(bf16[256,128,128]{2,1,0:T(8,128)(2,1)S(1)} %join.1.refs_0_, bf16[1808,128]{1,0:T(8,128)(2,1)S(1)} %collective-permute-done.refs_1_, bf16[1808,128]{1,0:T(8,128)(2,1)S(1)} %collective-permute-done.1.refs_2_), custom_call_target="tpu_custom_call" | custom-call | flops 8455716864 | bytes 2490368 | tf_op jit(solution)/shard_map/score/pallas_call | solution.py:321
  28.6 0.1 collective-permute-start.6
  28.6 2.0 %collective-permute-start.7 = (f32[24,128]{1,0:T(8,128)S(1)}, f32[24,128]{1,0:T(8,128)S(1)}, u32[]{:S(2)}, u32[]{:S(2)}) collective-permute-start(f32[24,128]{1,0:T(8,128)S(1)} %get-tuple-element.46), channel_id=1, source_target_pairs={{0,4},{1,5},{4,8},{5,9},{8,12},{9,13},{12,14},{13,15},{14,10},{15,... | collective-permute-start | bytes 36872 | tf_op jit(solution)/shard_map/ppermute | solution.py:456
  30.7 1.7 %collective-permute-done.6.refs_1_ = f32[24,128]{1,0:T(8,128)S(1)} collective-permute-done((f32[24,128]{1,0:T(8,128)S(1)}, f32[24,128]{1,0:T(8,128)S(1)}, u32[]{:S(2)}, u32[]{:S(2)}) %collective-permute-start.6) | collective-permute-done | bytes 12320 | tf_op jit(solution)/shard_map/ppermute | solution.py:456
  32.3 0.1 collective-permute-done.7.refs_7_
  32.4 0.0 collective-permute-done.4.refs_1_
  32.4 0.0 collective-permute-done.5.refs_2_
  32.4 2.0 %collective-permute-start.8 = (bf16[1808,128]{1,0:T(8,128)(2,1)S(1)}, bf16[1808,128]{1,0:T(8,128)(2,1)S(1)}, u32[]{:S(2)}, u32[]{:S(2)}) collective-permute-start(bf16[1808,128]{1,0:T(8,128)(2,1)S(1)} %collective-permute-done.4.refs_1_), channel_id=1, source_target_pairs={{0,4},{1,5},{4,8},{5,9},{8,12},{9,13},{12,14},{13,15},{14,10},{15,... | collective-permute-start | bytes 1388552 | tf_op jit(solution)/shard_map/ppermute | solution.py:456
  34.4 0.1 collective-permute-start.9
  34.4 8.4 %score.7 = (f32[24,128]{1,0:T(8,128)S(1)}, f32[24,128]{1,0:T(8,128)S(1)}) custom-call(bf16[256,128,128]{2,1,0:T(8,128)(2,1)S(1)} %join.1.refs_0_, bf16[1808,128]{1,0:T(8,128)(2,1)S(1)} %collective-permute-done.4.refs_1_, bf16[1808,128]{1,0:T(8,128)(2,1)S(1)} %collective-permute-done.5.refs_2_), custom_call_target="tpu_custom_call" | custom-call | flops 8455716864 | bytes 2490368 | tf_op jit(solution)/shard_map/score/pallas_call | solution.py:321
  42.8 0.3 collective-permute-done.8.refs_1_
  43.1 2.0 %collective-permute-done.9.refs_2_ = bf16[1808,128]{1,0:T(8,128)(2,1)S(1)} collective-permute-done((bf16[1808,128]{1,0:T(8,128)(2,1)S(1)}, bf16[1808,128]{1,0:T(8,128)(2,1)S(1)}, u32[]{:S(2)}, u32[]{:S(2)}) %collective-permute-start.9) | collective-permute-done | bytes 462880 | tf_op jit(solution)/shard_map/ppermute | solution.py:456
  45.1 0.1 collective-permute-start.11
  45.2 2.0 %collective-permute-start.10 = (bf16[896,128]{1,0:T(8,128)(2,1)S(1)}, bf16[896,128]{1,0:T(8,128)(2,1)S(1)}, u32[]{:S(2)}, u32[]{:S(2)}) collective-permute-start(bf16[896,128]{1,0:T(8,128)(2,1)S(1)} %slice.6), channel_id=1, source_target_pairs={{0,4},{1,5},{4,8},{5,9},{8,12},{9,13},{12,14},{13,15},{14,10},{15,... | collective-permute-start | bytes 688136 | tf_op jit(solution)/shard_map/ppermute | solution.py:456
  47.2 7.4 %score.8 = (f32[24,128]{1,0:T(8,128)S(1)}, f32[24,128]{1,0:T(8,128)S(1)}) custom-call(bf16[256,128,128]{2,1,0:T(8,128)(2,1)S(1)} %join.1.refs_0_, bf16[1808,128]{1,0:T(8,128)(2,1)S(1)} %collective-permute-done.8.refs_1_, bf16[1808,128]{1,0:T(8,128)(2,1)S(1)} %collective-permute-done.9.refs_2_), custom_call_target="tpu_custom_call" | custom-call | flops 8455716864 | bytes 2490368 | tf_op jit(solution)/shard_map/score/pallas_call | solution.py:321
  54.7 0.0 collective-permute-done.10.refs_1_
  54.7 0.0 collective-permute-done.11.refs_2_
  54.7 4.1 %score.9 = f32[24,128]{1,0:T(8,128)S(1)} custom-call(bf16[256,128,128]{2,1,0:T(8,128)(2,1)S(1)} %join.1.refs_0_, bf16[896,128]{1,0:T(8,128)(2,1)S(1)} %collective-permute-done.10.refs_1_, bf16[912,128]{1,0:T(8,128)(2,1)S(1)} %collective-permute-done.11.refs_2_), custom_call_target="tpu_custom_call" | custom-call | flops 4227858432 | bytes 1245184 | tf_op jit(solution)/shard_map/score/pallas_call | solution.py:321
  58.7 0.1 collective-permute-start.12
  58.8 3.0 %collective-permute-start.13 = (f32[24,128]{1,0:T(8,128)S(1)}, f32[24,128]{1,0:T(8,128)S(1)}, u32[]{:S(2)}, u32[]{:S(2)}) collective-permute-start(f32[24,128]{1,0:T(8,128)S(1)} %get-tuple-element.77), channel_id=1, source_target_pairs={{0,10},{1,11},{4,6},{5,7},{8,2},{9,3},{12,0},{13,1},{14,4},{15,5},... | collective-permute-start | bytes 36872 | tf_op jit(solution)/shard_map/ppermute | solution.py:456
  61.8 0.6 collective-permute-start.14
  62.4 1.8 %collective-permute-start.15 = (f32[24,128]{1,0:T(8,128)S(1)}, f32[24,128]{1,0:T(8,128)S(1)}, u32[]{:S(2)}, u32[]{:S(2)}) collective-permute-start(f32[24,128]{1,0:T(8,128)S(1)} %get-tuple-element.79), channel_id=1, source_target_pairs={{0,12},{1,13},{4,14},{5,15},{8,10},{9,11},{12,6},{13,7},{14,2},{15... | collective-permute-start | bytes 36872 | tf_op jit(solution)/shard_map/ppermute | solution.py:456
  64.1 0.2 collective-permute-start.16
  64.3 0.0 collective-permute-done.12.refs_2_
  64.3 0.1 collective-permute-done.13.refs_3_
  64.4 3.8 %collective-permute-done.14.refs_4_ = f32[24,128]{1,0:T(8,128)S(1)} collective-permute-done((f32[24,128]{1,0:T(8,128)S(1)}, f32[24,128]{1,0:T(8,128)S(1)}, u32[]{:S(2)}, u32[]{:S(2)}) %collective-permute-start.14) | collective-permute-done | bytes 12320 | tf_op jit(solution)/shard_map/ppermute | solution.py:456
  68.2 0.0 collective-permute-done.15.refs_5_
  68.2 0.5 collective-permute-done.16.refs_6_
  68.7 1.1 %finish.1 = (f32[56,128]{1,0:T(8,128)}, f32[56,100]{1,0:T(8,128)}) custom-call(s32[128,128]{1,0:T(8,128)S(1)} %get-tuple-element.42.slot_of, f32[24,128]{1,0:T(8,128)S(1)} %score.5.refs_0_, f32[24,128]{1,0:T(8,128)S(1)} %collective-permute-done.6.refs_1_, f32[24,128]{1,0:T(8,128)S(1)} %collective-permute-done.12.refs_2_, ...), custom_call_target="tpu_custom_call" | custom-call | tf_op jit(solution)/shard_map/finish/pallas_call | solution.py:421
  (2 shorter events, 0.0 us)
Async XLA Ops:
  0.6 9.8 %collective-permute-start.3 = (bf16[128,128,128]{2,1,0:T(8,128)(2,1)}, bf16[128,128,128]{2,1,0:T(8,128)(2,1)S(1)}, u32[]{:S(2)}, u32[]{:S(2)}) collective-permute-start(bf16[128,128,128]{2,1,0:T(8,128)(2,1)} %passages.1), channel_id=1, source_target_pairs={{0,1},{1,0},{2,3},{3,2},{4,5},{5,4},{6,7},{7,6},{8,9},{9,8},{10,11... | collective-permute-start | bytes 12582920 | tf_op jit(solution)/shard_map/ppermute | solution.py:459
  3.1 14.1 %collective-permute-start = (bf16[1808,128]{1,0:T(8,128)(2,1)}, bf16[1808,128]{1,0:T(8,128)(2,1)S(1)}, u32[]{:S(2)}, u32[]{:S(2)}) collective-permute-start(bf16[1808,128]{1,0:T(8,128)(2,1)} %pack.1.refs_1_), channel_id=1, source_target_pairs={{0,4},{1,5},{4,8},{5,9},{8,12},{9,13},{12,14},{13,15},{14,10},{15,... | collective-permute-start | bytes 1388552 | tf_op jit(solution)/shard_map/ppermute | solution.py:456
  5.7 12.9 %collective-permute-start.1 = (bf16[1808,128]{1,0:T(8,128)(2,1)}, bf16[1808,128]{1,0:T(8,128)(2,1)S(1)}, u32[]{:S(2)}, u32[]{:S(2)}) collective-permute-start(bf16[1808,128]{1,0:T(8,128)(2,1)} %pack.1.refs_1_), channel_id=1, source_target_pairs={{0,2},{1,3},{4,0},{5,1},{8,4},{9,5},{12,8},{13,9},{14,12},{15,13},... | collective-permute-start | bytes 1388552 | tf_op jit(solution)/shard_map/ppermute | solution.py:456
  5.7 4.6 %collective-permute-start.2 = (s32[128]{0:T(128)}, s32[128]{0:T(128)S(1)}, u32[]{:S(2)}, u32[]{:S(2)}) collective-permute-start(s32[128]{0:T(128)} %lens.1), channel_id=1, source_target_pairs={{0,1},{1,0},{2,3},{3,2},{4,5},{5,4},{6,7},{7,6},{8,9},{9,8},{10,11... | collective-permute-start | bytes 1544 | tf_op jit(solution)/shard_map/ppermute | solution.py:460
  5.9 0.7 copy-start.1
  6.6 0.7 copy-start.2
  10.4 2.0 %copy-start = (bf16[1808,128]{1,0:T(8,128)(2,1)S(1)}, bf16[1808,128]{1,0:T(8,128)(2,1)}, u32[]{:S(2)}) copy-start(bf16[1808,128]{1,0:T(8,128)(2,1)} %pack.1.refs_1_) | copy-start | bytes 1388548
  18.7 13.7 %collective-permute-start.4 = (bf16[1808,128]{1,0:T(8,128)(2,1)S(1)}, bf16[1808,128]{1,0:T(8,128)(2,1)S(1)}, u32[]{:S(2)}, u32[]{:S(2)}) collective-permute-start(bf16[1808,128]{1,0:T(8,128)(2,1)S(1)} %collective-permute-done.refs_1_), channel_id=1, source_target_pairs={{0,4},{1,5},{4,8},{5,9},{8,12},{9,13},{12,14},{13,15},{14,10},{15,... | collective-permute-start | bytes 1388552 | tf_op jit(solution)/shard_map/ppermute | solution.py:456
  20.2 12.2 %collective-permute-start.5 = (bf16[1808,128]{1,0:T(8,128)(2,1)S(1)}, bf16[1808,128]{1,0:T(8,128)(2,1)S(1)}, u32[]{:S(2)}, u32[]{:S(2)}) collective-permute-start(bf16[1808,128]{1,0:T(8,128)(2,1)S(1)} %collective-permute-done.1.refs_2_), channel_id=1, source_target_pairs={{0,2},{1,3},{4,0},{5,1},{8,4},{9,5},{12,8},{13,9},{14,12},{15,13},... | collective-permute-start | bytes 1388552 | tf_op jit(solution)/shard_map/ppermute | solution.py:456
  28.6 3.7 %collective-permute-start.6 = (f32[24,128]{1,0:T(8,128)S(1)}, f32[24,128]{1,0:T(8,128)S(1)}, u32[]{:S(2)}, u32[]{:S(2)}) collective-permute-start(f32[24,128]{1,0:T(8,128)S(1)} %get-tuple-element.48), channel_id=1, source_target_pairs={{0,2},{1,3},{4,0},{5,1},{8,4},{9,5},{12,8},{13,9},{14,12},{15,13},... | collective-permute-start | bytes 36872 | tf_op jit(solution)/shard_map/ppermute | solution.py:456
  28.6 3.7 %collective-permute-start.7 = (f32[24,128]{1,0:T(8,128)S(1)}, f32[24,128]{1,0:T(8,128)S(1)}, u32[]{:S(2)}, u32[]{:S(2)}) collective-permute-start(f32[24,128]{1,0:T(8,128)S(1)} %get-tuple-element.46), channel_id=1, source_target_pairs={{0,4},{1,5},{4,8},{5,9},{8,12},{9,13},{12,14},{13,15},{14,10},{15,... | collective-permute-start | bytes 36872 | tf_op jit(solution)/shard_map/ppermute | solution.py:456
  32.4 10.7 %collective-permute-start.8 = (bf16[1808,128]{1,0:T(8,128)(2,1)S(1)}, bf16[1808,128]{1,0:T(8,128)(2,1)S(1)}, u32[]{:S(2)}, u32[]{:S(2)}) collective-permute-start(bf16[1808,128]{1,0:T(8,128)(2,1)S(1)} %collective-permute-done.4.refs_1_), channel_id=1, source_target_pairs={{0,4},{1,5},{4,8},{5,9},{8,12},{9,13},{12,14},{13,15},{14,10},{15,... | collective-permute-start | bytes 1388552 | tf_op jit(solution)/shard_map/ppermute | solution.py:456
  34.4 10.7 %collective-permute-start.9 = (bf16[1808,128]{1,0:T(8,128)(2,1)S(1)}, bf16[1808,128]{1,0:T(8,128)(2,1)S(1)}, u32[]{:S(2)}, u32[]{:S(2)}) collective-permute-start(bf16[1808,128]{1,0:T(8,128)(2,1)S(1)} %collective-permute-done.5.refs_2_), channel_id=1, source_target_pairs={{0,2},{1,3},{4,0},{5,1},{8,4},{9,5},{12,8},{13,9},{14,12},{15,13},... | collective-permute-start | bytes 1388552 | tf_op jit(solution)/shard_map/ppermute | solution.py:456
  45.1 9.6 %collective-permute-start.11 = (bf16[912,128]{1,0:T(8,128)(2,1)S(1)}, bf16[912,128]{1,0:T(8,128)(2,1)S(1)}, u32[]{:S(2)}, u32[]{:S(2)}) collective-permute-start(bf16[912,128]{1,0:T(8,128)(2,1)S(1)} %slice.7), channel_id=1, source_target_pairs={{0,2},{1,3},{4,0},{5,1},{8,4},{9,5},{12,8},{13,9},{14,12},{15,13},... | collective-permute-start | bytes 700424 | tf_op jit(solution)/shard_map/ppermute | solution.py:456
  45.2 9.4 %collective-permute-start.10 = (bf16[896,128]{1,0:T(8,128)(2,1)S(1)}, bf16[896,128]{1,0:T(8,128)(2,1)S(1)}, u32[]{:S(2)}, u32[]{:S(2)}) collective-permute-start(bf16[896,128]{1,0:T(8,128)(2,1)S(1)} %slice.6), channel_id=1, source_target_pairs={{0,4},{1,5},{4,8},{5,9},{8,12},{9,13},{12,14},{13,15},{14,10},{15,... | collective-permute-start | bytes 688136 | tf_op jit(solution)/shard_map/ppermute | solution.py:456
  58.7 5.5 %collective-permute-start.12 = (f32[24,128]{1,0:T(8,128)S(1)}, f32[24,128]{1,0:T(8,128)S(1)}, u32[]{:S(2)}, u32[]{:S(2)}) collective-permute-start(f32[24,128]{1,0:T(8,128)S(1)} %get-tuple-element.76), channel_id=1, source_target_pairs={{0,6},{1,7},{4,2},{5,3},{8,0},{9,1},{12,4},{13,5},{14,8},{15,9},{1... | collective-permute-start | bytes 36872 | tf_op jit(solution)/shard_map/ppermute | solution.py:456
  58.8 5.5 %collective-permute-start.13 = (f32[24,128]{1,0:T(8,128)S(1)}, f32[24,128]{1,0:T(8,128)S(1)}, u32[]{:S(2)}, u32[]{:S(2)}) collective-permute-start(f32[24,128]{1,0:T(8,128)S(1)} %get-tuple-element.77), channel_id=1, source_target_pairs={{0,10},{1,11},{4,6},{5,7},{8,2},{9,3},{12,0},{13,1},{14,4},{15,5},... | collective-permute-start | bytes 36872 | tf_op jit(solution)/shard_map/ppermute | solution.py:456
  61.8 6.4 %collective-permute-start.14 = (f32[24,128]{1,0:T(8,128)S(1)}, f32[24,128]{1,0:T(8,128)S(1)}, u32[]{:S(2)}, u32[]{:S(2)}) collective-permute-start(f32[24,128]{1,0:T(8,128)S(1)} %score.9), channel_id=1, source_target_pairs={{0,14},{1,15},{4,10},{5,11},{8,6},{9,7},{12,2},{13,3},{14,0},{15,1... | collective-permute-start | bytes 36872 | tf_op jit(solution)/shard_map/ppermute | solution.py:456
  62.4 5.8 %collective-permute-start.15 = (f32[24,128]{1,0:T(8,128)S(1)}, f32[24,128]{1,0:T(8,128)S(1)}, u32[]{:S(2)}, u32[]{:S(2)}) collective-permute-start(f32[24,128]{1,0:T(8,128)S(1)} %get-tuple-element.79), channel_id=1, source_target_pairs={{0,12},{1,13},{4,14},{5,15},{8,10},{9,11},{12,6},{13,7},{14,2},{15... | collective-permute-start | bytes 36872 | tf_op jit(solution)/shard_map/ppermute | solution.py:456
  64.1 4.6 %collective-permute-start.16 = (f32[24,128]{1,0:T(8,128)S(1)}, f32[24,128]{1,0:T(8,128)S(1)}, u32[]{:S(2)}, u32[]{:S(2)}) collective-permute-start(f32[24,128]{1,0:T(8,128)S(1)} %get-tuple-element.80), channel_id=1, source_target_pairs={{0,8},{1,9},{4,12},{5,13},{8,14},{9,15},{12,10},{13,11},{14,6},{15... | collective-permute-start | bytes 36872 | tf_op jit(solution)/shard_map/ppermute | solution.py:456

commit v9 on v8

--- a/solution.py
+++ b/solution.py
@@ -132,16 +132,13 @@
     for load in loads:
         load.start()
     number = candidates.shape[1]
-    my_place = ring_place(lax.axis_index("corpus") // CORES, chips)
     wide = jnp.broadcast_to(candidates[...], (number, number)) // (CORES * per_owner)
     tall = wide.astype(jnp.float32).T.astype(jnp.int32)
     row = lax.broadcasted_iota(jnp.int32, (number, number), 0)
     lane = lax.broadcasted_iota(jnp.int32, (number, number), 1)
     earlier = jnp.where((wide == tall) & (lane < row), 1.0, 0.0)
     rank = jnp.sum(earlier, axis=1, keepdims=True).astype(jnp.int32)
-    ahead = ring_place(tall, chips) - my_place
-    ahead = jnp.where(ahead < 0, ahead + chips, ahead)
-    slot_of[...] = ahead * slots + rank
+    slot_of[...] = ring_place(tall, chips) * slots + rank
     for i, load in enumerate(loads):
         load.wait()
         fill_tiles(filled, lens, filled, 0, i * size, size)
@@ -222,13 +219,12 @@
     return parts[0]
 
 
-def score_kernel(pieces, slots, query_tok, chips, *refs):
+def score_kernel(pieces, offsets, slots, query_tok, chips, kept, *refs):
     blocks = len(pieces)
     arrays = sum(pieces)
     tiles = refs[0]
     held = refs[1 : 1 + arrays]
-    outs = refs[1 + arrays : 1 + arrays + blocks]
-    weights, nearest, plan_v, plan, sem, weight_sems = refs[1 + arrays + blocks :]
+    out, weights, nearest, plan_v, plan, sem, weight_sems = refs[1 + arrays + kept :]
     tile_rows = tiles.shape[1]
     my_place = ring_place(lax.axis_index("corpus") // CORES, chips)
     fact_rows = fact_rows_of(chips)
@@ -252,6 +248,10 @@
         at += count
     to_scalar = pltpu.make_async_copy(plan_v, plan, sem)
     to_scalar.start()
+    if kept:
+        out[...] = refs[1 + arrays][...]
+    else:
+        out[...] = jnp.zeros(out.shape, out.dtype)
     for load in loads:
         load.start()
     to_scalar.wait()
@@ -300,18 +300,17 @@
             parts.append(x)
         total = token_sums(parts, query_tok)
         total = jnp.where(slot_row < count, total / float(query_tok), 0.0)
-        for k in range(blocks):
-
-            @pl.when(b == k)
-            def _(k=k):
-                outs[k][...] = total
-
+        offset = offsets[-1]
+        for k in range(blocks - 1):
+            offset = jnp.where(b == k, offsets[k], offset)
+        place = my_place - offset
+        out[jnp.where(place < 0, place + chips, place)] = total
         return carry
 
     lax.fori_loop(0, blocks, score_block, 0)
 
 
-def score(held, slots, query_tok, chips, tiles):
+def score(held, offsets, slots, query_tok, chips, tiles, *earlier):
     pieces = tuple(len(arrays) for arrays in held)
     flat = [x for arrays in held for x in arrays]
     blocks = len(pieces)
@@ -319,10 +318,12 @@
     query_rows = sum(x.shape[0] for x in held[0]) - fact_rows_of(chips)
     flops = 2 * blocks * slots * tile_rows * feature * query_rows
     return pl.pallas_call(
-        functools.partial(score_kernel, pieces, slots, query_tok, chips),
-        out_shape=(jax.ShapeDtypeStruct((slots, LANES), jnp.float32),) * blocks,
-        in_specs=[pl.BlockSpec(memory_space=pltpu.VMEM)] * (1 + len(flat)),
-        out_specs=(pl.BlockSpec(memory_space=pltpu.VMEM),) * blocks,
+        functools.partial(
+            score_kernel, pieces, offsets, slots, query_tok, chips, len(earlier)
+        ),
+        out_shape=jax.ShapeDtypeStruct((chips, slots, LANES), jnp.float32),
+        in_specs=[pl.BlockSpec(memory_space=pltpu.VMEM)] * (1 + len(flat) + len(earlier)),
+        out_specs=pl.BlockSpec(memory_space=pltpu.VMEM),
         scratch_shapes=[
             pltpu.VMEM((blocks, query_rows, feature), tiles.dtype),
             pltpu.VMEM((query_rows // LANES, 8 * slots, LANES), jnp.float32),
@@ -338,7 +339,7 @@
             transcendentals=0,
         ),
         name="score",
-    )(tiles, *flat)
+    )(tiles, *flat, *earlier)
 
 
 def sort_descending(parts, lanes):
@@ -381,18 +382,17 @@
     return parts
 
 
-def finish_kernel(arrays, per_device, query_tok, topk, slot_of, *refs):
-    returned = refs[:arrays]
-    scores, best_scores, spread, ranked, rows, turned = refs[arrays:]
+def finish_kernel(
+    per_device, query_tok, topk,
+    slot_of, returned, scores, best_scores, ranked, rows, turned,
+):
     number = slot_of.shape[0]
-    step = returned[0].shape[0]
-    for at, ref in enumerate(returned):
-        spread[at * step : (at + 1) * step, :] = ref[...]
+    spread = returned[...].reshape(returned.shape[0] * returned.shape[1], LANES)
     total = spread.shape[0]
     lane = lax.broadcasted_iota(jnp.int32, (number, total), 1)
     choose = (slot_of[:, 0:1] == lane).astype(jnp.float32).astype(jnp.bfloat16)
     by_candidate = jnp.zeros((number, LANES), jnp.float32)
-    for part in split_exact(spread[...]):
+    for part in split_exact(spread):
         by_candidate += jnp.dot(choose, part, preferred_element_type=jnp.float32)
 
     each = LANES // query_tok
@@ -417,24 +417,22 @@
 
 def finish(per_device, query_tok, slot_of, returned):
     number = slot_of.shape[0]
-    total = sum(r.shape[0] for r in returned)
     return pl.pallas_call(
-        functools.partial(finish_kernel, len(returned), per_device, query_tok, TOPK),
+        functools.partial(finish_kernel, per_device, query_tok, TOPK),
         out_shape=(
             jax.ShapeDtypeStruct((per_device, number), jnp.float32),
             jax.ShapeDtypeStruct((per_device, TOPK), jnp.float32),
         ),
-        in_specs=[pl.BlockSpec(memory_space=pltpu.VMEM)] * (1 + len(returned)),
+        in_specs=[pl.BlockSpec(memory_space=pltpu.VMEM)] * 2,
         out_specs=(pl.BlockSpec(memory_space=pltpu.VMEM),) * 2,
         scratch_shapes=[
-            pltpu.VMEM((total, LANES), jnp.float32),
             pltpu.VMEM((number, LANES), jnp.float32),
             pltpu.VMEM((LANES, number), jnp.float32),
             pltpu.VMEM((LANES, number), jnp.float32),
         ],
         compiler_params=pltpu.CompilerParams(vmem_limit_bytes=VMEM_LIMIT),
         name="finish",
-    )(slot_of, *returned)
+    )(slot_of, returned)
 
 
 def local(queries, passages, lengths, candidates):
@@ -478,25 +476,24 @@
             ]
 
     send_on(1)
-    scored, back = {}, {}
-
-    def send_back(offsets):
-        return {offset % chips: moved(scored[offset], -offset) for offset in offsets}
-
+    scored = []
     for step in range(middle + 1):
         if 0 < step < middle:
             send_on(step + 1)
         offsets = (step,) if step in (0, middle) else (step, -step)
-        fresh = score([arrived[offset] for offset in offsets], slots, query_tok, chips, tiles)
-        scored.update(zip(offsets, fresh))
+        fresh = score(
+            [arrived[offset] for offset in offsets], tuple(offset % chips for offset in offsets),
+            slots, query_tok, chips, tiles, *scored,
+        )
         names = [] if step == middle else [step + 1, -step - 1] if step + 1 < middle else [middle]
-        held, scored, back = lax.optimization_barrier(
-            ([arrived[name] for name in names], scored, send_back(offsets) if step == 1 else back)
-        )
+        held, fresh = lax.optimization_barrier(([arrived[name] for name in names], fresh))
         arrived.update(zip(names, held))
-    back.update(send_back([offset for offset in scored if abs(offset) > 1]))
-    back[0] = scored[0]
-    return finish(per_device, query_tok, slot_of, [back[j] for j in range(chips)])
+        scored = [fresh]
+    by_place = [[order[i] * CORES + k for i in range(chips)] for k in range(CORES)]
+    returned = lax.all_to_all(
+        scored[0], "corpus", split_axis=0, concat_axis=0, tiled=True, axis_index_groups=by_place
+    )
+    return finish(per_device, query_tok, slot_of, returned)
 
 
 def solution(mesh):

time: 71.2 us -> 69 us (0.969); the launches traced: 69.9 us -> 68.7 us
  blocking collectives: 0 us -> 11.9 us
  starting transfers between devices: 17.2 us -> 9.56 us
  Pallas kernels: 39.9 us -> 34.3 us
    all_to_all x0 -> x1, blocking collectives: none -> 11.9 us  [local(): lax.all_to_all(scored[0], 'corpus', split_axis=0, concat_axis=0, tiled=Tr...]
    ppermute x15 -> x8, starting transfers between devices: 16.5 us -> 8.83 us  [moved(): return lax.ppermute(x, 'corpus', pairs)]
    pallas_call x6, Pallas kernels: 32.9 us -> 27.4 us  [the longest x5 26.2 us: score(): pl.pallas_call(functools.partial(score_kernel, pieces, offsets, slots, qu...]
    ppermute x15 -> x8, waiting for transfers between devices: 10.7 us -> 10.9 us  [moved(): return lax.ppermute(x, 'corpus', pairs)]
  transfers between devices with their start and end apart: 17 -> 10, of which waited for: 9 -> 6; matrix products, arithmetic and copies ran while one was open for 0% -> 0% of each run, Pallas kernels for 50% -> 43%
where the time goes in v9:
time: 69 us; the launch traced here: 68.7 us
  Pallas kernels  34.3 us (50%)
  blocking collectives  11.9 us (17%)
  waiting for transfers between devices  10.9 us (16%)
  starting transfers between devices  9.56 us (14%)
  local copies, waits for them, and re-layouts  1.35 us (2%)
  between operations  0.76 us (1%)
    pallas_call x5, Pallas kernels, score(): pl.pallas_call(functools.partial(score_kernel, pieces, offsets, slots, qu...  26.2 us
    all_to_all x1, blocking collectives, local(): lax.all_to_all(scored[0], 'corpus', split_axis=0, concat_axis=0, tiled=Tr...  11.9 us
    ppermute x8, waiting for transfers between devices, moved(): return lax.ppermute(x, 'corpus', pairs)  10.9 us
    ppermute x8, starting transfers between devices, moved(): return lax.ppermute(x, 'corpus', pairs)  8.83 us
    pallas_call x1, Pallas kernels, ready(): pl.pallas_call(functools.partial(ready_kernel, chips, slots, parts), out_...  3.04 us
    pallas_call x1, Pallas kernels, join(): pl.pallas_call(join_kernel, out_shape=jax.ShapeDtypeStruct((CORES * own.s...  1.94 us
    pallas_call x1, Pallas kernels, pack(): pl.pallas_call(functools.partial(pack_kernel, per_owner, chips, slots), o...  1.93 us
  transfers between devices with their start and end apart: 10, of which 6 were waited for; matrix products, arithmetic and copies ran while one was open for 0% of the time, Pallas kernels for 43%

profile of v9, /device:TPU:0, one launch (start us, length us, event | category | flops | bytes accessed | tf_op | source)
XLA Modules:
  0.0 68.7 jit_solution(12656719940075797715)
XLA Ops:
  0.6 0.5 collective-permute-start.1
  1.1 1.9 %pack.1.refs_1_ = bf16[1808,128]{1,0:T(8,128)(2,1)} custom-call(bf16[1792,128]{1,0:T(8,128)(2,1)} %bitcast.1, s32[1,128]{1,0:T(1,128)} %candidates_in.1), custom_call_target="tpu_custom_call" | custom-call | tf_op jit(solution)/shard_map/pack/pallas_call | solution.py:92
  3.1 2.6 %collective-permute-start.2 = (bf16[1808,128]{1,0:T(8,128)(2,1)}, bf16[1808,128]{1,0:T(8,128)(2,1)S(1)}, u32[]{:S(2)}, u32[]{:S(2)}) collective-permute-start(bf16[1808,128]{1,0:T(8,128)(2,1)} %pack.1.refs_1_), channel_id=1, source_target_pairs={{0,4},{1,5},{4,8},{5,9},{8,12},{9,13},{12,14},{13,15},{14,10},{15,... | collective-permute-start | bytes 1388552 | tf_op jit(solution)/shard_map/ppermute | solution.py:454
  5.7 0.0 collective-permute-start.3
  5.7 0.2 collective-permute-start
  5.9 0.0 copy-start.1
  6.0 0.7 copy-done.1
  6.6 0.0 copy-start.2
  6.6 0.7 copy-done.2
  7.3 3.0 %ready.1 = (s32[128,128]{1,0:T(8,128)S(1)}, bf16[128,128,128]{2,1,0:T(8,128)(2,1)S(1)}) custom-call(s32[128]{0:T(128)S(1)} %copy-done.2, s32[1,128]{1,0:T(1,128)S(1)} %copy-done.1, bf16[128,128,128]{2,1,0:T(8,128)(2,1)} %passages.1), custom_call_target="tpu_custom_call" | custom-call | tf_op jit(solution)/shard_map/ready/pallas_call | solution.py:151
  10.3 0.0 collective-permute-done.lens
  10.3 0.0 collective-permute-done.1.other
  10.3 0.0 copy-start
  10.3 1.9 %join.1.refs_0_ = bf16[256,128,128]{2,1,0:T(8,128)(2,1)S(1)} custom-call(s32[128]{0:T(128)S(1)} %collective-permute-done.lens, bf16[128,128,128]{2,1,0:T(8,128)(2,1)S(1)} %collective-permute-done.1.other, bf16[128,128,128]{2,1,0:T(8,128)(2,1)S(1)} %get-tuple-element.17.own), custom_call_target="tpu_custom_call" | custom-call | tf_op jit(solution)/shard_map/join/pallas_call | solution.py:179
  12.3 0.0 copy-done
  12.3 4.1 %score.5.refs_3_ = f32[8,24,128]{2,1,0:T(8,128)S(1)} custom-call(bf16[256,128,128]{2,1,0:T(8,128)(2,1)S(1)} %join.1.refs_0_, bf16[1808,128]{1,0:T(8,128)(2,1)S(1)} %copy-done), custom_call_target="tpu_custom_call" | custom-call | flops 4227858432 | bytes 1245184 | tf_op jit(solution)/shard_map/score/pallas_call | solution.py:320
  16.4 0.8 %collective-permute-done.2.refs_1_ = bf16[1808,128]{1,0:T(8,128)(2,1)S(1)} collective-permute-done((bf16[1808,128]{1,0:T(8,128)(2,1)}, bf16[1808,128]{1,0:T(8,128)(2,1)S(1)}, u32[]{:S(2)}, u32[]{:S(2)}) %collective-permute-start.2) | collective-permute-done | bytes 462880 | tf_op jit(solution)/shard_map/ppermute | solution.py:454
  17.1 1.5 %collective-permute-done.3.refs_2_ = bf16[1808,128]{1,0:T(8,128)(2,1)S(1)} collective-permute-done((bf16[1808,128]{1,0:T(8,128)(2,1)}, bf16[1808,128]{1,0:T(8,128)(2,1)S(1)}, u32[]{:S(2)}, u32[]{:S(2)}) %collective-permute-start.3) | collective-permute-done | bytes 462880 | tf_op jit(solution)/shard_map/ppermute | solution.py:454
  18.7 1.6 %collective-permute-start.4 = (bf16[1808,128]{1,0:T(8,128)(2,1)S(1)}, bf16[1808,128]{1,0:T(8,128)(2,1)S(1)}, u32[]{:S(2)}, u32[]{:S(2)}) collective-permute-start(bf16[1808,128]{1,0:T(8,128)(2,1)S(1)} %collective-permute-done.2.refs_1_), channel_id=1, source_target_pairs={{0,4},{1,5},{4,8},{5,9},{8,12},{9,13},{12,14},{13,15},{14,10},{15,... | collective-permute-start | bytes 1388552 | tf_op jit(solution)/shard_map/ppermute | solution.py:454
  20.2 0.4 collective-permute-start.5
  20.7 5.7 %score.6.refs_3_ = f32[8,24,128]{2,1,0:T(8,128)S(1)} custom-call(bf16[256,128,128]{2,1,0:T(8,128)(2,1)S(1)} %join.1.refs_0_, bf16[1808,128]{1,0:T(8,128)(2,1)S(1)} %collective-permute-done.2.refs_1_, bf16[1808,128]{1,0:T(8,128)(2,1)S(1)} %collective-permute-done.3.refs_2_, f32[8,24,128]{2,1,0:T(8,128)S(1)} %score.5.refs_3_), custom_call_target="tpu_custom_call" | custom-call | flops 8455716864 | bytes 2490368 | tf_op jit(solution)/shard_map/score/pallas_call | solution.py:320
  26.4 4.2 %collective-permute-done.4.refs_1_ = bf16[1808,128]{1,0:T(8,128)(2,1)S(1)} collective-permute-done((bf16[1808,128]{1,0:T(8,128)(2,1)S(1)}, bf16[1808,128]{1,0:T(8,128)(2,1)S(1)}, u32[]{:S(2)}, u32[]{:S(2)}) %collective-permute-start.4) | collective-permute-done | bytes 462880 | tf_op jit(solution)/shard_map/ppermute | solution.py:454
  30.6 1.3 %collective-permute-done.5.refs_2_ = bf16[1808,128]{1,0:T(8,128)(2,1)S(1)} collective-permute-done((bf16[1808,128]{1,0:T(8,128)(2,1)S(1)}, bf16[1808,128]{1,0:T(8,128)(2,1)S(1)}, u32[]{:S(2)}, u32[]{:S(2)}) %collective-permute-start.5) | collective-permute-done | bytes 462880 | tf_op jit(solution)/shard_map/ppermute | solution.py:454
  31.9 1.6 %collective-permute-start.6 = (bf16[1808,128]{1,0:T(8,128)(2,1)S(1)}, bf16[1808,128]{1,0:T(8,128)(2,1)S(1)}, u32[]{:S(2)}, u32[]{:S(2)}) collective-permute-start(bf16[1808,128]{1,0:T(8,128)(2,1)S(1)} %collective-permute-done.4.refs_1_), channel_id=1, source_target_pairs={{0,4},{1,5},{4,8},{5,9},{8,12},{9,13},{12,14},{13,15},{14,10},{15,... | collective-permute-start | bytes 1388552 | tf_op jit(solution)/shard_map/ppermute | solution.py:454
  33.4 0.4 collective-permute-start.7
  33.9 6.8 %score.7.refs_3_ = f32[8,24,128]{2,1,0:T(8,128)S(1)} custom-call(bf16[256,128,128]{2,1,0:T(8,128)(2,1)S(1)} %join.1.refs_0_, bf16[1808,128]{1,0:T(8,128)(2,1)S(1)} %collective-permute-done.4.refs_1_, bf16[1808,128]{1,0:T(8,128)(2,1)S(1)} %collective-permute-done.5.refs_2_, f32[8,24,128]{2,1,0:T(8,128)S(1)} %score.6.refs_3_), custom_call_target="tpu_custom_call" | custom-call | flops 8455716864 | bytes 2490368 | tf_op jit(solution)/shard_map/score/pallas_call | solution.py:320
  40.7 1.8 %collective-permute-done.6.refs_1_ = bf16[1808,128]{1,0:T(8,128)(2,1)S(1)} collective-permute-done((bf16[1808,128]{1,0:T(8,128)(2,1)S(1)}, bf16[1808,128]{1,0:T(8,128)(2,1)S(1)}, u32[]{:S(2)}, u32[]{:S(2)}) %collective-permute-start.6) | collective-permute-done | bytes 462880 | tf_op jit(solution)/shard_map/ppermute | solution.py:454
  42.6 1.3 %collective-permute-done.7.refs_2_ = bf16[1808,128]{1,0:T(8,128)(2,1)S(1)} collective-permute-done((bf16[1808,128]{1,0:T(8,128)(2,1)S(1)}, bf16[1808,128]{1,0:T(8,128)(2,1)S(1)}, u32[]{:S(2)}, u32[]{:S(2)}) %collective-permute-start.7) | collective-permute-done | bytes 462880 | tf_op jit(solution)/shard_map/ppermute | solution.py:454
  43.9 1.6 %collective-permute-start.8 = (bf16[896,128]{1,0:T(8,128)(2,1)S(1)}, bf16[896,128]{1,0:T(8,128)(2,1)S(1)}, u32[]{:S(2)}, u32[]{:S(2)}) collective-permute-start(bf16[896,128]{1,0:T(8,128)(2,1)S(1)} %slice.6), channel_id=1, source_target_pairs={{0,4},{1,5},{4,8},{5,9},{8,12},{9,13},{12,14},{13,15},{14,10},{15,... | collective-permute-start | bytes 688136 | tf_op jit(solution)/shard_map/ppermute | solution.py:454
  45.5 0.6 collective-permute-start.9
  46.0 6.2 %score.8.refs_3_ = f32[8,24,128]{2,1,0:T(8,128)S(1)} custom-call(bf16[256,128,128]{2,1,0:T(8,128)(2,1)S(1)} %join.1.refs_0_, bf16[1808,128]{1,0:T(8,128)(2,1)S(1)} %collective-permute-done.6.refs_1_, bf16[1808,128]{1,0:T(8,128)(2,1)S(1)} %collective-permute-done.7.refs_2_, f32[8,24,128]{2,1,0:T(8,128)S(1)} %score.7.refs_3_), custom_call_target="tpu_custom_call" | custom-call | flops 8455716864 | bytes 2490368 | tf_op jit(solution)/shard_map/score/pallas_call | solution.py:320
  52.2 0.0 collective-permute-done.8.refs_1_
  52.2 0.0 collective-permute-done.9.refs_2_
  52.3 3.4 %score.9 = f32[8,24,128]{2,1,0:T(8,128)S(1)} custom-call(bf16[256,128,128]{2,1,0:T(8,128)(2,1)S(1)} %join.1.refs_0_, bf16[896,128]{1,0:T(8,128)(2,1)S(1)} %collective-permute-done.8.refs_1_, bf16[912,128]{1,0:T(8,128)(2,1)S(1)} %collective-permute-done.9.refs_2_, f32[8,24,128]{2,1,0:T(8,128)S(1)} %score.8.refs_3_), custom_call_target="tpu_custom_call" | custom-call | flops 4227858432 | bytes 1245184 | tf_op jit(solution)/shard_map/score/pallas_call | solution.py:320
  55.7 11.9 %all_to_all.5.returned = f32[8,24,128]{2,1,0:T(8,128)S(1)} all-to-all(f32[8,24,128]{2,1,0:T(8,128)S(1)} %score.9), channel_id=1, replica_groups={{0,4,8,12,14,10,6,2},{1,5,9,13,15,11,7,3},{16,20,24,28,30,26,22,18},{17..., dimensions={0} | all-to-all | bytes 196608 | tf_op jit(solution)/shard_map/all_to_all | solution.py:493
  67.6 1.1 %finish.1 = (f32[56,128]{1,0:T(8,128)}, f32[56,100]{1,0:T(8,128)}) custom-call(s32[128,128]{1,0:T(8,128)S(1)} %get-tuple-element.16.slot_of, f32[8,24,128]{2,1,0:T(8,128)S(1)} %all_to_all.5.returned), custom_call_target="tpu_custom_call" | custom-call | tf_op jit(solution)/shard_map/finish/pallas_call | solution.py:420
  (2 shorter events, 0.0 us)
Async XLA Ops:
  0.6 9.7 %collective-permute-start.1 = (bf16[128,128,128]{2,1,0:T(8,128)(2,1)}, bf16[128,128,128]{2,1,0:T(8,128)(2,1)S(1)}, u32[]{:S(2)}, u32[]{:S(2)}) collective-permute-start(bf16[128,128,128]{2,1,0:T(8,128)(2,1)} %passages.1), channel_id=1, source_target_pairs={{0,1},{1,0},{2,3},{3,2},{4,5},{5,4},{6,7},{7,6},{8,9},{9,8},{10,11... | collective-permute-start | bytes 12582920 | tf_op jit(solution)/shard_map/ppermute | solution.py:457
  3.1 14.1 %collective-permute-start.2 = (bf16[1808,128]{1,0:T(8,128)(2,1)}, bf16[1808,128]{1,0:T(8,128)(2,1)S(1)}, u32[]{:S(2)}, u32[]{:S(2)}) collective-permute-start(bf16[1808,128]{1,0:T(8,128)(2,1)} %pack.1.refs_1_), channel_id=1, source_target_pairs={{0,4},{1,5},{4,8},{5,9},{8,12},{9,13},{12,14},{13,15},{14,10},{15,... | collective-permute-start | bytes 1388552 | tf_op jit(solution)/shard_map/ppermute | solution.py:454
  5.7 12.9 %collective-permute-start.3 = (bf16[1808,128]{1,0:T(8,128)(2,1)}, bf16[1808,128]{1,0:T(8,128)(2,1)S(1)}, u32[]{:S(2)}, u32[]{:S(2)}) collective-permute-start(bf16[1808,128]{1,0:T(8,128)(2,1)} %pack.1.refs_1_), channel_id=1, source_target_pairs={{0,2},{1,3},{4,0},{5,1},{8,4},{9,5},{12,8},{13,9},{14,12},{15,13},... | collective-permute-start | bytes 1388552 | tf_op jit(solution)/shard_map/ppermute | solution.py:454
  5.7 4.6 %collective-permute-start = (s32[128]{0:T(128)}, s32[128]{0:T(128)S(1)}, u32[]{:S(2)}, u32[]{:S(2)}) collective-permute-start(s32[128]{0:T(128)} %lens.1), channel_id=1, source_target_pairs={{0,1},{1,0},{2,3},{3,2},{4,5},{5,4},{6,7},{7,6},{8,9},{9,8},{10,11... | collective-permute-start | bytes 1544 | tf_op jit(solution)/shard_map/ppermute | solution.py:458
  5.9 0.7 copy-start.1
  6.6 0.7 copy-start.2
  10.3 2.0 %copy-start = (bf16[1808,128]{1,0:T(8,128)(2,1)S(1)}, bf16[1808,128]{1,0:T(8,128)(2,1)}, u32[]{:S(2)}) copy-start(bf16[1808,128]{1,0:T(8,128)(2,1)} %pack.1.refs_1_) | copy-start | bytes 1388548
  18.7 11.9 %collective-permute-start.4 = (bf16[1808,128]{1,0:T(8,128)(2,1)S(1)}, bf16[1808,128]{1,0:T(8,128)(2,1)S(1)}, u32[]{:S(2)}, u32[]{:S(2)}) collective-permute-start(bf16[1808,128]{1,0:T(8,128)(2,1)S(1)} %collective-permute-done.2.refs_1_), channel_id=1, source_target_pairs={{0,4},{1,5},{4,8},{5,9},{8,12},{9,13},{12,14},{13,15},{14,10},{15,... | collective-permute-start | bytes 1388552 | tf_op jit(solution)/shard_map/ppermute | solution.py:454
  20.2 11.6 %collective-permute-start.5 = (bf16[1808,128]{1,0:T(8,128)(2,1)S(1)}, bf16[1808,128]{1,0:T(8,128)(2,1)S(1)}, u32[]{:S(2)}, u32[]{:S(2)}) collective-permute-start(bf16[1808,128]{1,0:T(8,128)(2,1)S(1)} %collective-permute-done.3.refs_2_), channel_id=1, source_target_pairs={{0,2},{1,3},{4,0},{5,1},{8,4},{9,5},{12,8},{13,9},{14,12},{15,13},... | collective-permute-start | bytes 1388552 | tf_op jit(solution)/shard_map/ppermute | solution.py:454
  31.9 10.7 %collective-permute-start.6 = (bf16[1808,128]{1,0:T(8,128)(2,1)S(1)}, bf16[1808,128]{1,0:T(8,128)(2,1)S(1)}, u32[]{:S(2)}, u32[]{:S(2)}) collective-permute-start(bf16[1808,128]{1,0:T(8,128)(2,1)S(1)} %collective-permute-done.4.refs_1_), channel_id=1, source_target_pairs={{0,4},{1,5},{4,8},{5,9},{8,12},{9,13},{12,14},{13,15},{14,10},{15,... | collective-permute-start | bytes 1388552 | tf_op jit(solution)/shard_map/ppermute | solution.py:454
  33.4 10.4 %collective-permute-start.7 = (bf16[1808,128]{1,0:T(8,128)(2,1)S(1)}, bf16[1808,128]{1,0:T(8,128)(2,1)S(1)}, u32[]{:S(2)}, u32[]{:S(2)}) collective-permute-start(bf16[1808,128]{1,0:T(8,128)(2,1)S(1)} %collective-permute-done.5.refs_2_), channel_id=1, source_target_pairs={{0,2},{1,3},{4,0},{5,1},{8,4},{9,5},{12,8},{13,9},{14,12},{15,13},... | collective-permute-start | bytes 1388552 | tf_op jit(solution)/shard_map/ppermute | solution.py:454
  43.9 8.4 %collective-permute-start.8 = (bf16[896,128]{1,0:T(8,128)(2,1)S(1)}, bf16[896,128]{1,0:T(8,128)(2,1)S(1)}, u32[]{:S(2)}, u32[]{:S(2)}) collective-permute-start(bf16[896,128]{1,0:T(8,128)(2,1)S(1)} %slice.6), channel_id=1, source_target_pairs={{0,4},{1,5},{4,8},{5,9},{8,12},{9,13},{12,14},{13,15},{14,10},{15,... | collective-permute-start | bytes 688136 | tf_op jit(solution)/shard_map/ppermute | solution.py:454
  45.5 6.8 %collective-permute-start.9 = (bf16[912,128]{1,0:T(8,128)(2,1)S(1)}, bf16[912,128]{1,0:T(8,128)(2,1)S(1)}, u32[]{:S(2)}, u32[]{:S(2)}) collective-permute-start(bf16[912,128]{1,0:T(8,128)(2,1)S(1)} %slice.7), channel_id=1, source_target_pairs={{0,2},{1,3},{4,0},{5,1},{8,4},{9,5},{12,8},{13,9},{14,12},{15,13},... | collective-permute-start | bytes 700424 | tf_op jit(solution)/shard_map/ppermute | solution.py:454
